TPU v7x, 32 devices: a whole 2x2x4 slice. The times are simulated.
32 devices in a mesh: pos: 8 (over y, x, core), freq: 4 (over z).
Axes of the slice: x: 2, y: 2, z: 4, core: 2. Of those that a mesh axis runs over, the one named last changes fastest.
Arguments:
- footprint: int32 [16, 32], replicated, may hold values from 0 to 255, as said below
- basis: bfloat16 [16, 16, 2048, 256], P('pos', 'freq'), may hold values from -0.125 to 0.125
- weights: float32 [256], replicated, may hold values from 0.1 to 10
- conduct: float32 [2, 32, 256], P(None, 'pos', 'freq'), may hold values from 0.08 to 0.24
- baseline: float32 [32, 256], P('pos', 'freq'), may hold values from 0.2 to 2
Outputs:
- image: float32 [32, 256], P('pos', 'freq')
Inputs may be any that keep to these rules, and one draw needn't show every extreme that they name: `footprint`: tile t belongs to owner t // 32. Among the 64 entries of the rows of one index of pos, at most 16 lie in one owner's tiles, and in every draw one owner gets exactly 16 from every index of pos. Entries may repeat.
All inputs are finite; a program needn't handle non-finite values.
Results may differ from a plain program's by a relative error of at most 0.0003.
Values sent between devices are 32-bit elements; how exact they have to be, the bound alone decides.
No kernel may reach another device: no remote copies, remote signals or barrier semaphores. Data moves between devices by JAX's collectives and lax.ppermute only.
A program may use at most 64 MiB of HBM per device.

v0:
```python
import math

import jax
import jax.numpy as jnp
from jax import lax
from jax.sharding import PartitionSpec as P

TH = 4
TW = 8
TILE_DEV = 32
PASSES = 3


elem_pitch = 0.125
cell_spacing = 0.7
top_depth = 4.0
eps_value = 1e-06


def padded(cells, sides, width):
    for axis, dim in sides:
        count = lax.axis_size(axis)
        ends = count - 1
        head = lax.slice_in_dim(cells, 0, width, axis=dim)
        tail = lax.slice_in_dim(cells, cells.shape[dim] - width, cells.shape[dim], axis=dim)
        cells = jnp.concatenate(
            [
                lax.ppermute(tail, axis, [(i, (i + 1) % count) for i in range(ends)]),
                cells,
                lax.ppermute(head, axis, [((i + 1) % count, i) for i in range(ends)]),
            ],
            axis=dim,
        )
    return cells


def green_rows(tile_ids, pos_global, freq_global, elements, positions, freqs):
    cells = jnp.arange(TH * TW)
    grid_row = (tile_ids // TILE_DEV)[:, None] * TH + (cells // TW)[None, :]
    grid_col = (tile_ids % TILE_DEV)[:, None] * TW + (cells % TW)[None, :]
    depth = top_depth + cell_spacing * grid_row.reshape(-1).astype(jnp.float32)
    lateral = cell_spacing * grid_col.reshape(-1).astype(jnp.float32)
    centre = pos_global.astype(jnp.float32) * (cell_spacing * TW * TILE_DEV / positions)
    element = (
        jnp.arange(elements).astype(jnp.float32) - 0.5 * (elements - 1)
    ) * elem_pitch + centre
    across = lateral[:, None] - element[None, :]
    distance = jnp.sqrt(depth[:, None] * depth[:, None] + across * across)
    wavenum = 2.0 * math.pi * (0.5 + freq_global.astype(jnp.float32) / freqs)
    amplitude = jnp.sqrt(top_depth / distance)
    phase = wavenum * distance
    return jnp.concatenate([amplitude * jnp.cos(phase), amplitude * jnp.sin(phase)], axis=1).astype(
        jnp.bfloat16
    )


def relax(values, across_k, along_k):
    centre_x = across_k[1:-1, 1:-1]
    centre_z = along_k[1:-1, 1:-1]
    middle = values[1:-1, 1:-1]
    north = jnp.minimum(centre_x, across_k[:-2, 1:-1]) * (values[:-2, 1:-1] - middle)
    south = jnp.minimum(centre_x, across_k[2:, 1:-1]) * (values[2:, 1:-1] - middle)
    west = jnp.minimum(centre_z, along_k[1:-1, :-2]) * (values[1:-1, :-2] - middle)
    east = jnp.minimum(centre_z, along_k[1:-1, 2:]) * (values[1:-1, 2:] - middle)
    return middle + north + south + west + east


def body(footprint, basis, weights, conduct, baseline):
    pos_local, freq_local, doubled, rank = basis.shape
    elements = doubled // 2
    foot_tiles = footprint.shape[1]
    pos_count = lax.axis_size("pos")
    freq_count = lax.axis_size("freq")
    positions = pos_local * pos_count
    freqs = freq_local * freq_count
    my_pos = lax.axis_index("pos")
    first_pos = my_pos * pos_local
    first_freq = lax.axis_index("freq") * freq_local
    tile_cells = TH * TW
    my_ids = lax.dynamic_slice_in_dim(footprint, first_pos, pos_local, 0)

    def one_position(inputs):
        tile_ids, local_basis, offset = inputs

        def add_freq(running, pair):
            freq_basis, freq_offset = pair
            green = green_rows(
                tile_ids, first_pos + offset, first_freq + freq_offset, elements, positions, freqs
            )
            return (running + jnp.dot(green, freq_basis, preferred_element_type=jnp.float32), None)

        start = jnp.zeros((foot_tiles * tile_cells, rank), jnp.float32)
        total, _ = lax.scan(add_freq, start, (local_basis, jnp.arange(freq_local)))
        return total

    partial_value = lax.map(one_position, (my_ids, basis, jnp.arange(pos_local)))
    rows = pos_local * foot_tiles
    partial_value = partial_value.reshape(rows, tile_cells, rank)
    capacity = max(2, 2 * rows // pos_count)
    slots = pos_count * capacity
    owners = my_ids.reshape(rows) // TILE_DEV
    owner_hot = (owners[:, None] == jnp.arange(pos_count)[None, :]).astype(jnp.int32)
    before = jnp.cumsum(owner_hot, axis=0) - owner_hot
    order_in = jnp.sum(before * owner_hot, axis=1)
    slot_of = owners * capacity + order_in
    placing = (jnp.arange(slots)[:, None] == slot_of[None, :]).astype(jnp.float32)
    all_ids = footprint.reshape(pos_count, rows)
    mine = (all_ids // TILE_DEV == my_pos).astype(jnp.int32)
    mine_rank = jnp.cumsum(mine, axis=1) - mine
    hitting = (mine[:, None, :] == 1) & (
        mine_rank[:, None, :] == jnp.arange(capacity)[None, :, None]
    )
    incoming = jnp.max(jnp.where(hitting, (all_ids % TILE_DEV)[:, None, :], -1), axis=2).reshape(
        slots
    )
    gathering = (jnp.arange(TILE_DEV)[:, None] == incoming[None, :]).astype(jnp.float32)
    local_tiles = TILE_DEV // freq_count
    packed = jnp.dot(
        placing,
        partial_value.reshape(rows, -1),
        precision=lax.Precision.HIGHEST,
        preferred_element_type=jnp.float32,
    )
    arrived = lax.all_to_all(
        packed.reshape(pos_count, capacity, -1), "pos", split_axis=0, concat_axis=0, tiled=True
    )
    compound = jnp.dot(
        gathering,
        arrived.reshape(slots, -1),
        precision=lax.Precision.HIGHEST,
        preferred_element_type=jnp.float32,
    ).reshape(TILE_DEV, tile_cells, rank)
    summed = lax.psum_scatter(compound, "freq", scatter_dimension=0, tiled=True)
    energy = jnp.sum(summed * summed * weights, axis=-1) / rank
    intensity = jnp.sqrt(energy + eps_value)
    field = intensity.reshape(local_tiles, TH, TW).transpose(1, 0, 2).reshape(TH, local_tiles * TW)
    field = field + baseline
    rims = padded(conduct, (("pos", 1), ("freq", 2)), 1)
    values = field
    for sweep in range(PASSES):
        widened = padded(values, (("pos", 0), ("freq", 1)), 1)
        values = relax(widened, rims[0], rims[1])
    return values


def solution(mesh):
    return jax.shard_map(
        body,
        mesh=mesh,
        in_specs=(P(), P("pos", "freq", None, None), P(), P(None, "pos", "freq"), P("pos", "freq")),
        out_specs=P("pos", "freq"),
        check_vma=False,
    )
```

profile of v0, /device:TPU:17, one launch (start us, length us, event | category | flops | bytes accessed | tf_op | source)
XLA Modules:
  0.0 382.7 jit_solution(12756900967569812648)
XLA Ops:
  8.8 222.6 %while.37 = (s32[]{:T(128)}, f32[2,1024,256]{2,1,0:T(8,128)S(1)}, bf16[2,4,2048,256]{3,2,1,0:T(8,128)(2,1)}, s32[2]{0:T(128)S(1)}, s32[2,32]{1,0:T(2,128)S(1)}, ...) while((s32[]{:T(128)}, f32[2,1024,256]{2,1,0:T(8,128)S(1)}, ...), condition=%wide.region_7.8_spmd, body=%wide.region_4.7_spmd.sunk | while | flops 1092105600 | bytes 22064440 | solution.py:96
  10.2 4.4 %dynamic-slice_bitcast_fusion.2 = bf16[4,2048,256]{2,1,0:T(8,128)(2,1)} fusion(bf16[2,4,2048,256]{3,2,1,0:T(8,128)(2,1)} %get-tuple-element.712, s32[]{:T(128)} %get-tuple-element.695), kind=kLoop, calls=%fused_computation.33.clone.1 | loop fusion | bytes 8388612 | tf_op jit(solution)/shard_map/while/body/jit(dynamic_index_in_dim)/squeeze | solution.py:96
  14.6 105.5 %while.38 = (s32[]{:T(128)}, f32[1024,256]{1,0:T(8,128)S(1)}, s32[32,1]{0,1:T(1,128)S(1)}, s32[32]{0:T(128)S(1)}, s32[32,1]{0,1:T(1,128)S(1)}, /*index=5*/s32[32...) while((s32[]{:T(128)}, f32[1024,256]{1,0:T(8,128)S(1)}, ...), condition=%wide.region_6.6_spmd.clone, body=%wide.region_5.5_spmd.clone.sunk | while | flops 1092105472 | bytes 11577571 | solution.py:93
  16.2 20.6 %multiply_convert_fusion.3 = (bf16[1024,1024]{1,0:T(8,128)(2,1)}, bf16[1024,1024]{1,0:T(8,128)(2,1)}) fusion(f32[]{:T(128)S(6)} %mul.288, f32[1024]{0:T(1024)S(1)} %multiply_add_fusion.7, f32[1024]{0:T(1024)S(1)} %mul.289, f32[1024]{0:T(1024)S(1)} %reshape.372), kind=kLoop, calls=%fused_computation.5.clone.1 | loop fusion | flops 9437184 | bytes 4206596 | tf_op jit(solution)/shard_map/convert
  36.8 4.1 %fusion.48 = f32[1024,256]{1,0:T(8,128)S(1)} fusion(bf16[1024,1024]{1,0:T(8,128)(2,1)} %get-tuple-element.633, bf16[1024,1024]{1,0:T(8,128)(2,1)} %get-tuple-element.634, f32[1024,256]{1,0:T(8,128)S(1)} %get-tuple-element.651, bf16[4,2048,256]{2,1,0:T(8,128)(2,1)} %get-tuple-element.674, s32[]{:T(128)} %get-tuple-element.650, pred[]{:T(512)S(6)} %compare.53), kind=kOutput, calls=%fused_computation.9.clone.1 | convolution fusion | flops 1082654720 | bytes 7340545 | tf_op jit(solution)/shard_map/while/body/eval_jaxpr/while/body/eval_jaxpr/dot_general | solution.py:90
  42.6 20.6 %multiply_convert_fusion.3 = (bf16[1024,1024]{1,0:T(8,128)(2,1)}, bf16[1024,1024]{1,0:T(8,128)(2,1)}) fusion(f32[]{:T(128)S(6)} %mul.288, f32[1024]{0:T(1024)S(1)} %multiply_add_fusion.7, f32[1024]{0:T(1024)S(1)} %mul.289, f32[1024]{0:T(1024)S(1)} %reshape.372), kind=kLoop, calls=%fused_computation.5.clone.1 | loop fusion | flops 9437184 | bytes 4206596 | tf_op jit(solution)/shard_map/convert
  63.2 4.1 %fusion.48 = f32[1024,256]{1,0:T(8,128)S(1)} fusion(bf16[1024,1024]{1,0:T(8,128)(2,1)} %get-tuple-element.633, bf16[1024,1024]{1,0:T(8,128)(2,1)} %get-tuple-element.634, f32[1024,256]{1,0:T(8,128)S(1)} %get-tuple-element.651, bf16[4,2048,256]{2,1,0:T(8,128)(2,1)} %get-tuple-element.674, s32[]{:T(128)} %get-tuple-element.650, pred[]{:T(512)S(6)} %compare.53), kind=kOutput, calls=%fused_computation.9.clone.1 | convolution fusion | flops 1082654720 | bytes 7340545 | tf_op jit(solution)/shard_map/while/body/eval_jaxpr/while/body/eval_jaxpr/dot_general | solution.py:90
  68.9 20.6 %multiply_convert_fusion.3 = (bf16[1024,1024]{1,0:T(8,128)(2,1)}, bf16[1024,1024]{1,0:T(8,128)(2,1)}) fusion(f32[]{:T(128)S(6)} %mul.288, f32[1024]{0:T(1024)S(1)} %multiply_add_fusion.7, f32[1024]{0:T(1024)S(1)} %mul.289, f32[1024]{0:T(1024)S(1)} %reshape.372), kind=kLoop, calls=%fused_computation.5.clone.1 | loop fusion | flops 9437184 | bytes 4206596 | tf_op jit(solution)/shard_map/convert
  89.5 4.1 %fusion.48 = f32[1024,256]{1,0:T(8,128)S(1)} fusion(bf16[1024,1024]{1,0:T(8,128)(2,1)} %get-tuple-element.633, bf16[1024,1024]{1,0:T(8,128)(2,1)} %get-tuple-element.634, f32[1024,256]{1,0:T(8,128)S(1)} %get-tuple-element.651, bf16[4,2048,256]{2,1,0:T(8,128)(2,1)} %get-tuple-element.674, s32[]{:T(128)} %get-tuple-element.650, pred[]{:T(512)S(6)} %compare.53), kind=kOutput, calls=%fused_computation.9.clone.1 | convolution fusion | flops 1082654720 | bytes 7340545 | tf_op jit(solution)/shard_map/while/body/eval_jaxpr/while/body/eval_jaxpr/dot_general | solution.py:90
  95.3 20.6 %multiply_convert_fusion.3 = (bf16[1024,1024]{1,0:T(8,128)(2,1)}, bf16[1024,1024]{1,0:T(8,128)(2,1)}) fusion(f32[]{:T(128)S(6)} %mul.288, f32[1024]{0:T(1024)S(1)} %multiply_add_fusion.7, f32[1024]{0:T(1024)S(1)} %mul.289, f32[1024]{0:T(1024)S(1)} %reshape.372), kind=kLoop, calls=%fused_computation.5.clone.1 | loop fusion | flops 9437184 | bytes 4206596 | tf_op jit(solution)/shard_map/convert
  115.9 4.1 %fusion.48 = f32[1024,256]{1,0:T(8,128)S(1)} fusion(bf16[1024,1024]{1,0:T(8,128)(2,1)} %get-tuple-element.633, bf16[1024,1024]{1,0:T(8,128)(2,1)} %get-tuple-element.634, f32[1024,256]{1,0:T(8,128)S(1)} %get-tuple-element.651, bf16[4,2048,256]{2,1,0:T(8,128)(2,1)} %get-tuple-element.674, s32[]{:T(128)} %get-tuple-element.650, pred[]{:T(512)S(6)} %compare.53), kind=kOutput, calls=%fused_computation.9.clone.1 | convolution fusion | flops 1082654720 | bytes 7340545 | tf_op jit(solution)/shard_map/while/body/eval_jaxpr/while/body/eval_jaxpr/dot_general | solution.py:90
  121.5 4.4 %dynamic-slice_bitcast_fusion.2 = bf16[4,2048,256]{2,1,0:T(8,128)(2,1)} fusion(bf16[2,4,2048,256]{3,2,1,0:T(8,128)(2,1)} %get-tuple-element.712, s32[]{:T(128)} %get-tuple-element.695), kind=kLoop, calls=%fused_computation.33.clone.1 | loop fusion | bytes 8388612 | tf_op jit(solution)/shard_map/while/body/jit(dynamic_index_in_dim)/squeeze | solution.py:96
  125.9 105.5 %while.38 = (s32[]{:T(128)}, f32[1024,256]{1,0:T(8,128)S(1)}, s32[32,1]{0,1:T(1,128)S(1)}, s32[32]{0:T(128)S(1)}, s32[32,1]{0,1:T(1,128)S(1)}, /*index=5*/s32[32...) while((s32[]{:T(128)}, f32[1024,256]{1,0:T(8,128)S(1)}, ...), condition=%wide.region_6.6_spmd.clone, body=%wide.region_5.5_spmd.clone.sunk | while | flops 1092105472 | bytes 11577571 | solution.py:93
  127.5 20.6 %multiply_convert_fusion.3 = (bf16[1024,1024]{1,0:T(8,128)(2,1)}, bf16[1024,1024]{1,0:T(8,128)(2,1)}) fusion(f32[]{:T(128)S(6)} %mul.288, f32[1024]{0:T(1024)S(1)} %multiply_add_fusion.7, f32[1024]{0:T(1024)S(1)} %mul.289, f32[1024]{0:T(1024)S(1)} %reshape.372), kind=kLoop, calls=%fused_computation.5.clone.1 | loop fusion | flops 9437184 | bytes 4206596 | tf_op jit(solution)/shard_map/convert
  148.1 4.1 %fusion.48 = f32[1024,256]{1,0:T(8,128)S(1)} fusion(bf16[1024,1024]{1,0:T(8,128)(2,1)} %get-tuple-element.633, bf16[1024,1024]{1,0:T(8,128)(2,1)} %get-tuple-element.634, f32[1024,256]{1,0:T(8,128)S(1)} %get-tuple-element.651, bf16[4,2048,256]{2,1,0:T(8,128)(2,1)} %get-tuple-element.674, s32[]{:T(128)} %get-tuple-element.650, pred[]{:T(512)S(6)} %compare.53), kind=kOutput, calls=%fused_computation.9.clone.1 | convolution fusion | flops 1082654720 | bytes 7340545 | tf_op jit(solution)/shard_map/while/body/eval_jaxpr/while/body/eval_jaxpr/dot_general | solution.py:90
  153.9 20.6 %multiply_convert_fusion.3 = (bf16[1024,1024]{1,0:T(8,128)(2,1)}, bf16[1024,1024]{1,0:T(8,128)(2,1)}) fusion(f32[]{:T(128)S(6)} %mul.288, f32[1024]{0:T(1024)S(1)} %multiply_add_fusion.7, f32[1024]{0:T(1024)S(1)} %mul.289, f32[1024]{0:T(1024)S(1)} %reshape.372), kind=kLoop, calls=%fused_computation.5.clone.1 | loop fusion | flops 9437184 | bytes 4206596 | tf_op jit(solution)/shard_map/convert
  174.5 4.1 %fusion.48 = f32[1024,256]{1,0:T(8,128)S(1)} fusion(bf16[1024,1024]{1,0:T(8,128)(2,1)} %get-tuple-element.633, bf16[1024,1024]{1,0:T(8,128)(2,1)} %get-tuple-element.634, f32[1024,256]{1,0:T(8,128)S(1)} %get-tuple-element.651, bf16[4,2048,256]{2,1,0:T(8,128)(2,1)} %get-tuple-element.674, s32[]{:T(128)} %get-tuple-element.650, pred[]{:T(512)S(6)} %compare.53), kind=kOutput, calls=%fused_computation.9.clone.1 | convolution fusion | flops 1082654720 | bytes 7340545 | tf_op jit(solution)/shard_map/while/body/eval_jaxpr/while/body/eval_jaxpr/dot_general | solution.py:90
  180.3 20.6 %multiply_convert_fusion.3 = (bf16[1024,1024]{1,0:T(8,128)(2,1)}, bf16[1024,1024]{1,0:T(8,128)(2,1)}) fusion(f32[]{:T(128)S(6)} %mul.288, f32[1024]{0:T(1024)S(1)} %multiply_add_fusion.7, f32[1024]{0:T(1024)S(1)} %mul.289, f32[1024]{0:T(1024)S(1)} %reshape.372), kind=kLoop, calls=%fused_computation.5.clone.1 | loop fusion | flops 9437184 | bytes 4206596 | tf_op jit(solution)/shard_map/convert
  200.9 4.1 %fusion.48 = f32[1024,256]{1,0:T(8,128)S(1)} fusion(bf16[1024,1024]{1,0:T(8,128)(2,1)} %get-tuple-element.633, bf16[1024,1024]{1,0:T(8,128)(2,1)} %get-tuple-element.634, f32[1024,256]{1,0:T(8,128)S(1)} %get-tuple-element.651, bf16[4,2048,256]{2,1,0:T(8,128)(2,1)} %get-tuple-element.674, s32[]{:T(128)} %get-tuple-element.650, pred[]{:T(512)S(6)} %compare.53), kind=kOutput, calls=%fused_computation.9.clone.1 | convolution fusion | flops 1082654720 | bytes 7340545 | tf_op jit(solution)/shard_map/while/body/eval_jaxpr/while/body/eval_jaxpr/dot_general | solution.py:90
  206.6 20.6 %multiply_convert_fusion.3 = (bf16[1024,1024]{1,0:T(8,128)(2,1)}, bf16[1024,1024]{1,0:T(8,128)(2,1)}) fusion(f32[]{:T(128)S(6)} %mul.288, f32[1024]{0:T(1024)S(1)} %multiply_add_fusion.7, f32[1024]{0:T(1024)S(1)} %mul.289, f32[1024]{0:T(1024)S(1)} %reshape.372), kind=kLoop, calls=%fused_computation.5.clone.1 | loop fusion | flops 9437184 | bytes 4206596 | tf_op jit(solution)/shard_map/convert
  227.2 4.1 %fusion.48 = f32[1024,256]{1,0:T(8,128)S(1)} fusion(bf16[1024,1024]{1,0:T(8,128)(2,1)} %get-tuple-element.633, bf16[1024,1024]{1,0:T(8,128)(2,1)} %get-tuple-element.634, f32[1024,256]{1,0:T(8,128)S(1)} %get-tuple-element.651, bf16[4,2048,256]{2,1,0:T(8,128)(2,1)} %get-tuple-element.674, s32[]{:T(128)} %get-tuple-element.650, pred[]{:T(512)S(6)} %compare.53), kind=kOutput, calls=%fused_computation.9.clone.1 | convolution fusion | flops 1082654720 | bytes 7340545 | tf_op jit(solution)/shard_map/while/body/eval_jaxpr/while/body/eval_jaxpr/dot_general | solution.py:90
  234.6 3.9 %fusion.17 = f32[8,16,8192]{2,1,0:T(8,128)} fusion(f32[64,8192,1]{1,0,2:T(8,128)S(1)} %reshape.368, s32[64]{0:T(128)S(1)} %copy-done.6, s32[8,16]{1,0:T(8,128)S(1)} %copy-done.2), kind=kOutput, calls=%fused_computation.43 | convolution fusion | flops 805314560 | bytes 6292224 | tf_op jit(solution)/shard_map/dot_general | solution.py:118
  238.5 5.2 %all-to-all-start = ((f32[8,16,8192]{2,1,0:T(8,128)}), f32[8,16,8192]{2,1,0:T(8,128)}, u32[]{:S(2)}, u32[]{:S(2)}) async-start(f32[8,16,8192]{2,1,0:T(8,128)} %fusion.17), calls=%async_computation | async-start | bytes 8388608 | tf_op jit(solution)/shard_map/all_to_all | solution.py:124
  244.3 45.0 %all-to-all-done = f32[8,16,8192]{2,1,0:T(8,128)} async-done(((f32[8,16,8192]{2,1,0:T(8,128)}), f32[8,16,8192]{2,1,0:T(8,128)}, u32[]{:S(2)}, u32[]{:S(2)}) %all-to-all-start) | async-done | bytes 4194336 | tf_op jit(solution)/shard_map/all_to_all | solution.py:124
  289.3 5.7 %copy.16 = f32[8192,128]{1,0:T(8,128)} copy(f32[8192,128]{0,1:T(8,128)} %bitcast.8) | data formatting | bytes 8388608 | tf_op jit(solution)/shard_map/dot_general | solution.py:127
  295.0 5.6 %fusion.23 = f32[32,32,256]{2,0,1:T(8,128)} fusion(f32[32,256,128]{2,1,0:T(8,128)} %bitcast.61, s32[128]{0:T(128)S(1)} %eq.111), kind=kOutput, calls=%fused_computation.52 | convolution fusion | flops 402657280 | bytes 5243392 | tf_op jit(solution)/shard_map/dot_general | solution.py:127
  300.6 5.7 %collective-permute-start = (f32[2,1,64]{2,1,0:T(1,128)S(1)}, f32[2,1,64]{2,1,0:T(1,128)S(1)}, u32[]{:S(2)}, u32[]{:S(2)}) collective-permute-start(f32[2,1,64]{2,1,0:T(1,128)S(1)} %get-tuple-element.466), channel_id=1, source_target_pairs={{0,4},{4,8},{8,12},{12,16},{16,20},{20,24},{24,28},{1,5},{5,9},{9,... | collective-permute-start | bytes 1544 | tf_op jit(solution)/shard_map/ppermute | solution.py:28
  306.3 1.9 collective-permute-start.1
  308.2 3.3 collective-permute-done.1
  311.7 3.2 collective-permute-start.2
  314.9 2.0 collective-permute-start.3
  317.0 3.1 collective-permute-done.3
  320.1 8.8 %reduce-scatter.2.cloned.1.call-done = f32[8,32,256]{2,0,1:T(8,128)} async-done(((f32[32,32,256]{2,0,1:T(8,128)}), f32[8,32,256]{2,0,1:T(8,128)}) %reduce-scatter.2.cloned.1.call-update) | async-done | bytes 262160 | tf_op jit(solution)/shard_map/reduce_scatter | solution.py:133
  330.3 3.6 collective-permute-start.4
  333.9 1.9 collective-permute-start.5
  335.9 2.9 collective-permute-done.5
  338.9 2.2 collective-permute-start.6
  341.0 3.1 collective-permute-start.7
  345.6 3.4 collective-permute-start.8
  349.0 1.9 collective-permute-start.9
  350.9 2.9 collective-permute-done.9
  353.9 1.9 collective-permute-start.10
  355.9 3.4 collective-permute-start.11
  360.4 3.2 collective-permute-start.12
  363.6 1.9 collective-permute-start.13
  365.5 3.3 collective-permute-done.13
  368.9 1.9 collective-permute-start.14
  370.8 3.4 collective-permute-start.15
  (151 shorter events, 20.7 us)
Async XLA Ops:
  231.5 1.4 copy-start
  232.8 1.8 copy-start.2
  232.8 1.8 copy-start.6
  238.5 5.2 %copy-start.3 = (s32[16,32]{1,0:T(8,128)S(1)}, s32[16,32]{1,0:T(8,128)}, u32[]{:S(2)}) copy-start(s32[16,32]{1,0:T(8,128)} %param.9) | copy-start | bytes 6148
  238.5 50.8 %all-to-all-start = ((f32[8,16,8192]{2,1,0:T(8,128)}), f32[8,16,8192]{2,1,0:T(8,128)}, u32[]{:S(2)}, u32[]{:S(2)}) async-start(f32[8,16,8192]{2,1,0:T(8,128)} %fusion.17), calls=%async_computation | async-start | bytes 8388608 | tf_op jit(solution)/shard_map/all_to_all | solution.py:124
  243.7 85.3 %reduce-scatter.2.cloned.1.call-start = ((), (), s32[]{:S(2)}) async-start(), calls=%async_computation.2 | async-start | bytes 1310720 | tf_op jit(solution)/shard_map/reduce_scatter | solution.py:133
  295.0 5.6 %copy-start.1 = (f32[2,4,64]{2,1,0:T(4,128)S(1)}, f32[2,4,64]{2,1,0:T(4,128)}, u32[]{:S(2)}) copy-start(f32[2,4,64]{2,1,0:T(4,128)} %param.12) | copy-start | bytes 6148
  295.0 34.0 %copy-start.5 = (f32[256]{0:T(256)S(1)}, f32[256]{0:T(256)}, u32[]{:S(2)}) copy-start(f32[256]{0:T(256)} %param.11) | copy-start | bytes 3076
  295.0 35.3 %copy-start.4 = (f32[4,64]{1,0:T(4,128)S(1)}, f32[4,64]{1,0:T(4,128)}, u32[]{:S(2)}) copy-start(f32[4,64]{1,0:T(4,128)} %param.13) | copy-start | bytes 3076
  300.6 7.6 %collective-permute-start = (f32[2,1,64]{2,1,0:T(1,128)S(1)}, f32[2,1,64]{2,1,0:T(1,128)S(1)}, u32[]{:S(2)}, u32[]{:S(2)}) collective-permute-start(f32[2,1,64]{2,1,0:T(1,128)S(1)} %get-tuple-element.466), channel_id=1, source_target_pairs={{0,4},{4,8},{8,12},{12,16},{16,20},{20,24},{24,28},{1,5},{5,9},{9,... | collective-permute-start | bytes 1544 | tf_op jit(solution)/shard_map/ppermute | solution.py:28
  306.3 5.3 %collective-permute-start.1 = (f32[2,1,64]{2,1,0:T(1,128)S(1)}, f32[2,1,64]{2,1,0:T(1,128)S(1)}, u32[]{:S(2)}, u32[]{:S(2)}) collective-permute-start(f32[2,1,64]{2,1,0:T(1,128)S(1)} %get-tuple-element.467), channel_id=1, source_target_pairs={{4,0},{8,4},{12,8},{16,12},{20,16},{24,20},{28,24},{5,1},{9,5},{13... | collective-permute-start | bytes 1544 | tf_op jit(solution)/shard_map/ppermute | solution.py:30
  311.7 5.3 %collective-permute-start.2 = (f32[2,6,1]{2,1,0:T(8,128)S(1)}, f32[2,6,1]{2,1,0:T(8,128)S(1)}, u32[]{:S(2)}, u32[]{:S(2)}) collective-permute-start(f32[2,6,1]{2,1,0:T(8,128)S(1)} %get-tuple-element.460), channel_id=1, source_target_pairs={{0,1},{1,2},{2,3},{4,5},{5,6},{6,7},{8,9},{9,10},{10,11},{12,13},{... | collective-permute-start | bytes 152 | tf_op jit(solution)/shard_map/ppermute | solution.py:28
  314.9 5.1 %collective-permute-start.3 = (f32[2,6,1]{2,1,0:T(8,128)S(1)}, f32[2,6,1]{2,1,0:T(8,128)S(1)}, u32[]{:S(2)}, u32[]{:S(2)}) collective-permute-start(f32[2,6,1]{2,1,0:T(8,128)S(1)} %get-tuple-element.461), channel_id=1, source_target_pairs={{1,0},{2,1},{3,2},{5,4},{6,5},{7,6},{9,8},{10,9},{11,10},{13,12},{... | collective-permute-start | bytes 152 | tf_op jit(solution)/shard_map/ppermute | solution.py:30
  330.3 5.6 %collective-permute-start.4 = (f32[1,64]{1,0:T(1,128)S(1)}, f32[1,64]{1,0:T(1,128)S(1)}, u32[]{:S(2)}, u32[]{:S(2)}) collective-permute-start(f32[1,64]{1,0:T(1,128)S(1)} %get-tuple-element.486), channel_id=1, source_target_pairs={{0,4},{4,8},{8,12},{12,16},{16,20},{20,24},{24,28},{1,5},{5,9},{9,... | collective-permute-start | bytes 776 | tf_op jit(solution)/shard_map/ppermute | solution.py:28
  333.9 4.9 %collective-permute-start.5 = (f32[1,64]{1,0:T(1,128)S(1)}, f32[1,64]{1,0:T(1,128)S(1)}, u32[]{:S(2)}, u32[]{:S(2)}) collective-permute-start(f32[1,64]{1,0:T(1,128)S(1)} %get-tuple-element.487), channel_id=1, source_target_pairs={{4,0},{8,4},{12,8},{16,12},{20,16},{24,20},{28,24},{5,1},{9,5},{13... | collective-permute-start | bytes 776 | tf_op jit(solution)/shard_map/ppermute | solution.py:30
  338.9 5.3 %collective-permute-start.6 = (f32[6,1]{1,0:T(8,128)S(1)}, f32[6,1]{1,0:T(8,128)S(1)}, u32[]{:S(2)}, u32[]{:S(2)}) collective-permute-start(f32[6,1]{1,0:T(8,128)S(1)} %get-tuple-element.468), channel_id=1, source_target_pairs={{0,1},{1,2},{2,3},{4,5},{5,6},{6,7},{8,9},{9,10},{10,11},{12,13},{... | collective-permute-start | bytes 80 | tf_op jit(solution)/shard_map/ppermute | solution.py:28
  341.0 4.4 %collective-permute-start.7 = (f32[6,1]{1,0:T(8,128)S(1)}, f32[6,1]{1,0:T(8,128)S(1)}, u32[]{:S(2)}, u32[]{:S(2)}) collective-permute-start(f32[6,1]{1,0:T(8,128)S(1)} %get-tuple-element.469), channel_id=1, source_target_pairs={{1,0},{2,1},{3,2},{5,4},{6,5},{7,6},{9,8},{10,9},{11,10},{13,12},{... | collective-permute-start | bytes 80 | tf_op jit(solution)/shard_map/ppermute | solution.py:30
  345.6 5.4 %collective-permute-start.8 = (f32[1,64]{1,0:T(1,128)S(1)}, f32[1,64]{1,0:T(1,128)S(1)}, u32[]{:S(2)}, u32[]{:S(2)}) collective-permute-start(f32[1,64]{1,0:T(1,128)S(1)} %get-tuple-element.482), channel_id=1, source_target_pairs={{0,4},{4,8},{8,12},{12,16},{16,20},{20,24},{24,28},{1,5},{5,9},{9,... | collective-permute-start | bytes 776 | tf_op jit(solution)/shard_map/ppermute | solution.py:28
  349.0 4.9 %collective-permute-start.9 = (f32[1,64]{1,0:T(1,128)S(1)}, f32[1,64]{1,0:T(1,128)S(1)}, u32[]{:S(2)}, u32[]{:S(2)}) collective-permute-start(f32[1,64]{1,0:T(1,128)S(1)} %get-tuple-element.483), channel_id=1, source_target_pairs={{4,0},{8,4},{12,8},{16,12},{20,16},{24,20},{28,24},{5,1},{9,5},{13... | collective-permute-start | bytes 776 | tf_op jit(solution)/shard_map/ppermute | solution.py:30
  353.9 5.3 %collective-permute-start.10 = (f32[6,1]{1,0:T(8,128)S(1)}, f32[6,1]{1,0:T(8,128)S(1)}, u32[]{:S(2)}, u32[]{:S(2)}) collective-permute-start(f32[6,1]{1,0:T(8,128)S(1)} %get-tuple-element.464), channel_id=1, source_target_pairs={{0,1},{1,2},{2,3},{4,5},{5,6},{6,7},{8,9},{9,10},{10,11},{12,13},{... | collective-permute-start | bytes 80 | tf_op jit(solution)/shard_map/ppermute | solution.py:28
  355.9 4.4 %collective-permute-start.11 = (f32[6,1]{1,0:T(8,128)S(1)}, f32[6,1]{1,0:T(8,128)S(1)}, u32[]{:S(2)}, u32[]{:S(2)}) collective-permute-start(f32[6,1]{1,0:T(8,128)S(1)} %get-tuple-element.465), channel_id=1, source_target_pairs={{1,0},{2,1},{3,2},{5,4},{6,5},{7,6},{9,8},{10,9},{11,10},{13,12},{... | collective-permute-start | bytes 80 | tf_op jit(solution)/shard_map/ppermute | solution.py:30
  360.4 5.1 %collective-permute-start.12 = (f32[1,64]{1,0:T(1,128)S(1)}, f32[1,64]{1,0:T(1,128)S(1)}, u32[]{:S(2)}, u32[]{:S(2)}) collective-permute-start(f32[1,64]{1,0:T(1,128)S(1)} %get-tuple-element.478), channel_id=1, source_target_pairs={{0,4},{4,8},{8,12},{12,16},{16,20},{20,24},{24,28},{1,5},{5,9},{9,... | collective-permute-start | bytes 776 | tf_op jit(solution)/shard_map/ppermute | solution.py:28
  363.6 5.2 %collective-permute-start.13 = (f32[1,64]{1,0:T(1,128)S(1)}, f32[1,64]{1,0:T(1,128)S(1)}, u32[]{:S(2)}, u32[]{:S(2)}) collective-permute-start(f32[1,64]{1,0:T(1,128)S(1)} %get-tuple-element.479), channel_id=1, source_target_pairs={{4,0},{8,4},{12,8},{16,12},{20,16},{24,20},{28,24},{5,1},{9,5},{13... | collective-permute-start | bytes 776 | tf_op jit(solution)/shard_map/ppermute | solution.py:30
  368.9 5.3 %collective-permute-start.14 = (f32[6,1]{1,0:T(8,128)S(1)}, f32[6,1]{1,0:T(8,128)S(1)}, u32[]{:S(2)}, u32[]{:S(2)}) collective-permute-start(f32[6,1]{1,0:T(8,128)S(1)} %get-tuple-element.462), channel_id=1, source_target_pairs={{0,1},{1,2},{2,3},{4,5},{5,6},{6,7},{8,9},{9,10},{10,11},{12,13},{... | collective-permute-start | bytes 80 | tf_op jit(solution)/shard_map/ppermute | solution.py:28
  370.8 4.4 %collective-permute-start.15 = (f32[6,1]{1,0:T(8,128)S(1)}, f32[6,1]{1,0:T(8,128)S(1)}, u32[]{:S(2)}, u32[]{:S(2)}) collective-permute-start(f32[6,1]{1,0:T(8,128)S(1)} %get-tuple-element.463), channel_id=1, source_target_pairs={{1,0},{2,1},{3,2},{5,4},{6,5},{7,6},{9,8},{10,9},{11,10},{13,12},{... | collective-permute-start | bytes 80 | tf_op jit(solution)/shard_map/ppermute | solution.py:30
Sparse Core Ops, SparseCore 0:
  300.7 28.1 reduce-scatter.1
where the time goes:
time: 389 us; the launch traced here: 383 us
  other arithmetic  170 us (44%)
  waiting for transfers between devices  72.5 us (19%)
  starting transfers between devices  49.9 us (13%)
  matrix products  42.5 us (11%)
  local copies, waits for them, and re-layouts  26.9 us (7%)
  between operations  13.7 us (4%)
  loops' own time  7.19 us (2%)
    another operation x8, other arithmetic  165 us
    all_to_all x1, waiting for transfers between devices, body(): lax.all_to_all(packed.reshape(pos_count, capacity, -1), 'pos', split_axis...  45 us
    dot_general x8, matrix products, add_freq(): jnp.dot(green, freq_basis, preferred_element_type=jnp.float32)  33.1 us
    ppermute x8, starting transfers between devices, padded(): lax.ppermute(tail, axis, [(i, (i + 1) % count) for i in range(ends)])  25.1 us
    ppermute x8, starting transfers between devices, padded(): lax.ppermute(head, axis, [((i + 1) % count, i) for i in range(ends)])  19.6 us
    ppermute x8, waiting for transfers between devices, padded(): lax.ppermute(head, axis, [((i + 1) % count, i) for i in range(ends)])  18.7 us
    reduce_scatter x1, waiting for transfers between devices, body(): summed = lax.psum_scatter(compound, 'freq', scatter_dimension=0, tiled=True)  8.84 us
    squeeze x2, local copies, waits for them, and re-layouts, body(): lax.map(one_position, (my_ids, basis, jnp.arange(pos_local)))  8.84 us
  transfers between devices with their start and end apart: 18, of which 10 were waited for; matrix products, arithmetic and copies ran while one was open for 0% of the time, Pallas kernels for 0%

commit v1 on v0

v1 whole, which is shorter than its diff:
```python
import functools

import jax
import jax.numpy as jnp
from jax import lax
from jax.experimental import pallas as pl
from jax.experimental.pallas import tpu as pltpu
from jax.sharding import PartitionSpec as P

TH = 4
TW = 8
CELLS = TH * TW
TILE_DEV = 32
PASSES = 3
LANES = 128
ELEM_BLOCK = 256

elem_pitch = 0.125
cell_spacing = 0.7
top_depth = 4.0
eps_value = 1e-06

COS_PI = (0.9999999403953552, -4.934792995452881, 4.058411121368408, -1.331876516342163, 0.21968960762023926)
SIN_PI = (3.1415927410125732, -5.167710304260254, 2.550077438354492, -0.598291277885437, 0.07765766233205795)

HIGHEST = lax.Precision.HIGHEST
VMEM_LIMIT = 48 * 1024 * 1024


def half_turn(turns):
    x = turns - jnp.round(turns)
    square = x * x
    c = COS_PI[-1]
    for term in COS_PI[-2::-1]:
        c = c * square + term
    s = SIN_PI[-1]
    for term in SIN_PI[-2::-1]:
        s = s * square + term
    return c, s * x


def waves(distance, inverse, centre_turns, half_step, count):
    c, s = half_turn(centre_turns * distance)
    amplitude = 2.0 * (inverse * lax.rsqrt(inverse))
    twice = (amplitude + amplitude) * c
    mid_c = twice * c - amplitude
    mid_s = twice * s
    c, s = half_turn(half_step * distance)
    twice = c + c
    step_c = twice * c - 1.0
    step_s = twice * s
    cc, ss, cs, sc = mid_c * step_c, mid_s * step_s, mid_c * step_s, mid_s * step_c
    low, high = (cc + ss, sc - cs), (cc - ss, sc + cs)
    lows, highs = [low], [high]
    factor = 4.0 * (step_c * step_c) - 2.0
    before_low, before_high = high, low
    for _ in range(count // 2 - 1):
        low, before_low = tuple(factor * a - b for a, b in zip(low, before_low)), low
        high, before_high = tuple(factor * a - b for a, b in zip(high, before_high)), high
        lows.append(low)
        highs.append(high)
    return lows[::-1] + highs


def project_kernel(sizes, part, where_ref, foot_ref, basis_ref, *refs):
    pos_count, freqs, positions, elements, pos_local, freq_local, foot = sizes
    groups = pos_count // TH
    per_dest = TW // groups
    out_refs, (green_ref, total_ref) = refs[:groups], refs[groups:]
    offset, block = pl.program_id(0), pl.program_id(1)
    my_pos, my_freq = where_ref[0], where_ref[1]
    pos_global = my_pos * pos_local + offset
    cell_row = (my_pos // groups) ^ part
    my_group = lax.rem(my_pos, groups)
    first_freq = (my_freq * freq_local).astype(jnp.float32)
    centre_turns = 0.5 + (first_freq + 0.5 * (freq_local - 1)) / freqs
    half_step = 0.5 / freqs
    centre = pos_global.astype(jnp.float32) * (cell_spacing * TW * TILE_DEV / positions)

    row = lax.broadcasted_iota(jnp.int32, (16, LANES), 0)
    sub = row % TW
    cell_col = ((sub // per_dest) ^ my_group) * per_dest + sub % per_dest
    lane = lax.broadcasted_iota(jnp.int32, (16, LANES), 1)

    def rows(pair, _):
        first = foot_ref[pos_global, 2 * pair]
        second = foot_ref[pos_global, 2 * pair + 1]
        tile = jnp.where(row < TW, first, second)
        tile_row, tile_col = tile // TILE_DEV, tile % TILE_DEV
        grid_row = (tile_row * TH + cell_row).astype(jnp.float32)
        grid_col = (tile_col * TW + cell_col).astype(jnp.float32)
        depth = top_depth + cell_spacing * grid_row
        depth_square = depth * depth
        lateral = cell_spacing * grid_col
        for piece in range(ELEM_BLOCK // LANES):
            index = (block * ELEM_BLOCK + piece * LANES + lane).astype(jnp.float32)
            element = (index - 0.5 * (elements - 1)) * elem_pitch + centre
            across = lateral - element
            square = depth_square + across * across
            inverse = lax.rsqrt(square)
            distance = square * inverse
            for number, pair_of in enumerate(waves(distance, inverse, centre_turns, half_step, freq_local)):
                for part_of, wave in enumerate(pair_of):
                    start = (number * 2 + part_of) * ELEM_BLOCK + piece * LANES
                    green_ref[pl.ds(pl.multiple_of(pair * 16, 16), 16), start : start + LANES] = wave.astype(
                        jnp.bfloat16
                    )
        return 0

    lax.fori_loop(0, foot // 2, rows, 0)
    gain = jnp.dot(
        green_ref[...],
        basis_ref[...].reshape(freq_local * 2 * ELEM_BLOCK, -1),
        preferred_element_type=jnp.float32,
    )

    spans = [slice(start, start + LANES) for start in range(0, gain.shape[1], LANES)]

    @pl.when(block == 0)
    def _():
        for half, span in enumerate(spans):
            total_ref[half] = gain[:, span]

    @pl.when(block > 0)
    def _():
        for half, span in enumerate(spans):
            total_ref[half] = total_ref[half] + gain[:, span]

    @pl.when(block == pl.num_programs(1) - 1)
    def _():
        for group in range(groups):
            for cell in range(per_dest):
                for half, span in enumerate(spans):
                    out_refs[group][cell, :, span] = total_ref[half, pl.ds(group * per_dest + cell, foot, stride=TW), :]


def project(sizes, part, where, footprint, basis):
    pos_count, freqs, positions, elements, pos_local, freq_local, foot = sizes
    groups = pos_count // TH
    per_dest = TW // groups
    rank = basis.shape[-1]
    blocks = elements // ELEM_BLOCK
    rows = foot * TW
    flops = 2 * pos_local * rows * freq_local * 2 * elements * rank
    return pl.pallas_call(
        functools.partial(project_kernel, sizes, part),
        grid=(pos_local, blocks),
        in_specs=[
            pl.BlockSpec(memory_space=pltpu.SMEM),
            pl.BlockSpec(memory_space=pltpu.SMEM),
            pl.BlockSpec((None, freq_local, 2, ELEM_BLOCK, rank), lambda p, e: (p, 0, 0, e, 0)),
        ],
        out_specs=[pl.BlockSpec((per_dest, foot, rank), lambda p, e: (0, p, 0))] * groups,
        out_shape=[jax.ShapeDtypeStruct((per_dest, pos_local * foot, rank), jnp.float32)] * groups,
        scratch_shapes=[
            pltpu.VMEM((rows, freq_local * 2 * ELEM_BLOCK), jnp.bfloat16),
            pltpu.VMEM((rank // LANES, rows, LANES), jnp.float32),
        ],
        compiler_params=pltpu.CompilerParams(vmem_limit_bytes=VMEM_LIMIT),
        cost_estimate=pl.CostEstimate(flops=flops, bytes_accessed=basis.size * 2, transcendentals=0),
        name=f"project_{part}",
    )(where, footprint, basis)


def three_terms(values):
    high = values.astype(jnp.bfloat16)
    rest = values - high.astype(jnp.float32)
    mid = rest.astype(jnp.bfloat16)
    return high, mid, (rest - mid.astype(jnp.float32)).astype(jnp.bfloat16)


def gather_kernel(pos_count, freq_count, tile_rows, where_ref, ids_ref, *refs):
    in_refs, out_refs = refs[:pos_count], refs[pos_count:]
    cells, entries, rank = in_refs[0].shape
    shard = out_refs[0].shape[1]
    tile_cols = shard // tile_rows
    groups = pos_count // TH
    my_pos, my_freq = where_ref[0], where_ref[1]
    left = (lax.rem(my_pos, groups) * 2 >= groups).astype(jnp.int32)
    row = lax.broadcasted_iota(jnp.int32, (shard, entries), 0)
    wanted = (row % tile_rows) * TILE_DEV + row // tile_rows - left
    hot = []
    for other in range(freq_count):
        base = (my_freq ^ other) * (tile_cols - 1)
        col = row // tile_rows - left + base
        hot_row = []
        for source in range(pos_count):
            ids = ids_ref[pl.ds(my_pos ^ source, 1), :]
            hit = (wanted + base == ids) & (col >= 0) & (col < TILE_DEV)
            hot_row.append(hit.astype(jnp.float32).astype(jnp.bfloat16))
        hot_row = jnp.concatenate(hot_row, axis=1)
        hot.append(jnp.concatenate([hot_row] * 3, axis=1))
    for cell in range(cells):
        values = jnp.concatenate([ref[cell] for ref in in_refs], axis=0)
        terms = jnp.concatenate(three_terms(values), axis=0)
        for other in range(freq_count):
            out_refs[other][cell] = jnp.dot(hot[other], terms, preferred_element_type=jnp.float32)


def gather_tiles(freq_count, where, ids, parts):
    pos_count = len(parts)
    cells, entries, rank = parts[0].shape
    tile_rows = pos_count
    shard = (TILE_DEV // freq_count + 1) * tile_rows
    return pl.pallas_call(
        functools.partial(gather_kernel, pos_count, freq_count, tile_rows),
        in_specs=[pl.BlockSpec(memory_space=pltpu.SMEM)] + [pl.BlockSpec(memory_space=pltpu.VMEM)] * (1 + pos_count),
        out_specs=[pl.BlockSpec(memory_space=pltpu.VMEM)] * freq_count,
        out_shape=[jax.ShapeDtypeStruct((cells, shard, rank), jnp.float32)] * freq_count,
        compiler_params=pltpu.CompilerParams(vmem_limit_bytes=VMEM_LIMIT),
        name="tiles",
    )(where, ids, *parts)


def energy_kernel(freq_count, weights_ref, rims_ref, left_ref, right_ref, *refs):
    in_refs, out_ref = refs[:freq_count], refs[freq_count]
    cells, shard, rank = in_refs[0].shape
    weights = jnp.broadcast_to(weights_ref[...], (8, rank))
    for cell in range(cells):
        summed = in_refs[0][cell]
        for ref in in_refs[1:]:
            summed = summed + ref[cell]
        energy = lax.dot_general(
            weights,
            summed * summed,
            (((1,), (1,)), ((), ())),
            precision=HIGHEST,
            preferred_element_type=jnp.float32,
        )
        out_ref[pl.ds(cell, 1), 0:shard] = jnp.sqrt(energy[0:1] / rank + eps_value)
    rims, edge = rims_ref.shape, left_ref.shape[1]
    out_ref[cells : cells + rims[0], 0 : rims[1]] = rims_ref[...]
    out_ref[cells : cells + rims[0], rims[1] : rims[1] + edge] = right_ref[...]
    out_ref[cells : cells + rims[0], out_ref.shape[1] - edge :] = left_ref[...]


def energies(weights, rims, left, right, shards):
    cells, shard, rank = shards[0].shape
    rows = cells + rims.shape[0]
    width = -(-max(shard, rims.shape[1] + 2 * left.shape[1]) // LANES) * LANES
    return pl.pallas_call(
        functools.partial(energy_kernel, len(shards)),
        in_specs=[pl.BlockSpec(memory_space=pltpu.VMEM)] * (4 + len(shards)),
        out_specs=pl.BlockSpec(memory_space=pltpu.VMEM),
        out_shape=jax.ShapeDtypeStruct((rows, width), jnp.float32),
        compiler_params=pltpu.CompilerParams(vmem_limit_bytes=VMEM_LIMIT),
        name="energies",
    )(weights, rims, left, right, *shards)


def diffuse_kernel(cells, shard, where_ref, strips_ref, out_ref, field_ref):
    pos_count, _, width = strips_ref.shape
    tile_rows = pos_count
    tile_cols = shard // tile_rows
    groups = pos_count // TH
    my_pos = where_ref[0]
    tile_row = lax.broadcasted_iota(jnp.int32, (tile_rows, width), 0)
    spot = lax.broadcasted_iota(jnp.int32, (tile_rows, width), 1)
    here = (spot % tile_rows == tile_row) & (spot < shard)
    source = lax.broadcasted_iota(jnp.int32, (width, LANES), 0)
    target = lax.broadcasted_iota(jnp.int32, (width, LANES), 1)
    field = [jnp.zeros((tile_rows, LANES), jnp.float32) for _ in range(TH)]
    for group in range(groups):
        left = 1 if group * 2 >= groups else 0
        for cell in range(cells):
            col = (source // tile_rows - left) * TW + group * cells + cell
            place = ((target == (col + LANES) % LANES) & (source < shard)).astype(jnp.float32)
            for row in range(TH):
                line = strips_ref[row * groups + group, pl.ds(cell, 1), :]
                spread = jnp.where(here, jnp.broadcast_to(line, (tile_rows, width)), 0.0)
                field[row] = field[row] + jnp.dot(
                    spread, place, precision=HIGHEST, preferred_element_type=jnp.float32
                )

    def strip(which, row):
        return strips_ref[:, cells + which * TH + row, 0:LANES]

    across_k = [strip(0, row) for row in range(TH)]
    along_k = [strip(1, row) for row in range(TH)]
    field = [field[row] + strip(2, row) for row in range(TH)]

    def above(rows, row):
        if row:
            return rows[row - 1]
        return jnp.where(tile_row[:, :LANES] == 0, 0.0, pltpu.roll(rows[TH - 1], 1, 0))

    def below(rows, row):
        if row < TH - 1:
            return rows[row + 1]
        return jnp.where(tile_row[:, :LANES] == tile_rows - 1, 0.0, pltpu.roll(rows[0], tile_rows - 1, 0))

    north_k = [jnp.minimum(across_k[r], above(across_k, r)) for r in range(TH)]
    south_k = [jnp.minimum(across_k[r], below(across_k, r)) for r in range(TH)]
    west_k = [jnp.minimum(k, pltpu.roll(k, 1, 1)) for k in along_k]
    east_k = [jnp.minimum(k, pltpu.roll(k, LANES - 1, 1)) for k in along_k]
    for _ in range(PASSES):
        field = [
            field[r]
            + north_k[r] * (above(field, r) - field[r])
            + south_k[r] * (below(field, r) - field[r])
            + west_k[r] * (pltpu.roll(field[r], 1, 1) - field[r])
            + east_k[r] * (pltpu.roll(field[r], LANES - 1, 1) - field[r])
            for r in range(TH)
        ]
    for row in range(TH):
        field_ref[...] = field[row]
        out_ref[pl.ds(row, 1), :] = field_ref[pl.ds(my_pos, 1), 0 : out_ref.shape[1]]


def diffuse(cells, shard, where, strips, columns):
    return pl.pallas_call(
        functools.partial(diffuse_kernel, cells, shard),
        in_specs=[pl.BlockSpec(memory_space=pltpu.SMEM), pl.BlockSpec(memory_space=pltpu.VMEM)],
        out_specs=pl.BlockSpec(memory_space=pltpu.VMEM),
        out_shape=jax.ShapeDtypeStruct((TH, columns), jnp.float32),
        scratch_shapes=[pltpu.VMEM((strips.shape[0], LANES), jnp.float32)],
        compiler_params=pltpu.CompilerParams(vmem_limit_bytes=VMEM_LIMIT),
        name="diffuse",
    )(where, strips)


def swap(array, axis, distance):
    return lax.ppermute(array, axis, [(i, i ^ distance) for i in range(lax.axis_size(axis))])


def body(footprint, basis, weights, conduct, baseline):
    pos_local, freq_local, doubled, rank = basis.shape
    elements = doubled // 2
    foot = footprint.shape[1]
    pos_count = lax.axis_size("pos")
    freq_count = lax.axis_size("freq")
    columns = baseline.shape[1]
    sizes = (
        pos_count,
        freq_local * freq_count,
        pos_local * pos_count,
        elements,
        pos_local,
        freq_local,
        foot,
    )
    where = jnp.stack([lax.axis_index("pos"), lax.axis_index("freq")]).astype(jnp.int32)
    ids = footprint.reshape(pos_count, pos_local * foot)
    rims = jnp.concatenate([conduct[0], conduct[1], baseline], axis=0)
    left = lax.ppermute(rims[:, columns - TW :], "freq", [(i, i + 1) for i in range(freq_count - 1)])
    right = lax.ppermute(rims[:, :TW], "freq", [(i + 1, i) for i in range(freq_count - 1)])
    split = basis.reshape(pos_local, freq_local, 2, elements, rank)
    groups = pos_count // TH
    parts = [None] * pos_count
    for part in range(TH - 1, -1, -1):
        sent = project(sizes, part, where, footprint, split)
        for group in range(groups):
            distance = part * groups + group
            parts[distance] = swap(sent[group], "pos", distance) if distance else sent[group]
    tiles = gather_tiles(freq_count, where, ids, parts)
    shards = [swap(tiles[d], "freq", d) if d else tiles[d] for d in range(freq_count)]
    strip = energies(weights.reshape(1, rank), rims, left, right, shards)
    strips = lax.all_gather(strip, "pos")
    return diffuse(CELLS // pos_count, shards[0].shape[1], where, strips, columns)


def solution(mesh):
    return jax.shard_map(
        body,
        mesh=mesh,
        in_specs=(P(), P("pos", "freq", None, None), P(), P(None, "pos", "freq"), P("pos", "freq")),
        out_specs=P("pos", "freq"),
        check_vma=False,
    )
```

time: 389 us -> 126 us (0.32); the launches traced: 383 us -> 126 us
  other arithmetic: 170 us -> 0.08 us
  Pallas kernels: 0 us -> 67.1 us
  matrix products: 42.5 us -> 0 us
  waiting for transfers between devices: 72.5 us -> 32 us
  starting transfers between devices: 49.9 us -> 16 us
  local copies, waits for them, and re-layouts: 26.9 us -> 0.86 us
  between operations: 13.7 us -> 0.12 us
  blocking collectives: 0 us -> 9.49 us
  loops' own time: 7.19 us -> 0 us
    another operation x10 -> x1, other arithmetic: 165 us -> 0.07 us  [body(): jnp.stack([lax.axis_index('pos'), lax.axis_index('freq')]).astype(jnp.int32)]
    pallas_call x0 -> x7, Pallas kernels: none -> 67.1 us  [the longest x4 61.6 us: project(): pl.pallas_call(functools.partial(project_kernel, sizes, part), grid=(pos_...]
    all_to_all x1 -> x0, waiting for transfers between devices: 45 us -> none  [body(): lax.all_to_all(packed.reshape(pos_count, capacity, -1), 'pos', split_axis...]
    dot_general x10 -> x0, matrix products: 42.5 us -> none  [the longest x8 33.1 us: add_freq(): jnp.dot(green, freq_basis, preferred_element_type=jnp.float32)]
    ppermute x16 -> x12, starting transfers between devices: 44.7 us -> 16 us  [the longest x10 10.7 us: swap(): lax.ppermute(array, axis, [(i, i ^ distance) for i in range(lax.axis_size...]
    ppermute x16 -> x12, waiting for transfers between devices: 18.7 us -> 32 us  [the longest x1 20.1 us: body(): lax.ppermute(rims[:, columns - TW:], 'freq', [(i, i + 1) for i in range(f...]
    all_gather x0 -> x1, blocking collectives: none -> 9.49 us  [body(): strips = lax.all_gather(strip, 'pos')]
    reduce_scatter x1 -> x0, waiting for transfers between devices: 8.84 us -> none  [body(): summed = lax.psum_scatter(compound, 'freq', scatter_dimension=0, tiled=True)]
  transfers between devices with their start and end apart: 18 -> 12, of which waited for: 10 -> 3; matrix products, arithmetic and copies ran while one was open for 0% -> 0% of each run, Pallas kernels for 0% -> 37%
where the time goes in v1:
time: 126 us
  Pallas kernels  67.1 us (53%)
  waiting for transfers between devices  32 us (25%)
  starting transfers between devices  16 us (13%)
  blocking collectives  9.49 us (8%)
    pallas_call x4, Pallas kernels, project(): pl.pallas_call(functools.partial(project_kernel, sizes, part), grid=(pos_...  61.6 us
    ppermute x1, waiting for transfers between devices, body(): lax.ppermute(rims[:, columns - TW:], 'freq', [(i, i + 1) for i in range(f...  20.1 us
    ppermute x10, waiting for transfers between devices, swap(): lax.ppermute(array, axis, [(i, i ^ distance) for i in range(lax.axis_size...  11.9 us
    ppermute x10, starting transfers between devices, swap(): lax.ppermute(array, axis, [(i, i ^ distance) for i in range(lax.axis_size...  10.7 us
    all_gather x1, blocking collectives, body(): strips = lax.all_gather(strip, 'pos')  9.49 us
    ppermute x1, starting transfers between devices, body(): lax.ppermute(rims[:, :TW], 'freq', [(i + 1, i) for i in range(freq_count...  3.04 us
    pallas_call x1, Pallas kernels, gather_tiles(): pl.pallas_call(functools.partial(gather_kernel, pos_count, freq_count, ti...  2.8 us
  transfers between devices with their start and end apart: 12, of which 3 were waited for; matrix products, arithmetic and copies ran while one was open for 0% of the time, Pallas kernels for 37%

profile of v1, /device:TPU:17, one launch (start us, length us, event | category | flops | bytes accessed | tf_op | source)
XLA Modules:
  0.0 125.7 jit_solution(6857380817326223144)
XLA Ops:
  0.0 0.1 pad_add_fusion.where_ref
  0.1 0.0 copy-start
  0.1 0.7 copy-done
  0.8 15.4 %project_0.1 = (f32[4,64,256]{2,1,0:T(8,128)S(1)}, f32[4,64,256]{2,1,0:T(8,128)S(1)}) custom-call(s32[2]{0:T(128)S(1)} %pad_add_fusion.where_ref, s32[16,32]{1,0:T(8,128)S(1)} %copy-done, bf16[2,4,2,1024,256]{4,3,2,1,0:T(8,128)(2,1)} %bitcast.11), custom_call_target="tpu_custom_call" | custom-call | flops 2147483648 | bytes 8388608 | tf_op jit(solution)/shard_map/project_0/pallas_call | solution.py:145
  16.2 0.8 collective-permute-start.2
  16.9 15.4 %project_1.1 = (f32[4,64,256]{2,1,0:T(8,128)S(1)}, f32[4,64,256]{2,1,0:T(8,128)S(1)}) custom-call(s32[2]{0:T(128)S(1)} %pad_add_fusion.where_ref, s32[16,32]{1,0:T(8,128)S(1)} %copy-done, bf16[2,4,2,1024,256]{4,3,2,1,0:T(8,128)(2,1)} %bitcast.12), custom_call_target="tpu_custom_call" | custom-call | flops 2147483648 | bytes 8388608 | tf_op jit(solution)/shard_map/project_1/pallas_call | solution.py:145
  32.3 1.3 %collective-permute-start.3 = (f32[4,64,256]{2,1,0:T(8,128)S(1)}, f32[4,64,256]{2,1,0:T(8,128)S(1)}, u32[]{:S(2)}, u32[]{:S(2)}) collective-permute-start(f32[4,64,256]{2,1,0:T(8,128)S(1)} %get-tuple-element.19), channel_id=1, source_target_pairs={{0,8},{4,12},{8,0},{12,4},{16,24},{20,28},{24,16},{28,20},{1,9},{5... | collective-permute-start | bytes 786440 | tf_op jit(solution)/shard_map/ppermute | solution.py:323
  33.6 0.0 copy-start.1
  33.6 0.0 copy-start.3
  33.6 0.0 copy-start.4
  33.6 0.0 copy-start.2
  33.6 0.6 collective-permute-start.4
  34.2 15.4 %project_2.1 = (f32[4,64,256]{2,1,0:T(8,128)S(1)}, f32[4,64,256]{2,1,0:T(8,128)S(1)}) custom-call(s32[2]{0:T(128)S(1)} %pad_add_fusion.where_ref, s32[16,32]{1,0:T(8,128)S(1)} %copy-done, bf16[2,4,2,1024,256]{4,3,2,1,0:T(8,128)(2,1)} %bitcast.13), custom_call_target="tpu_custom_call" | custom-call | flops 2147483648 | bytes 8388608 | tf_op jit(solution)/shard_map/project_2/pallas_call | solution.py:145
  49.6 1.3 %collective-permute-start.5 = (f32[4,64,256]{2,1,0:T(8,128)S(1)}, f32[4,64,256]{2,1,0:T(8,128)S(1)}, u32[]{:S(2)}, u32[]{:S(2)}) collective-permute-start(f32[4,64,256]{2,1,0:T(8,128)S(1)} %get-tuple-element.21), channel_id=1, source_target_pairs={{0,16},{4,20},{8,24},{12,28},{16,0},{20,4},{24,8},{28,12},{1,17},{... | collective-permute-start | bytes 786440 | tf_op jit(solution)/shard_map/ppermute | solution.py:323
  50.9 0.6 collective-permute-start.6
  51.4 15.4 %project_3.1 = (f32[4,64,256]{2,1,0:T(8,128)S(1)}, f32[4,64,256]{2,1,0:T(8,128)S(1)}) custom-call(s32[2]{0:T(128)S(1)} %pad_add_fusion.where_ref, s32[16,32]{1,0:T(8,128)S(1)} %copy-done, bf16[2,4,2,1024,256]{4,3,2,1,0:T(8,128)(2,1)} %bitcast.14), custom_call_target="tpu_custom_call" | custom-call | flops 2147483648 | bytes 8388608 | tf_op jit(solution)/shard_map/project_3/pallas_call | solution.py:145
  66.9 0.0 collective-permute-done.2.refs_1_
  66.9 2.2 %collective-permute-start.7 = (f32[4,64,256]{2,1,0:T(8,128)S(1)}, f32[4,64,256]{2,1,0:T(8,128)S(1)}, u32[]{:S(2)}, u32[]{:S(2)}) collective-permute-start(f32[4,64,256]{2,1,0:T(8,128)S(1)} %get-tuple-element.23), channel_id=1, source_target_pairs={{0,24},{4,28},{8,16},{12,20},{16,8},{20,12},{24,0},{28,4},{1,25},{... | collective-permute-start | bytes 786440 | tf_op jit(solution)/shard_map/ppermute | solution.py:323
  69.1 0.0 collective-permute-done.3.refs_2_
  69.1 0.4 collective-permute-start.8
  69.5 0.0 copy-done.1
  69.5 0.1 reshape.10.ids_ref
  69.6 0.0 copy-done.3
  69.6 0.0 collective-permute-done.4.refs_3_
  69.6 0.0 collective-permute-done.5.refs_4_
  69.6 0.0 collective-permute-done.6.refs_5_
  69.6 6.1 %collective-permute-done.7.refs_6_ = f32[4,64,256]{2,1,0:T(8,128)S(1)} collective-permute-done((f32[4,64,256]{2,1,0:T(8,128)S(1)}, f32[4,64,256]{2,1,0:T(8,128)S(1)}, u32[]{:S(2)}, u32[]{:S(2)}) %collective-permute-start.7) | collective-permute-done | bytes 262176 | tf_op jit(solution)/shard_map/ppermute | solution.py:323
  75.7 5.8 %collective-permute-done.8.refs_7_ = f32[4,64,256]{2,1,0:T(8,128)S(1)} collective-permute-done((f32[4,64,256]{2,1,0:T(8,128)S(1)}, f32[4,64,256]{2,1,0:T(8,128)S(1)}, u32[]{:S(2)}, u32[]{:S(2)}) %collective-permute-start.8) | collective-permute-done | bytes 262176 | tf_op jit(solution)/shard_map/ppermute | solution.py:323
  81.5 2.8 %tiles.1 = (f32[4,72,256]{2,1,0:T(8,128)S(1)}, f32[4,72,256]{2,1,0:T(8,128)S(1)}, f32[4,72,256]{2,1,0:T(8,128)S(1)}, f32[4,72,256]{2,1,0:T(8,128)S(1)}) custom-call(s32[2]{0:T(128)S(1)} %pad_add_fusion.where_ref, s32[8,64]{1,0:T(8,128)S(1)} %reshape.10.ids_ref, f32[4,64,256]{2,1,0:T(8,128)S(1)} %get-tuple-element.17.refs_0_, ...), custom_call_target="tpu_custom_call" | custom-call | tf_op jit(solution)/shard_map/tiles/pallas_call | solution.py:205
  84.3 0.1 collective-permute-start.10
  84.4 2.4 %collective-permute-start.11 = (f32[4,72,256]{2,1,0:T(8,128)S(1)}, f32[4,72,256]{2,1,0:T(8,128)S(1)}, u32[]{:S(2)}, u32[]{:S(2)}) collective-permute-start(f32[4,72,256]{2,1,0:T(8,128)S(1)} %get-tuple-element.28), channel_id=1, source_target_pairs={{0,3},{1,2},{2,1},{3,0},{4,7},{5,6},{6,5},{7,4},{8,11},{9,10},{10,... | collective-permute-start | bytes 884744 | tf_op jit(solution)/shard_map/ppermute | solution.py:323
  86.8 1.1 collective-permute-start.9
  87.9 0.0 copy-done.4
  87.9 0.1 fusion
  88.0 2.2 %collective-permute-start = (f32[12,8]{1,0:T(8,128)S(1)}, f32[12,8]{1,0:T(8,128)S(1)}, u32[]{:S(2)}, u32[]{:S(2)}) collective-permute-start(f32[12,8]{1,0:T(8,128)S(1)} %get-tuple-element.30), channel_id=1, source_target_pairs={{0,1},{1,2},{2,3},{4,5},{5,6},{6,7},{8,9},{9,10},{10,11},{12,13},{... | collective-permute-start | bytes 1160 | tf_op jit(solution)/shard_map/ppermute | solution.py:345
  90.2 3.0 %collective-permute-start.1 = (f32[12,8]{1,0:T(8,128)S(1)}, f32[12,8]{1,0:T(8,128)S(1)}, u32[]{:S(2)}, u32[]{:S(2)}) collective-permute-start(f32[12,8]{1,0:T(8,128)S(1)} %get-tuple-element.29), channel_id=1, source_target_pairs={{1,0},{2,1},{3,2},{5,4},{6,5},{7,6},{9,8},{10,9},{11,10},{13,12},{... | collective-permute-start | bytes 1160 | tf_op jit(solution)/shard_map/ppermute | solution.py:346
  93.3 20.1 %collective-permute-done.left_ref = f32[12,8]{1,0:T(8,128)S(1)} collective-permute-done((f32[12,8]{1,0:T(8,128)S(1)}, f32[12,8]{1,0:T(8,128)S(1)}, u32[]{:S(2)}, u32[]{:S(2)}) %collective-permute-start) | collective-permute-done | bytes 416 | tf_op jit(solution)/shard_map/ppermute | solution.py:345
  113.4 0.0 collective-permute-done.1.right_ref
  113.4 0.0 collective-permute-done.10.refs_2_
  113.4 0.0 collective-permute-done.11.refs_3_
  113.4 0.0 collective-permute-done.9.refs_1_
  113.4 0.0 copy-done.2
  113.4 0.4 energies.1
  113.8 9.5 %all-gather = f32[128,128]{1,0:T(8,128)S(1)} all-gather(f32[16,128]{1,0:T(8,128)S(1)} %energies.1), channel_id=2, replica_groups=mesh['pos'=8,'freq'=4] {'pos'}, dimensions={0}, use_global_device_ids=true | all-gather | bytes 73728 | tf_op jit(solution)/shard_map/all_gather | solution.py:358
  123.3 2.4 %diffuse.1 = f32[4,64]{1,0:T(4,128)} custom-call(s32[2]{0:T(128)S(1)} %pad_add_fusion.where_ref, f32[8,16,128]{2,1,0:T(8,128)S(1)} %bitcast.9), custom_call_target="tpu_custom_call" | custom-call | tf_op jit(solution)/shard_map/diffuse/pallas_call | solution.py:311
  (2 shorter events, 0.0 us)
Async XLA Ops:
  0.1 0.7 copy-start
  16.2 50.7 %collective-permute-start.2 = (f32[4,64,256]{2,1,0:T(8,128)S(1)}, f32[4,64,256]{2,1,0:T(8,128)S(1)}, u32[]{:S(2)}, u32[]{:S(2)}) collective-permute-start(f32[4,64,256]{2,1,0:T(8,128)S(1)} %get-tuple-element.18), channel_id=1, source_target_pairs={{0,4},{4,0},{8,12},{12,8},{16,20},{20,16},{24,28},{28,24},{1,5},{5... | collective-permute-start | bytes 786440 | tf_op jit(solution)/shard_map/ppermute | solution.py:323
  32.3 36.8 %collective-permute-start.3 = (f32[4,64,256]{2,1,0:T(8,128)S(1)}, f32[4,64,256]{2,1,0:T(8,128)S(1)}, u32[]{:S(2)}, u32[]{:S(2)}) collective-permute-start(f32[4,64,256]{2,1,0:T(8,128)S(1)} %get-tuple-element.19), channel_id=1, source_target_pairs={{0,8},{4,12},{8,0},{12,4},{16,24},{20,28},{24,16},{28,20},{1,9},{5... | collective-permute-start | bytes 786440 | tf_op jit(solution)/shard_map/ppermute | solution.py:323
  33.6 35.9 %copy-start.1 = (s32[16,32]{1,0:T(8,128)S(1)}, s32[16,32]{1,0:T(8,128)}, u32[]{:S(2)}) copy-start(s32[16,32]{1,0:T(8,128)} %foot_ref.7) | copy-start | bytes 6148
  33.6 36.0 %copy-start.3 = (f32[2,4,64]{2,1,0:T(4,128)S(1)}, f32[2,4,64]{2,1,0:T(4,128)}, u32[]{:S(2)}) copy-start(f32[2,4,64]{2,1,0:T(4,128)} %param.8) | copy-start | bytes 6148
  33.6 54.3 %copy-start.4 = (f32[4,64]{1,0:T(4,128)S(1)}, f32[4,64]{1,0:T(4,128)}, u32[]{:S(2)}) copy-start(f32[4,64]{1,0:T(4,128)} %param.9) | copy-start | bytes 3076
  33.6 79.8 %copy-start.2 = (f32[256]{0:T(256)S(1)}, f32[256]{0:T(256)}, u32[]{:S(2)}) copy-start(f32[256]{0:T(256)} %param.7) | copy-start | bytes 3076
  33.6 36.0 %collective-permute-start.4 = (f32[4,64,256]{2,1,0:T(8,128)S(1)}, f32[4,64,256]{2,1,0:T(8,128)S(1)}, u32[]{:S(2)}, u32[]{:S(2)}) collective-permute-start(f32[4,64,256]{2,1,0:T(8,128)S(1)} %get-tuple-element.20), channel_id=1, source_target_pairs={{0,12},{4,8},{8,4},{12,0},{16,28},{20,24},{24,20},{28,16},{1,13},{... | collective-permute-start | bytes 786440 | tf_op jit(solution)/shard_map/ppermute | solution.py:323
  49.6 20.0 %collective-permute-start.5 = (f32[4,64,256]{2,1,0:T(8,128)S(1)}, f32[4,64,256]{2,1,0:T(8,128)S(1)}, u32[]{:S(2)}, u32[]{:S(2)}) collective-permute-start(f32[4,64,256]{2,1,0:T(8,128)S(1)} %get-tuple-element.21), channel_id=1, source_target_pairs={{0,16},{4,20},{8,24},{12,28},{16,0},{20,4},{24,8},{28,12},{1,17},{... | collective-permute-start | bytes 786440 | tf_op jit(solution)/shard_map/ppermute | solution.py:323
  50.9 18.7 %collective-permute-start.6 = (f32[4,64,256]{2,1,0:T(8,128)S(1)}, f32[4,64,256]{2,1,0:T(8,128)S(1)}, u32[]{:S(2)}, u32[]{:S(2)}) collective-permute-start(f32[4,64,256]{2,1,0:T(8,128)S(1)} %get-tuple-element.22), channel_id=1, source_target_pairs={{0,20},{4,16},{8,28},{12,24},{16,4},{20,0},{24,12},{28,8},{1,21},{... | collective-permute-start | bytes 786440 | tf_op jit(solution)/shard_map/ppermute | solution.py:323
  66.9 8.9 %collective-permute-start.7 = (f32[4,64,256]{2,1,0:T(8,128)S(1)}, f32[4,64,256]{2,1,0:T(8,128)S(1)}, u32[]{:S(2)}, u32[]{:S(2)}) collective-permute-start(f32[4,64,256]{2,1,0:T(8,128)S(1)} %get-tuple-element.23), channel_id=1, source_target_pairs={{0,24},{4,28},{8,16},{12,20},{16,8},{20,12},{24,0},{28,4},{1,25},{... | collective-permute-start | bytes 786440 | tf_op jit(solution)/shard_map/ppermute | solution.py:323
  69.1 12.4 %collective-permute-start.8 = (f32[4,64,256]{2,1,0:T(8,128)S(1)}, f32[4,64,256]{2,1,0:T(8,128)S(1)}, u32[]{:S(2)}, u32[]{:S(2)}) collective-permute-start(f32[4,64,256]{2,1,0:T(8,128)S(1)} %get-tuple-element.24), channel_id=1, source_target_pairs={{0,28},{4,24},{8,20},{12,16},{16,12},{20,8},{24,4},{28,0},{1,29},{... | collective-permute-start | bytes 786440 | tf_op jit(solution)/shard_map/ppermute | solution.py:323
  84.3 29.1 %collective-permute-start.10 = (f32[4,72,256]{2,1,0:T(8,128)S(1)}, f32[4,72,256]{2,1,0:T(8,128)S(1)}, u32[]{:S(2)}, u32[]{:S(2)}) collective-permute-start(f32[4,72,256]{2,1,0:T(8,128)S(1)} %get-tuple-element.27), channel_id=1, source_target_pairs={{0,2},{1,3},{2,0},{3,1},{4,6},{5,7},{6,4},{7,5},{8,10},{9,11},{10,... | collective-permute-start | bytes 884744 | tf_op jit(solution)/shard_map/ppermute | solution.py:323
  84.4 29.0 %collective-permute-start.11 = (f32[4,72,256]{2,1,0:T(8,128)S(1)}, f32[4,72,256]{2,1,0:T(8,128)S(1)}, u32[]{:S(2)}, u32[]{:S(2)}) collective-permute-start(f32[4,72,256]{2,1,0:T(8,128)S(1)} %get-tuple-element.28), channel_id=1, source_target_pairs={{0,3},{1,2},{2,1},{3,0},{4,7},{5,6},{6,5},{7,4},{8,11},{9,10},{10,... | collective-permute-start | bytes 884744 | tf_op jit(solution)/shard_map/ppermute | solution.py:323
  86.8 26.6 %collective-permute-start.9 = (f32[4,72,256]{2,1,0:T(8,128)S(1)}, f32[4,72,256]{2,1,0:T(8,128)S(1)}, u32[]{:S(2)}, u32[]{:S(2)}) collective-permute-start(f32[4,72,256]{2,1,0:T(8,128)S(1)} %get-tuple-element.26), channel_id=1, source_target_pairs={{0,1},{1,0},{2,3},{3,2},{4,5},{5,4},{6,7},{7,6},{8,9},{9,8},{10,11... | collective-permute-start | bytes 884744 | tf_op jit(solution)/shard_map/ppermute | solution.py:323
  88.0 25.4 %collective-permute-start = (f32[12,8]{1,0:T(8,128)S(1)}, f32[12,8]{1,0:T(8,128)S(1)}, u32[]{:S(2)}, u32[]{:S(2)}) collective-permute-start(f32[12,8]{1,0:T(8,128)S(1)} %get-tuple-element.30), channel_id=1, source_target_pairs={{0,1},{1,2},{2,3},{4,5},{5,6},{6,7},{8,9},{9,10},{10,11},{12,13},{... | collective-permute-start | bytes 1160 | tf_op jit(solution)/shard_map/ppermute | solution.py:345
  90.2 23.2 %collective-permute-start.1 = (f32[12,8]{1,0:T(8,128)S(1)}, f32[12,8]{1,0:T(8,128)S(1)}, u32[]{:S(2)}, u32[]{:S(2)}) collective-permute-start(f32[12,8]{1,0:T(8,128)S(1)} %get-tuple-element.29), channel_id=1, source_target_pairs={{1,0},{2,1},{3,2},{5,4},{6,5},{7,6},{9,8},{10,9},{11,10},{13,12},{... | collective-permute-start | bytes 1160 | tf_op jit(solution)/shard_map/ppermute | solution.py:346

commit v2 on v1

--- a/solution.py
+++ b/solution.py
@@ -1,4 +1,5 @@
 import functools
+import math
 
 import jax
 import jax.numpy as jnp
@@ -20,39 +21,39 @@
 top_depth = 4.0
 eps_value = 1e-06
 
-COS_PI = (0.9999999403953552, -4.934792995452881, 4.058411121368408, -1.331876516342163, 0.21968960762023926)
-SIN_PI = (3.1415927410125732, -5.167710304260254, 2.550077438354492, -0.598291277885437, 0.07765766233205795)
+SIN_PI = tuple(
+    math.sqrt(2.0) * term
+    for term in (3.1415927410125732, -5.167710304260254, 2.550077438354492, -0.598291277885437, 0.07765766233205795)
+)
+TINY = 1e-12
 
 HIGHEST = lax.Precision.HIGHEST
-VMEM_LIMIT = 48 * 1024 * 1024
+VMEM_LIMIT = 24 * 1024 * 1024
 
 
 def half_turn(turns):
     x = turns - jnp.round(turns)
     square = x * x
-    c = COS_PI[-1]
-    for term in COS_PI[-2::-1]:
-        c = c * square + term
     s = SIN_PI[-1]
     for term in SIN_PI[-2::-1]:
         s = s * square + term
-    return c, s * x
-
-
-def waves(distance, inverse, centre_turns, half_step, count):
-    c, s = half_turn(centre_turns * distance)
-    amplitude = 2.0 * (inverse * lax.rsqrt(inverse))
-    twice = (amplitude + amplitude) * c
-    mid_c = twice * c - amplitude
-    mid_s = twice * s
-    c, s = half_turn(half_step * distance)
-    twice = c + c
-    step_c = twice * c - 1.0
-    step_s = twice * s
+    s = s * x
+    rest = jnp.maximum(2.0 - s * s, TINY)
+    return rest * lax.rsqrt(rest), s, rest - 1.0
+
+
+def waves(distance, centre_turns, half_step, count):
+    c, s, cosine = half_turn(centre_turns * distance)
+    amplitude = lax.rsqrt(distance * (1.0 / top_depth))
+    mid_c = amplitude * cosine
+    mid_s = (amplitude * c) * s
+    c, s, step_c = half_turn(half_step * distance)
+    step_s = c * s
     cc, ss, cs, sc = mid_c * step_c, mid_s * step_s, mid_c * step_s, mid_s * step_c
     low, high = (cc + ss, sc - cs), (cc - ss, sc + cs)
     lows, highs = [low], [high]
-    factor = 4.0 * (step_c * step_c) - 2.0
+    twice = step_c + step_c
+    factor = twice * twice - 2.0
     before_low, before_high = high, low
     for _ in range(count // 2 - 1):
         low, before_low = tuple(factor * a - b for a, b in zip(low, before_low)), low
@@ -62,104 +63,145 @@
     return lows[::-1] + highs
 
 
-def project_kernel(sizes, part, where_ref, foot_ref, basis_ref, *refs):
+def project_kernel(sizes, part, first, where_ref, foot_ref, basis_ref, after_ref, *refs):
     pos_count, freqs, positions, elements, pos_local, freq_local, foot = sizes
     groups = pos_count // TH
     per_dest = TW // groups
-    out_refs, (green_ref, total_ref) = refs[:groups], refs[groups:]
-    offset, block = pl.program_id(0), pl.program_id(1)
+    blocks = elements // ELEM_BLOCK
+    steps = pos_local * blocks
+    rows = foot * TW
+    out_refs, refs = refs[:groups], refs[groups:]
+    if first:
+        held_ref, refs, sems = refs[0], refs[1:-1], refs[-1]
+    else:
+        held_ref = basis_ref
+    green_even, green_odd, total_ref, depth_ref, lateral_ref, element_ref = refs
     my_pos, my_freq = where_ref[0], where_ref[1]
-    pos_global = my_pos * pos_local + offset
+
+    def fetch(step):
+        offset, block = step // blocks, step % blocks
+        spot = pl.ds(block * ELEM_BLOCK, ELEM_BLOCK)
+        return pltpu.make_async_copy(basis_ref.at[offset, :, :, spot, :], held_ref.at[step], sems.at[step])
+
+    if first:
+        for step in range(steps):
+            fetch(step).start()
+
     cell_row = (my_pos // groups) ^ part
     my_group = lax.rem(my_pos, groups)
     first_freq = (my_freq * freq_local).astype(jnp.float32)
     centre_turns = 0.5 + (first_freq + 0.5 * (freq_local - 1)) / freqs
     half_step = 0.5 / freqs
-    centre = pos_global.astype(jnp.float32) * (cell_spacing * TW * TILE_DEV / positions)
-
-    row = lax.broadcasted_iota(jnp.int32, (16, LANES), 0)
-    sub = row % TW
-    cell_col = ((sub // per_dest) ^ my_group) * per_dest + sub % per_dest
-    lane = lax.broadcasted_iota(jnp.int32, (16, LANES), 1)
-
-    def rows(pair, _):
-        first = foot_ref[pos_global, 2 * pair]
-        second = foot_ref[pos_global, 2 * pair + 1]
-        tile = jnp.where(row < TW, first, second)
-        tile_row, tile_col = tile // TILE_DEV, tile % TILE_DEV
-        grid_row = (tile_row * TH + cell_row).astype(jnp.float32)
-        grid_col = (tile_col * TW + cell_col).astype(jnp.float32)
-        depth = top_depth + cell_spacing * grid_row
-        depth_square = depth * depth
-        lateral = cell_spacing * grid_col
-        for piece in range(ELEM_BLOCK // LANES):
-            index = (block * ELEM_BLOCK + piece * LANES + lane).astype(jnp.float32)
-            element = (index - 0.5 * (elements - 1)) * elem_pitch + centre
-            across = lateral - element
-            square = depth_square + across * across
-            inverse = lax.rsqrt(square)
-            distance = square * inverse
-            for number, pair_of in enumerate(waves(distance, inverse, centre_turns, half_step, freq_local)):
-                for part_of, wave in enumerate(pair_of):
-                    start = (number * 2 + part_of) * ELEM_BLOCK + piece * LANES
-                    green_ref[pl.ds(pl.multiple_of(pair * 16, 16), 16), start : start + LANES] = wave.astype(
-                        jnp.bfloat16
-                    )
+
+    row = lax.broadcasted_iota(jnp.int32, (TW, LANES), 0)
+    lane = lax.broadcasted_iota(jnp.int32, (TW, LANES), 1)
+    cell_col = ((row // per_dest) ^ my_group) * per_dest + row % per_dest
+    for offset in range(pos_local):
+        pos_global = my_pos * pos_local + offset
+        centre = pos_global.astype(jnp.float32) * (cell_spacing * TW * TILE_DEV / positions)
+        for piece in range(elements // LANES):
+            index = (piece * LANES + lane).astype(jnp.float32)
+            element_ref[offset, piece] = (index - 0.5 * (elements - 1)) * elem_pitch + centre
+
+        def place(entry, _, offset=offset, pos_global=pos_global):
+            tile = foot_ref[pos_global, entry]
+            grid_row = (tile // TILE_DEV) * TH + cell_row
+            grid_col = ((tile % TILE_DEV) * TW + cell_col).astype(jnp.float32)
+            depth = top_depth + cell_spacing * jnp.full((TW, LANES), grid_row, jnp.int32).astype(jnp.float32)
+            depth_ref[offset, entry] = depth * depth
+            lateral_ref[offset, entry] = cell_spacing * grid_col
+            return 0
+
+        lax.fori_loop(0, foot, place, 0, unroll=4)
+    total_ref[...] = jnp.zeros_like(total_ref)
+
+    def green(step, green_ref):
+        offset, block = step // blocks, step % blocks
+        for pair in range(foot // 2):
+            entry = 2 * pair
+            depth_square = depth_ref[offset, pl.ds(entry, 2)].reshape(2 * TW, LANES)
+            lateral = lateral_ref[offset, pl.ds(entry, 2)].reshape(2 * TW, LANES)
+            spot = pl.ds(entry * TW, 2 * TW)
+            for sub in range(ELEM_BLOCK // LANES):
+                element = element_ref[offset, block * (ELEM_BLOCK // LANES) + sub]
+                across = lateral - jnp.concatenate([element, element], axis=0)
+                square = depth_square + across * across
+                distance = square * lax.rsqrt(square)
+                for number, both in enumerate(waves(distance, centre_turns, half_step, freq_local)):
+                    for part_of, wave in enumerate(both):
+                        start = (number * 2 + part_of) * ELEM_BLOCK + sub * LANES
+                        green_ref[spot, start : start + LANES] = wave.astype(jnp.bfloat16)
+
+    def apply(step, green_ref):
+        offset = step // blocks
+        weights = held_ref[step].reshape(freq_local * 2 * ELEM_BLOCK, -1)
+        gain = jnp.dot(green_ref[...], weights, preferred_element_type=jnp.float32)
+        for half in range(gain.shape[1] // LANES):
+            total_ref[offset, half] = total_ref[offset, half] + gain[:, half * LANES : (half + 1) * LANES]
+
+    def run(make, into, use, out_of):
+        if use is not None:
+            if first:
+                fetch(use).wait()
+            apply(use, out_of)
+        if make is not None:
+            green(make, into)
+
+    run(0, green_even, None, None)
+
+    def two(pair, _):
+        run(2 * pair + 1, green_odd, 2 * pair, green_even)
+        run(2 * pair + 2, green_even, 2 * pair + 1, green_odd)
         return 0
 
-    lax.fori_loop(0, foot // 2, rows, 0)
-    gain = jnp.dot(
-        green_ref[...],
-        basis_ref[...].reshape(freq_local * 2 * ELEM_BLOCK, -1),
-        preferred_element_type=jnp.float32,
-    )
-
-    spans = [slice(start, start + LANES) for start in range(0, gain.shape[1], LANES)]
-
-    @pl.when(block == 0)
-    def _():
-        for half, span in enumerate(spans):
-            total_ref[half] = gain[:, span]
-
-    @pl.when(block > 0)
-    def _():
-        for half, span in enumerate(spans):
-            total_ref[half] = total_ref[half] + gain[:, span]
-
-    @pl.when(block == pl.num_programs(1) - 1)
-    def _():
+    lax.fori_loop(0, steps // 2 - 1, two, 0)
+    run(steps - 1, green_odd, steps - 2, green_even)
+    run(None, None, steps - 1, green_odd)
+
+    for offset in range(pos_local):
         for group in range(groups):
             for cell in range(per_dest):
-                for half, span in enumerate(spans):
-                    out_refs[group][cell, :, span] = total_ref[half, pl.ds(group * per_dest + cell, foot, stride=TW), :]
-
-
-def project(sizes, part, where, footprint, basis):
+                for half in range(total_ref.shape[1]):
+                    out_refs[group][cell, offset * foot : (offset + 1) * foot, half * LANES : (half + 1) * LANES] = (
+                        total_ref[offset, half, pl.ds(group * per_dest + cell, foot, stride=TW), :]
+                    )
+
+
+def project(sizes, part, first, where, footprint, basis, after):
     pos_count, freqs, positions, elements, pos_local, freq_local, foot = sizes
     groups = pos_count // TH
     per_dest = TW // groups
     rank = basis.shape[-1]
-    blocks = elements // ELEM_BLOCK
     rows = foot * TW
+    steps = pos_local * elements // ELEM_BLOCK
     flops = 2 * pos_local * rows * freq_local * 2 * elements * rank
+    green = pltpu.VMEM((rows, freq_local * 2 * ELEM_BLOCK), jnp.bfloat16)
+    out_shape = [jax.ShapeDtypeStruct((per_dest, pos_local * foot, rank), jnp.float32)] * groups
+    if first:
+        out_shape.append(jax.ShapeDtypeStruct((steps, freq_local, 2, ELEM_BLOCK, rank), jnp.bfloat16))
     return pl.pallas_call(
-        functools.partial(project_kernel, sizes, part),
-        grid=(pos_local, blocks),
+        functools.partial(project_kernel, sizes, part, first),
         in_specs=[
             pl.BlockSpec(memory_space=pltpu.SMEM),
             pl.BlockSpec(memory_space=pltpu.SMEM),
-            pl.BlockSpec((None, freq_local, 2, ELEM_BLOCK, rank), lambda p, e: (p, 0, 0, e, 0)),
+            pl.BlockSpec(memory_space=pl.ANY if first else pltpu.VMEM),
+            pl.BlockSpec(memory_space=pl.ANY),
         ],
-        out_specs=[pl.BlockSpec((per_dest, foot, rank), lambda p, e: (0, p, 0))] * groups,
-        out_shape=[jax.ShapeDtypeStruct((per_dest, pos_local * foot, rank), jnp.float32)] * groups,
+        out_specs=[pl.BlockSpec(memory_space=pltpu.VMEM)] * len(out_shape),
+        out_shape=out_shape,
         scratch_shapes=[
-            pltpu.VMEM((rows, freq_local * 2 * ELEM_BLOCK), jnp.bfloat16),
-            pltpu.VMEM((rank // LANES, rows, LANES), jnp.float32),
-        ],
+            green,
+            green,
+            pltpu.VMEM((pos_local, rank // LANES, rows, LANES), jnp.float32),
+            pltpu.VMEM((pos_local, foot, TW, LANES), jnp.float32),
+            pltpu.VMEM((pos_local, foot, TW, LANES), jnp.float32),
+            pltpu.VMEM((pos_local, elements // LANES, TW, LANES), jnp.float32),
+        ]
+        + ([pltpu.SemaphoreType.DMA((steps,))] if first else []),
         compiler_params=pltpu.CompilerParams(vmem_limit_bytes=VMEM_LIMIT),
         cost_estimate=pl.CostEstimate(flops=flops, bytes_accessed=basis.size * 2, transcendentals=0),
         name=f"project_{part}",
-    )(where, footprint, basis)
+    )(where, footprint, basis, after)
 
 
 def three_terms(values):
@@ -169,7 +211,7 @@
     return high, mid, (rest - mid.astype(jnp.float32)).astype(jnp.bfloat16)
 
 
-def gather_kernel(pos_count, freq_count, tile_rows, where_ref, ids_ref, *refs):
+def gather_kernel(pos_count, freq_count, tile_rows, where_ref, ids_ref, left_ref, right_ref, *refs):
     in_refs, out_refs = refs[:pos_count], refs[pos_count:]
     cells, entries, rank = in_refs[0].shape
     shard = out_refs[0].shape[1]
@@ -197,19 +239,21 @@
             out_refs[other][cell] = jnp.dot(hot[other], terms, preferred_element_type=jnp.float32)
 
 
-def gather_tiles(freq_count, where, ids, parts):
+def gather_tiles(freq_count, where, ids, left, right, parts):
     pos_count = len(parts)
     cells, entries, rank = parts[0].shape
     tile_rows = pos_count
     shard = (TILE_DEV // freq_count + 1) * tile_rows
     return pl.pallas_call(
         functools.partial(gather_kernel, pos_count, freq_count, tile_rows),
-        in_specs=[pl.BlockSpec(memory_space=pltpu.SMEM)] + [pl.BlockSpec(memory_space=pltpu.VMEM)] * (1 + pos_count),
+        in_specs=[pl.BlockSpec(memory_space=pltpu.SMEM), pl.BlockSpec(memory_space=pltpu.VMEM)]
+        + [pl.BlockSpec(memory_space=pl.ANY)] * 2
+        + [pl.BlockSpec(memory_space=pltpu.VMEM)] * pos_count,
         out_specs=[pl.BlockSpec(memory_space=pltpu.VMEM)] * freq_count,
         out_shape=[jax.ShapeDtypeStruct((cells, shard, rank), jnp.float32)] * freq_count,
         compiler_params=pltpu.CompilerParams(vmem_limit_bytes=VMEM_LIMIT),
         name="tiles",
-    )(where, ids, *parts)
+    )(where, ids, left, right, *parts)
 
 
 def energy_kernel(freq_count, weights_ref, rims_ref, left_ref, right_ref, *refs):
@@ -347,12 +391,15 @@
     split = basis.reshape(pos_local, freq_local, 2, elements, rank)
     groups = pos_count // TH
     parts = [None] * pos_count
+    held, after = split, footprint
     for part in range(TH - 1, -1, -1):
-        sent = project(sizes, part, where, footprint, split)
+        first = part == TH - 1
+        sent = list(project(sizes, part, first, where, footprint, held, after))
+        held, after = sent.pop() if first else held, sent[0]
         for group in range(groups):
             distance = part * groups + group
             parts[distance] = swap(sent[group], "pos", distance) if distance else sent[group]
-    tiles = gather_tiles(freq_count, where, ids, parts)
+    tiles = gather_tiles(freq_count, where, ids, left, right, parts)
     shards = [swap(tiles[d], "freq", d) if d else tiles[d] for d in range(freq_count)]
     strip = energies(weights.reshape(1, rank), rims, left, right, shards)
     strips = lax.all_gather(strip, "pos")

time: 126 us -> 121 us (0.960)
  Pallas kernels: 67.1 us -> 45.5 us
  waiting for transfers between devices: 32 us -> 44.5 us
  local copies, waits for them, and re-layouts: 0.86 us -> 4.25 us
    ppermute x10, waiting for transfers between devices: 11.9 us -> 43.7 us  [swap(): lax.ppermute(array, axis, [(i, i ^ distance) for i in range(lax.axis_size...]
    pallas_call x4, Pallas kernels: 61.6 us -> 39.9 us  [project(): pl.pallas_call(functools.partial(project_kernel, sizes, part, first), in_...]
    ppermute x1, waiting for transfers between devices: 20.1 us -> 0.01 us  [body(): lax.ppermute(rims[:, columns - TW:], 'freq', [(i, i + 1) for i in range(f...]
    unnamed x10 -> x12, local copies, waits for them, and re-layouts: 0.71 us -> 4.1 us
  transfers between devices with their start and end apart: 12 -> 12, of which waited for: 3 -> 5; matrix products, arithmetic and copies ran while one was open for 0% -> 0% of each run, Pallas kernels for 37% -> 8%
where the time goes in v2:
time: 121 us
  Pallas kernels  45.5 us (38%)
  waiting for transfers between devices  44.5 us (37%)
  starting transfers between devices  17 us (14%)
  blocking collectives  9.46 us (8%)
  local copies, waits for them, and re-layouts  4.25 us (4%)
    ppermute x10, waiting for transfers between devices, swap(): lax.ppermute(array, axis, [(i, i ^ distance) for i in range(lax.axis_size...  43.7 us
    pallas_call x4, Pallas kernels, project(): pl.pallas_call(functools.partial(project_kernel, sizes, part, first), in_...  39.9 us
    ppermute x10, starting transfers between devices, swap(): lax.ppermute(array, axis, [(i, i ^ distance) for i in range(lax.axis_size...  11.7 us
    all_gather x1, blocking collectives, body(): strips = lax.all_gather(strip, 'pos')  9.46 us
    unnamed x12, local copies, waits for them, and re-layouts  4.1 us
    ppermute x1, starting transfers between devices, body(): lax.ppermute(rims[:, columns - TW:], 'freq', [(i, i + 1) for i in range(f...  3.2 us
    pallas_call x1, Pallas kernels, gather_tiles(): pl.pallas_call(functools.partial(gather_kernel, pos_count, freq_count, ti...  2.82 us
  transfers between devices with their start and end apart: 12, of which 5 were waited for; matrix products, arithmetic and copies ran while one was open for 0% of the time, Pallas kernels for 8%

profile of v2, /device:TPU:17, one launch (start us, length us, event | category | flops | bytes accessed | tf_op | source)
XLA Modules:
  0.0 120.8 jit_solution(14027714153466034816)
XLA Ops:
  0.0 0.1 pad_add_fusion.where_ref
  0.1 0.0 copy-start
  0.1 3.4 %copy-done = bf16[2,4,2048,256]{3,2,1,0:T(8,128)(2,1)S(1)} copy-done((bf16[2,4,2048,256]{3,2,1,0:T(8,128)(2,1)S(1)}, bf16[2,4,2048,256]{3,2,1,0:T(8,128)(2,1)}, u32[]{:S(2)}) %copy-start) | copy-done | bytes 8388632
  3.5 0.0 copy-start.1
  3.5 0.7 copy-done.1
  4.2 11.9 %project_3.1 = (f32[4,64,256]{2,1,0:T(8,128)S(1)}, f32[4,64,256]{2,1,0:T(8,128)S(1)}, bf16[8,4,2,256,256]{4,3,2,1,0:T(8,128)(2,1)S(1)}) custom-call(s32[2]{0:T(128)S(1)} %pad_add_fusion.where_ref, s32[16,32]{1,0:T(8,128)S(1)} %copy-done.1, bf16[2,4,2,1024,256]{4,3,2,1,0:T(8,128)(2,1)S(1)} %bitcast.9, s32[16,32]{1,0:T(8,128)S(1)} %copy-done.1), custom_call_target="tpu_custom_call" | custom-call | flops 2147483648 | bytes 8388608 | tf_op jit(solution)/shard_map/project_3/pallas_call | solution.py:182
  16.1 9.3 %project_2.1 = (f32[4,64,256]{2,1,0:T(8,128)S(1)}, f32[4,64,256]{2,1,0:T(8,128)S(1)}) custom-call(s32[2]{0:T(128)S(1)} %pad_add_fusion.where_ref, s32[16,32]{1,0:T(8,128)S(1)} %copy-done.1, bf16[8,4,2,256,256]{4,3,2,1,0:T(8,128)(2,1)S(1)} %get-tuple-element.18.basis_ref, f32[4,64,256]{2,1,0:T(8,128)S(1)} %get-tuple-element.19.after_ref), custom_call_target="tpu_custom_call" | custom-call | flops 2147483648 | bytes 8388608 | tf_op jit(solution)/shard_map/project_2/pallas_call | solution.py:182
  25.3 0.0 copy-start.4
  25.4 0.0 copy-start.5
  25.4 0.0 copy-start.2
  25.4 0.0 copy-start.3
  25.4 9.5 %project_1.1 = (f32[4,64,256]{2,1,0:T(8,128)S(1)}, f32[4,64,256]{2,1,0:T(8,128)S(1)}) custom-call(s32[2]{0:T(128)S(1)} %pad_add_fusion.where_ref, s32[16,32]{1,0:T(8,128)S(1)} %copy-done.1, bf16[8,4,2,256,256]{4,3,2,1,0:T(8,128)(2,1)S(1)} %get-tuple-element.18.basis_ref, f32[4,64,256]{2,1,0:T(8,128)S(1)} %get-tuple-element.20.after_ref), custom_call_target="tpu_custom_call" | custom-call | flops 2147483648 | bytes 8388608 | tf_op jit(solution)/shard_map/project_1/pallas_call | solution.py:182
  34.9 1.3 %collective-permute-start.3 = (f32[4,64,256]{2,1,0:T(8,128)S(1)}, f32[4,64,256]{2,1,0:T(8,128)S(1)}, u32[]{:S(2)}, u32[]{:S(2)}) collective-permute-start(f32[4,64,256]{2,1,0:T(8,128)S(1)} %get-tuple-element.21.after_ref), channel_id=1, source_target_pairs={{0,8},{4,12},{8,0},{12,4},{16,24},{20,28},{24,16},{28,20},{1,9},{5... | collective-permute-start | bytes 786440 | tf_op jit(solution)/shard_map/ppermute | solution.py:367
  36.1 9.3 %project_0.1 = (f32[4,64,256]{2,1,0:T(8,128)S(1)}, f32[4,64,256]{2,1,0:T(8,128)S(1)}) custom-call(s32[2]{0:T(128)S(1)} %pad_add_fusion.where_ref, s32[16,32]{1,0:T(8,128)S(1)} %copy-done.1, bf16[8,4,2,256,256]{4,3,2,1,0:T(8,128)(2,1)S(1)} %get-tuple-element.18.basis_ref, f32[4,64,256]{2,1,0:T(8,128)S(1)} %get-tuple-element.21.after_ref), custom_call_target="tpu_custom_call" | custom-call | flops 2147483648 | bytes 8388608 | tf_op jit(solution)/shard_map/project_0/pallas_call | solution.py:182
  45.4 1.0 collective-permute-start.2
  46.4 0.0 copy-done.4
  46.4 0.0 copy-done.5
  46.5 0.1 fusion
  46.5 3.2 %collective-permute-start = (f32[12,8]{1,0:T(8,128)S(1)}, f32[12,8]{1,0:T(8,128)S(1)}, u32[]{:S(2)}, u32[]{:S(2)}) collective-permute-start(f32[12,8]{1,0:T(8,128)S(1)} %get-tuple-element.32), channel_id=1, source_target_pairs={{0,1},{1,2},{2,3},{4,5},{5,6},{6,7},{8,9},{9,10},{10,11},{12,13},{... | collective-permute-start | bytes 1160 | tf_op jit(solution)/shard_map/ppermute | solution.py:389
  49.7 2.1 %collective-permute-start.1 = (f32[12,8]{1,0:T(8,128)S(1)}, f32[12,8]{1,0:T(8,128)S(1)}, u32[]{:S(2)}, u32[]{:S(2)}) collective-permute-start(f32[12,8]{1,0:T(8,128)S(1)} %get-tuple-element.31), channel_id=1, source_target_pairs={{1,0},{2,1},{3,2},{5,4},{6,5},{7,6},{9,8},{10,9},{11,10},{13,12},{... | collective-permute-start | bytes 1160 | tf_op jit(solution)/shard_map/ppermute | solution.py:390
  51.8 1.3 %collective-permute-start.5 = (f32[4,64,256]{2,1,0:T(8,128)S(1)}, f32[4,64,256]{2,1,0:T(8,128)S(1)}, u32[]{:S(2)}, u32[]{:S(2)}) collective-permute-start(f32[4,64,256]{2,1,0:T(8,128)S(1)} %get-tuple-element.20.after_ref), channel_id=1, source_target_pairs={{0,16},{4,20},{8,24},{12,28},{16,0},{20,4},{24,8},{28,12},{1,17},{... | collective-permute-start | bytes 786440 | tf_op jit(solution)/shard_map/ppermute | solution.py:367
  53.1 0.0 collective-permute-done.left_ref
  53.1 0.2 collective-permute-start.7
  53.3 0.8 collective-permute-done.1.right_ref
  54.1 1.6 %collective-permute-start.4 = (f32[4,64,256]{2,1,0:T(8,128)S(1)}, f32[4,64,256]{2,1,0:T(8,128)S(1)}, u32[]{:S(2)}, u32[]{:S(2)}) collective-permute-start(f32[4,64,256]{2,1,0:T(8,128)S(1)} %get-tuple-element.24), channel_id=1, source_target_pairs={{0,12},{4,8},{8,4},{12,0},{16,28},{20,24},{24,20},{28,16},{1,13},{... | collective-permute-start | bytes 786440 | tf_op jit(solution)/shard_map/ppermute | solution.py:367
  55.7 0.0 collective-permute-done.2.refs_1_
  55.7 1.0 collective-permute-start.6
  56.7 0.0 collective-permute-done.3.refs_2_
  56.7 1.7 %collective-permute-start.8 = (f32[4,64,256]{2,1,0:T(8,128)S(1)}, f32[4,64,256]{2,1,0:T(8,128)S(1)}, u32[]{:S(2)}, u32[]{:S(2)}) collective-permute-start(f32[4,64,256]{2,1,0:T(8,128)S(1)} %get-tuple-element.26), channel_id=1, source_target_pairs={{0,28},{4,24},{8,20},{12,16},{16,12},{20,8},{24,4},{28,0},{1,29},{... | collective-permute-start | bytes 786440 | tf_op jit(solution)/shard_map/ppermute | solution.py:367
  58.4 0.0 copy-done.2
  58.4 0.1 reshape.10.ids_ref
  58.5 9.9 %collective-permute-done.4.refs_3_ = f32[4,64,256]{2,1,0:T(8,128)S(1)} collective-permute-done((f32[4,64,256]{2,1,0:T(8,128)S(1)}, f32[4,64,256]{2,1,0:T(8,128)S(1)}, u32[]{:S(2)}, u32[]{:S(2)}) %collective-permute-start.4) | collective-permute-done | bytes 262176 | tf_op jit(solution)/shard_map/ppermute | solution.py:367
  68.4 0.0 collective-permute-done.5.refs_4_
  68.4 8.4 %collective-permute-done.6.refs_5_ = f32[4,64,256]{2,1,0:T(8,128)S(1)} collective-permute-done((f32[4,64,256]{2,1,0:T(8,128)S(1)}, f32[4,64,256]{2,1,0:T(8,128)S(1)}, u32[]{:S(2)}, u32[]{:S(2)}) %collective-permute-start.6) | collective-permute-done | bytes 262176 | tf_op jit(solution)/shard_map/ppermute | solution.py:367
  76.8 0.0 collective-permute-done.7.refs_6_
  76.8 0.0 collective-permute-done.8.refs_7_
  76.8 2.8 %tiles.1 = (f32[4,72,256]{2,1,0:T(8,128)S(1)}, f32[4,72,256]{2,1,0:T(8,128)S(1)}, f32[4,72,256]{2,1,0:T(8,128)S(1)}, f32[4,72,256]{2,1,0:T(8,128)S(1)}) custom-call(s32[2]{0:T(128)S(1)} %pad_add_fusion.where_ref, s32[8,64]{1,0:T(8,128)S(1)} %reshape.10.ids_ref, f32[12,8]{1,0:T(8,128)S(1)} %collective-permute-done.left_ref, ...), custom_call_target="tpu_custom_call" | custom-call | tf_op jit(solution)/shard_map/tiles/pallas_call | solution.py:247
  79.6 0.1 collective-permute-start.10
  79.7 2.5 %collective-permute-start.11 = (f32[4,72,256]{2,1,0:T(8,128)S(1)}, f32[4,72,256]{2,1,0:T(8,128)S(1)}, u32[]{:S(2)}, u32[]{:S(2)}) collective-permute-start(f32[4,72,256]{2,1,0:T(8,128)S(1)} %get-tuple-element.30), channel_id=1, source_target_pairs={{0,3},{1,2},{2,1},{3,0},{4,7},{5,6},{6,5},{7,4},{8,11},{9,10},{10,... | collective-permute-start | bytes 884744 | tf_op jit(solution)/shard_map/ppermute | solution.py:367
  82.1 1.1 collective-permute-start.9
  83.2 16.0 %collective-permute-done.10.refs_2_ = f32[4,72,256]{2,1,0:T(8,128)S(1)} collective-permute-done((f32[4,72,256]{2,1,0:T(8,128)S(1)}, f32[4,72,256]{2,1,0:T(8,128)S(1)}, u32[]{:S(2)}, u32[]{:S(2)}) %collective-permute-start.10) | collective-permute-done | bytes 294944 | tf_op jit(solution)/shard_map/ppermute | solution.py:367
  99.2 9.4 %collective-permute-done.11.refs_3_ = f32[4,72,256]{2,1,0:T(8,128)S(1)} collective-permute-done((f32[4,72,256]{2,1,0:T(8,128)S(1)}, f32[4,72,256]{2,1,0:T(8,128)S(1)}, u32[]{:S(2)}, u32[]{:S(2)}) %collective-permute-start.11) | collective-permute-done | bytes 294944 | tf_op jit(solution)/shard_map/ppermute | solution.py:367
  108.6 0.0 collective-permute-done.9.refs_1_
  108.6 0.0 copy-done.3
  108.6 0.4 energies.1
  109.0 9.5 %all-gather = f32[128,128]{1,0:T(8,128)S(1)} all-gather(f32[16,128]{1,0:T(8,128)S(1)} %energies.1), channel_id=2, replica_groups=mesh['pos'=8,'freq'=4] {'pos'}, dimensions={0}, use_global_device_ids=true | all-gather | bytes 73728 | tf_op jit(solution)/shard_map/all_gather | solution.py:405
  118.4 2.4 %diffuse.1 = f32[4,64]{1,0:T(4,128)} custom-call(s32[2]{0:T(128)S(1)} %pad_add_fusion.where_ref, f32[8,16,128]{2,1,0:T(8,128)S(1)} %bitcast.10), custom_call_target="tpu_custom_call" | custom-call | tf_op jit(solution)/shard_map/diffuse/pallas_call | solution.py:355
  (2 shorter events, 0.0 us)
Async XLA Ops:
  0.1 3.4 %copy-start = (bf16[2,4,2048,256]{3,2,1,0:T(8,128)(2,1)S(1)}, bf16[2,4,2048,256]{3,2,1,0:T(8,128)(2,1)}, u32[]{:S(2)}) copy-start(bf16[2,4,2048,256]{3,2,1,0:T(8,128)(2,1)} %param.6) | copy-start | bytes 25165828
  3.5 0.7 copy-start.1
  25.3 21.1 %copy-start.4 = (f32[2,4,64]{2,1,0:T(4,128)S(1)}, f32[2,4,64]{2,1,0:T(4,128)}, u32[]{:S(2)}) copy-start(f32[2,4,64]{2,1,0:T(4,128)} %param.8) | copy-start | bytes 6148
  25.4 21.1 %copy-start.5 = (f32[4,64]{1,0:T(4,128)S(1)}, f32[4,64]{1,0:T(4,128)}, u32[]{:S(2)}) copy-start(f32[4,64]{1,0:T(4,128)} %param.9) | copy-start | bytes 3076
  25.4 33.1 %copy-start.2 = (s32[16,32]{1,0:T(8,128)S(1)}, s32[16,32]{1,0:T(8,128)}, u32[]{:S(2)}) copy-start(s32[16,32]{1,0:T(8,128)} %foot_ref.7) | copy-start | bytes 6148
  25.4 83.2 %copy-start.3 = (f32[256]{0:T(256)S(1)}, f32[256]{0:T(256)}, u32[]{:S(2)}) copy-start(f32[256]{0:T(256)} %param.7) | copy-start | bytes 3076
  34.9 21.9 %collective-permute-start.3 = (f32[4,64,256]{2,1,0:T(8,128)S(1)}, f32[4,64,256]{2,1,0:T(8,128)S(1)}, u32[]{:S(2)}, u32[]{:S(2)}) collective-permute-start(f32[4,64,256]{2,1,0:T(8,128)S(1)} %get-tuple-element.21.after_ref), channel_id=1, source_target_pairs={{0,8},{4,12},{8,0},{12,4},{16,24},{20,28},{24,16},{28,20},{1,9},{5... | collective-permute-start | bytes 786440 | tf_op jit(solution)/shard_map/ppermute | solution.py:367
  45.4 10.3 %collective-permute-start.2 = (f32[4,64,256]{2,1,0:T(8,128)S(1)}, f32[4,64,256]{2,1,0:T(8,128)S(1)}, u32[]{:S(2)}, u32[]{:S(2)}) collective-permute-start(f32[4,64,256]{2,1,0:T(8,128)S(1)} %get-tuple-element.23), channel_id=1, source_target_pairs={{0,4},{4,0},{8,12},{12,8},{16,20},{20,16},{24,28},{28,24},{1,5},{5... | collective-permute-start | bytes 786440 | tf_op jit(solution)/shard_map/ppermute | solution.py:367
  46.5 6.6 %collective-permute-start = (f32[12,8]{1,0:T(8,128)S(1)}, f32[12,8]{1,0:T(8,128)S(1)}, u32[]{:S(2)}, u32[]{:S(2)}) collective-permute-start(f32[12,8]{1,0:T(8,128)S(1)} %get-tuple-element.32), channel_id=1, source_target_pairs={{0,1},{1,2},{2,3},{4,5},{5,6},{6,7},{8,9},{9,10},{10,11},{12,13},{... | collective-permute-start | bytes 1160 | tf_op jit(solution)/shard_map/ppermute | solution.py:389
  49.7 4.4 %collective-permute-start.1 = (f32[12,8]{1,0:T(8,128)S(1)}, f32[12,8]{1,0:T(8,128)S(1)}, u32[]{:S(2)}, u32[]{:S(2)}) collective-permute-start(f32[12,8]{1,0:T(8,128)S(1)} %get-tuple-element.31), channel_id=1, source_target_pairs={{1,0},{2,1},{3,2},{5,4},{6,5},{7,6},{9,8},{10,9},{11,10},{13,12},{... | collective-permute-start | bytes 1160 | tf_op jit(solution)/shard_map/ppermute | solution.py:390
  51.8 16.6 %collective-permute-start.5 = (f32[4,64,256]{2,1,0:T(8,128)S(1)}, f32[4,64,256]{2,1,0:T(8,128)S(1)}, u32[]{:S(2)}, u32[]{:S(2)}) collective-permute-start(f32[4,64,256]{2,1,0:T(8,128)S(1)} %get-tuple-element.20.after_ref), channel_id=1, source_target_pairs={{0,16},{4,20},{8,24},{12,28},{16,0},{20,4},{24,8},{28,12},{1,17},{... | collective-permute-start | bytes 786440 | tf_op jit(solution)/shard_map/ppermute | solution.py:367
  53.1 23.6 %collective-permute-start.7 = (f32[4,64,256]{2,1,0:T(8,128)S(1)}, f32[4,64,256]{2,1,0:T(8,128)S(1)}, u32[]{:S(2)}, u32[]{:S(2)}) collective-permute-start(f32[4,64,256]{2,1,0:T(8,128)S(1)} %get-tuple-element.19.after_ref), channel_id=1, source_target_pairs={{0,24},{4,28},{8,16},{12,20},{16,8},{20,12},{24,0},{28,4},{1,25},{... | collective-permute-start | bytes 786440 | tf_op jit(solution)/shard_map/ppermute | solution.py:367
  54.1 14.3 %collective-permute-start.4 = (f32[4,64,256]{2,1,0:T(8,128)S(1)}, f32[4,64,256]{2,1,0:T(8,128)S(1)}, u32[]{:S(2)}, u32[]{:S(2)}) collective-permute-start(f32[4,64,256]{2,1,0:T(8,128)S(1)} %get-tuple-element.24), channel_id=1, source_target_pairs={{0,12},{4,8},{8,4},{12,0},{16,28},{20,24},{24,20},{28,16},{1,13},{... | collective-permute-start | bytes 786440 | tf_op jit(solution)/shard_map/ppermute | solution.py:367
  55.7 21.0 %collective-permute-start.6 = (f32[4,64,256]{2,1,0:T(8,128)S(1)}, f32[4,64,256]{2,1,0:T(8,128)S(1)}, u32[]{:S(2)}, u32[]{:S(2)}) collective-permute-start(f32[4,64,256]{2,1,0:T(8,128)S(1)} %get-tuple-element.25), channel_id=1, source_target_pairs={{0,20},{4,16},{8,28},{12,24},{16,4},{20,0},{24,12},{28,8},{1,21},{... | collective-permute-start | bytes 786440 | tf_op jit(solution)/shard_map/ppermute | solution.py:367
  56.7 20.0 %collective-permute-start.8 = (f32[4,64,256]{2,1,0:T(8,128)S(1)}, f32[4,64,256]{2,1,0:T(8,128)S(1)}, u32[]{:S(2)}, u32[]{:S(2)}) collective-permute-start(f32[4,64,256]{2,1,0:T(8,128)S(1)} %get-tuple-element.26), channel_id=1, source_target_pairs={{0,28},{4,24},{8,20},{12,16},{16,12},{20,8},{24,4},{28,0},{1,29},{... | collective-permute-start | bytes 786440 | tf_op jit(solution)/shard_map/ppermute | solution.py:367
  79.6 19.6 %collective-permute-start.10 = (f32[4,72,256]{2,1,0:T(8,128)S(1)}, f32[4,72,256]{2,1,0:T(8,128)S(1)}, u32[]{:S(2)}, u32[]{:S(2)}) collective-permute-start(f32[4,72,256]{2,1,0:T(8,128)S(1)} %get-tuple-element.29), channel_id=1, source_target_pairs={{0,2},{1,3},{2,0},{3,1},{4,6},{5,7},{6,4},{7,5},{8,10},{9,11},{10,... | collective-permute-start | bytes 884744 | tf_op jit(solution)/shard_map/ppermute | solution.py:367
  79.7 28.9 %collective-permute-start.11 = (f32[4,72,256]{2,1,0:T(8,128)S(1)}, f32[4,72,256]{2,1,0:T(8,128)S(1)}, u32[]{:S(2)}, u32[]{:S(2)}) collective-permute-start(f32[4,72,256]{2,1,0:T(8,128)S(1)} %get-tuple-element.30), channel_id=1, source_target_pairs={{0,3},{1,2},{2,1},{3,0},{4,7},{5,6},{6,5},{7,4},{8,11},{9,10},{10,... | collective-permute-start | bytes 884744 | tf_op jit(solution)/shard_map/ppermute | solution.py:367
  82.1 26.4 %collective-permute-start.9 = (f32[4,72,256]{2,1,0:T(8,128)S(1)}, f32[4,72,256]{2,1,0:T(8,128)S(1)}, u32[]{:S(2)}, u32[]{:S(2)}) collective-permute-start(f32[4,72,256]{2,1,0:T(8,128)S(1)} %get-tuple-element.28), channel_id=1, source_target_pairs={{0,1},{1,0},{2,3},{3,2},{4,5},{5,4},{6,7},{7,6},{8,9},{9,8},{10,11... | collective-permute-start | bytes 884744 | tf_op jit(solution)/shard_map/ppermute | solution.py:367

commit v3 on v2

--- a/solution.py
+++ b/solution.py
@@ -63,14 +63,14 @@
     return lows[::-1] + highs
 
 
-def project_kernel(sizes, part, first, where_ref, foot_ref, basis_ref, after_ref, *refs):
+def project_kernel(sizes, part, first, waits, where_ref, foot_ref, basis_ref, *refs):
     pos_count, freqs, positions, elements, pos_local, freq_local, foot = sizes
     groups = pos_count // TH
     per_dest = TW // groups
     blocks = elements // ELEM_BLOCK
     steps = pos_local * blocks
     rows = foot * TW
-    out_refs, refs = refs[:groups], refs[groups:]
+    out_refs, refs = refs[waits : waits + groups], refs[waits + groups :]
     if first:
         held_ref, refs, sems = refs[0], refs[1:-1], refs[-1]
     else:
@@ -180,13 +180,13 @@
     if first:
         out_shape.append(jax.ShapeDtypeStruct((steps, freq_local, 2, ELEM_BLOCK, rank), jnp.bfloat16))
     return pl.pallas_call(
-        functools.partial(project_kernel, sizes, part, first),
+        functools.partial(project_kernel, sizes, part, first, len(after)),
         in_specs=[
             pl.BlockSpec(memory_space=pltpu.SMEM),
             pl.BlockSpec(memory_space=pltpu.SMEM),
-            pl.BlockSpec(memory_space=pl.ANY if first else pltpu.VMEM),
-            pl.BlockSpec(memory_space=pl.ANY),
-        ],
+            pl.BlockSpec(memory_space=pltpu.HBM if first else pltpu.VMEM),
+        ]
+        + [pl.BlockSpec(memory_space=pl.ANY)] * len(after),
         out_specs=[pl.BlockSpec(memory_space=pltpu.VMEM)] * len(out_shape),
         out_shape=out_shape,
         scratch_shapes=[
@@ -199,9 +199,9 @@
         ]
         + ([pltpu.SemaphoreType.DMA((steps,))] if first else []),
         compiler_params=pltpu.CompilerParams(vmem_limit_bytes=VMEM_LIMIT),
-        cost_estimate=pl.CostEstimate(flops=flops, bytes_accessed=basis.size * 2, transcendentals=0),
+        cost_estimate=pl.CostEstimate(flops=flops, bytes_accessed=flops, transcendentals=0),
         name=f"project_{part}",
-    )(where, footprint, basis, after)
+    )(where, footprint, basis, *after)
 
 
 def three_terms(values):
@@ -211,7 +211,7 @@
     return high, mid, (rest - mid.astype(jnp.float32)).astype(jnp.bfloat16)
 
 
-def gather_kernel(pos_count, freq_count, tile_rows, where_ref, ids_ref, left_ref, right_ref, *refs):
+def gather_kernel(pos_count, freq_count, tile_rows, where_ref, ids_ref, *refs):
     in_refs, out_refs = refs[:pos_count], refs[pos_count:]
     cells, entries, rank = in_refs[0].shape
     shard = out_refs[0].shape[1]
@@ -239,7 +239,7 @@
             out_refs[other][cell] = jnp.dot(hot[other], terms, preferred_element_type=jnp.float32)
 
 
-def gather_tiles(freq_count, where, ids, left, right, parts):
+def gather_tiles(freq_count, where, ids, parts):
     pos_count = len(parts)
     cells, entries, rank = parts[0].shape
     tile_rows = pos_count
@@ -247,13 +247,12 @@
     return pl.pallas_call(
         functools.partial(gather_kernel, pos_count, freq_count, tile_rows),
         in_specs=[pl.BlockSpec(memory_space=pltpu.SMEM), pl.BlockSpec(memory_space=pltpu.VMEM)]
-        + [pl.BlockSpec(memory_space=pl.ANY)] * 2
         + [pl.BlockSpec(memory_space=pltpu.VMEM)] * pos_count,
         out_specs=[pl.BlockSpec(memory_space=pltpu.VMEM)] * freq_count,
         out_shape=[jax.ShapeDtypeStruct((cells, shard, rank), jnp.float32)] * freq_count,
         compiler_params=pltpu.CompilerParams(vmem_limit_bytes=VMEM_LIMIT),
         name="tiles",
-    )(where, ids, left, right, *parts)
+    )(where, ids, *parts)
 
 
 def energy_kernel(freq_count, weights_ref, rims_ref, left_ref, right_ref, *refs):
@@ -391,15 +390,20 @@
     split = basis.reshape(pos_local, freq_local, 2, elements, rank)
     groups = pos_count // TH
     parts = [None] * pos_count
-    held, after = split, footprint
+    held, after = split, ()
     for part in range(TH - 1, -1, -1):
         first = part == TH - 1
         sent = list(project(sizes, part, first, where, footprint, held, after))
-        held, after = sent.pop() if first else held, sent[0]
+        held = sent.pop() if first else held
         for group in range(groups):
             distance = part * groups + group
             parts[distance] = swap(sent[group], "pos", distance) if distance else sent[group]
-    tiles = gather_tiles(freq_count, where, ids, left, right, parts)
+        after = (sent[0],)
+        if first:
+            after += (left, right)
+        if part == 1:
+            after += tuple(parts[-groups:])
+    tiles = gather_tiles(freq_count, where, ids, parts)
     shards = [swap(tiles[d], "freq", d) if d else tiles[d] for d in range(freq_count)]
     strip = energies(weights.reshape(1, rank), rims, left, right, shards)
     strips = lax.all_gather(strip, "pos")

time: 121 us -> 105 us (0.87)
  waiting for transfers between devices: 44.5 us -> 26.8 us
    ppermute x10, waiting for transfers between devices: 43.7 us -> 26.8 us  [swap(): lax.ppermute(array, axis, [(i, i ^ distance) for i in range(lax.axis_size...]
    unnamed x12 -> x8, local copies, waits for them, and re-layouts: 4.1 us -> 4.09 us
  transfers between devices with their start and end apart: 12 -> 12, of which waited for: 5 -> 3; matrix products, arithmetic and copies ran while one was open for 0% -> 0% of each run, Pallas kernels for 8% -> 38%
where the time goes in v3:
time: 105 us; the launch traced here: 104 us
  Pallas kernels  45.5 us (43%)
  waiting for transfers between devices  26.8 us (26%)
  starting transfers between devices  16.6 us (16%)
  blocking collectives  9.51 us (9%)
  local copies, waits for them, and re-layouts  4.93 us (5%)
    pallas_call x4, Pallas kernels, project(): pl.pallas_call(functools.partial(project_kernel, sizes, part, first, len(...  39.9 us
    ppermute x10, waiting for transfers between devices, swap(): lax.ppermute(array, axis, [(i, i ^ distance) for i in range(lax.axis_size...  26.8 us
    ppermute x10, starting transfers between devices, swap(): lax.ppermute(array, axis, [(i, i ^ distance) for i in range(lax.axis_size...  11.3 us
    all_gather x1, blocking collectives, body(): strips = lax.all_gather(strip, 'pos')  9.51 us
    unnamed x8, local copies, waits for them, and re-layouts  4.09 us
    ppermute x1, starting transfers between devices, body(): lax.ppermute(rims[:, columns - TW:], 'freq', [(i, i + 1) for i in range(f...  3.19 us
    pallas_call x1, Pallas kernels, gather_tiles(): pl.pallas_call(functools.partial(gather_kernel, pos_count, freq_count, ti...  2.8 us
    pallas_call x1, Pallas kernels, diffuse(): pl.pallas_call(functools.partial(diffuse_kernel, cells, shard), in_specs=...  2.4 us
  transfers between devices with their start and end apart: 12, of which 3 were waited for; matrix products, arithmetic and copies ran while one was open for 0% of the time, Pallas kernels for 38%

profile of v3, /device:TPU:17, one launch (start us, length us, event | category | flops | bytes accessed | tf_op | source)
XLA Modules:
  0.0 104.2 jit_solution(3352843220234572232)
XLA Ops:
  0.0 0.7 slice_bitcast_fusion.1
  0.7 0.7 pad_maximum_fusion.rims_ref
  1.4 0.1 fusion
  1.5 3.2 %collective-permute-start = (f32[12,8]{1,0:T(8,128)S(1)}, f32[12,8]{1,0:T(8,128)S(1)}, u32[]{:S(2)}, u32[]{:S(2)}) collective-permute-start(f32[12,8]{1,0:T(8,128)S(1)} %get-tuple-element.32), channel_id=1, source_target_pairs={{0,1},{1,2},{2,3},{4,5},{5,6},{6,7},{8,9},{9,10},{10,11},{12,13},{... | collective-permute-start | bytes 1160 | tf_op jit(solution)/shard_map/ppermute | solution.py:388
  4.7 2.1 %collective-permute-start.1 = (f32[12,8]{1,0:T(8,128)S(1)}, f32[12,8]{1,0:T(8,128)S(1)}, u32[]{:S(2)}, u32[]{:S(2)}) collective-permute-start(f32[12,8]{1,0:T(8,128)S(1)} %get-tuple-element.31), channel_id=1, source_target_pairs={{1,0},{2,1},{3,2},{5,4},{6,5},{7,6},{9,8},{10,9},{11,10},{13,12},{... | collective-permute-start | bytes 1160 | tf_op jit(solution)/shard_map/ppermute | solution.py:389
  6.8 0.1 pad_add_fusion.where_ref
  6.8 0.0 copy-start
  6.8 3.4 %copy-done = bf16[2,4,2048,256]{3,2,1,0:T(8,128)(2,1)S(1)} copy-done((bf16[2,4,2048,256]{3,2,1,0:T(8,128)(2,1)S(1)}, bf16[2,4,2048,256]{3,2,1,0:T(8,128)(2,1)}, u32[]{:S(2)}) %copy-start) | copy-done | bytes 8388632
  10.2 0.0 copy-start.1
  10.2 0.7 copy-done.1
  10.9 11.9 %project_3.1 = (f32[4,64,256]{2,1,0:T(8,128)S(1)}, f32[4,64,256]{2,1,0:T(8,128)S(1)}, bf16[8,4,2,256,256]{4,3,2,1,0:T(8,128)(2,1)S(1)}) custom-call(s32[2]{0:T(128)S(1)} %pad_add_fusion.where_ref, s32[16,32]{1,0:T(8,128)S(1)} %copy-done.1, bf16[2,4,2,1024,256]{4,3,2,1,0:T(8,128)(2,1)S(1)} %bitcast.9), custom_call_target="tpu_custom_call" | custom-call | flops 2147483648 | bytes 2147483648 | tf_op jit(solution)/shard_map/project_3/pallas_call | solution.py:182
  22.8 2.2 %collective-permute-start.2 = (f32[4,64,256]{2,1,0:T(8,128)S(1)}, f32[4,64,256]{2,1,0:T(8,128)S(1)}, u32[]{:S(2)}, u32[]{:S(2)}) collective-permute-start(f32[4,64,256]{2,1,0:T(8,128)S(1)} %get-tuple-element.19.refs_0_), channel_id=1, source_target_pairs={{0,24},{4,28},{8,16},{12,20},{16,8},{20,12},{24,0},{28,4},{1,25},{... | collective-permute-start | bytes 786440 | tf_op jit(solution)/shard_map/ppermute | solution.py:366
  25.0 1.6 %collective-permute-start.3 = (f32[4,64,256]{2,1,0:T(8,128)S(1)}, f32[4,64,256]{2,1,0:T(8,128)S(1)}, u32[]{:S(2)}, u32[]{:S(2)}) collective-permute-start(f32[4,64,256]{2,1,0:T(8,128)S(1)} %get-tuple-element.22), channel_id=1, source_target_pairs={{0,28},{4,24},{8,20},{12,16},{16,12},{20,8},{24,4},{28,0},{1,29},{... | collective-permute-start | bytes 786440 | tf_op jit(solution)/shard_map/ppermute | solution.py:366
  26.6 0.0 collective-permute-done.refs_1_.left_ref
  26.6 0.0 collective-permute-done.1.refs_2_.right_ref
  26.7 9.3 %project_2.1 = (f32[4,64,256]{2,1,0:T(8,128)S(1)}, f32[4,64,256]{2,1,0:T(8,128)S(1)}) custom-call(s32[2]{0:T(128)S(1)} %pad_add_fusion.where_ref, s32[16,32]{1,0:T(8,128)S(1)} %copy-done.1, bf16[8,4,2,256,256]{4,3,2,1,0:T(8,128)(2,1)S(1)} %get-tuple-element.18.basis_ref, f32[4,64,256]{2,1,0:T(8,128)S(1)} %get-tuple-element.19.refs_0_, ...), custom_call_target="tpu_custom_call" | custom-call | flops 2147483648 | bytes 2147483648 | tf_op jit(solution)/shard_map/project_2/pallas_call | solution.py:182
  35.9 0.0 copy-start.2
  35.9 0.0 copy-start.3
  36.0 1.3 %collective-permute-start.7 = (f32[4,64,256]{2,1,0:T(8,128)S(1)}, f32[4,64,256]{2,1,0:T(8,128)S(1)}, u32[]{:S(2)}, u32[]{:S(2)}) collective-permute-start(f32[4,64,256]{2,1,0:T(8,128)S(1)} %get-tuple-element.20.refs_0_), channel_id=1, source_target_pairs={{0,16},{4,20},{8,24},{12,28},{16,0},{20,4},{24,8},{28,12},{1,17},{... | collective-permute-start | bytes 786440 | tf_op jit(solution)/shard_map/ppermute | solution.py:366
  37.3 9.5 %project_1.1 = (f32[4,64,256]{2,1,0:T(8,128)S(1)}, f32[4,64,256]{2,1,0:T(8,128)S(1)}) custom-call(s32[2]{0:T(128)S(1)} %pad_add_fusion.where_ref, s32[16,32]{1,0:T(8,128)S(1)} %copy-done.1, bf16[8,4,2,256,256]{4,3,2,1,0:T(8,128)(2,1)S(1)} %get-tuple-element.18.basis_ref, f32[4,64,256]{2,1,0:T(8,128)S(1)} %get-tuple-element.20.refs_0_), custom_call_target="tpu_custom_call" | custom-call | flops 2147483648 | bytes 2147483648 | tf_op jit(solution)/shard_map/project_1/pallas_call | solution.py:182
  46.7 1.3 %collective-permute-start.5 = (f32[4,64,256]{2,1,0:T(8,128)S(1)}, f32[4,64,256]{2,1,0:T(8,128)S(1)}, u32[]{:S(2)}, u32[]{:S(2)}) collective-permute-start(f32[4,64,256]{2,1,0:T(8,128)S(1)} %get-tuple-element.21.refs_0_), channel_id=1, source_target_pairs={{0,8},{4,12},{8,0},{12,4},{16,24},{20,28},{24,16},{28,20},{1,9},{5... | collective-permute-start | bytes 786440 | tf_op jit(solution)/shard_map/ppermute | solution.py:366
  48.0 0.0 collective-permute-start.6
  48.0 0.0 collective-permute-done.2.refs_1_.refs_6_
  48.0 0.8 collective-permute-start.8
  48.8 0.0 collective-permute-done.3.refs_2_.refs_7_
  48.8 9.3 %project_0.1 = (f32[4,64,256]{2,1,0:T(8,128)S(1)}, f32[4,64,256]{2,1,0:T(8,128)S(1)}) custom-call(s32[2]{0:T(128)S(1)} %pad_add_fusion.where_ref, s32[16,32]{1,0:T(8,128)S(1)} %copy-done.1, bf16[8,4,2,256,256]{4,3,2,1,0:T(8,128)(2,1)S(1)} %get-tuple-element.18.basis_ref, f32[4,64,256]{2,1,0:T(8,128)S(1)} %get-tuple-element.21.refs_0_, ...), custom_call_target="tpu_custom_call" | custom-call | flops 2147483648 | bytes 2147483648 | tf_op jit(solution)/shard_map/project_0/pallas_call | solution.py:182
  58.1 0.5 collective-permute-start.4
  58.6 0.0 copy-done.2
  58.6 0.1 reshape.10.ids_ref
  58.7 0.0 collective-permute-done.5.refs_2_
  58.7 1.5 %collective-permute-done.6.refs_3_ = f32[4,64,256]{2,1,0:T(8,128)S(1)} collective-permute-done((f32[4,64,256]{2,1,0:T(8,128)S(1)}, f32[4,64,256]{2,1,0:T(8,128)S(1)}, u32[]{:S(2)}, u32[]{:S(2)}) %collective-permute-start.6) | collective-permute-done | bytes 262176 | tf_op jit(solution)/shard_map/ppermute | solution.py:366
  60.2 0.0 collective-permute-done.7.refs_4_
  60.2 0.0 collective-permute-done.8.refs_5_
  60.2 0.0 collective-permute-done.4.refs_1_
  60.2 2.8 %tiles.1 = (f32[4,72,256]{2,1,0:T(8,128)S(1)}, f32[4,72,256]{2,1,0:T(8,128)S(1)}, f32[4,72,256]{2,1,0:T(8,128)S(1)}, f32[4,72,256]{2,1,0:T(8,128)S(1)}) custom-call(s32[2]{0:T(128)S(1)} %pad_add_fusion.where_ref, s32[8,64]{1,0:T(8,128)S(1)} %reshape.10.ids_ref, f32[4,64,256]{2,1,0:T(8,128)S(1)} %get-tuple-element.23.refs_0_, ...), custom_call_target="tpu_custom_call" | custom-call | tf_op jit(solution)/shard_map/tiles/pallas_call | solution.py:247
  63.0 0.1 collective-permute-start.10
  63.1 2.5 %collective-permute-start.11 = (f32[4,72,256]{2,1,0:T(8,128)S(1)}, f32[4,72,256]{2,1,0:T(8,128)S(1)}, u32[]{:S(2)}, u32[]{:S(2)}) collective-permute-start(f32[4,72,256]{2,1,0:T(8,128)S(1)} %get-tuple-element.30), channel_id=1, source_target_pairs={{0,3},{1,2},{2,1},{3,0},{4,7},{5,6},{6,5},{7,4},{8,11},{9,10},{10,... | collective-permute-start | bytes 884744 | tf_op jit(solution)/shard_map/ppermute | solution.py:366
  65.6 1.1 %collective-permute-start.9 = (f32[4,72,256]{2,1,0:T(8,128)S(1)}, f32[4,72,256]{2,1,0:T(8,128)S(1)}, u32[]{:S(2)}, u32[]{:S(2)}) collective-permute-start(f32[4,72,256]{2,1,0:T(8,128)S(1)} %get-tuple-element.28), channel_id=1, source_target_pairs={{0,1},{1,0},{2,3},{3,2},{4,5},{5,4},{6,7},{7,6},{8,9},{9,8},{10,11... | collective-permute-start | bytes 884744 | tf_op jit(solution)/shard_map/ppermute | solution.py:366
  66.6 15.1 %collective-permute-done.10.refs_2_ = f32[4,72,256]{2,1,0:T(8,128)S(1)} collective-permute-done((f32[4,72,256]{2,1,0:T(8,128)S(1)}, f32[4,72,256]{2,1,0:T(8,128)S(1)}, u32[]{:S(2)}, u32[]{:S(2)}) %collective-permute-start.10) | collective-permute-done | bytes 294944 | tf_op jit(solution)/shard_map/ppermute | solution.py:366
  81.8 10.1 %collective-permute-done.11.refs_3_ = f32[4,72,256]{2,1,0:T(8,128)S(1)} collective-permute-done((f32[4,72,256]{2,1,0:T(8,128)S(1)}, f32[4,72,256]{2,1,0:T(8,128)S(1)}, u32[]{:S(2)}, u32[]{:S(2)}) %collective-permute-start.11) | collective-permute-done | bytes 294944 | tf_op jit(solution)/shard_map/ppermute | solution.py:366
  91.9 0.0 collective-permute-done.9.refs_1_
  91.9 0.0 copy-done.3
  91.9 0.4 energies.1
  92.3 9.5 %all-gather = f32[128,128]{1,0:T(8,128)S(1)} all-gather(f32[16,128]{1,0:T(8,128)S(1)} %energies.1), channel_id=2, replica_groups=mesh['pos'=8,'freq'=4] {'pos'}, dimensions={0}, use_global_device_ids=true | all-gather | bytes 73728 | tf_op jit(solution)/shard_map/all_gather | solution.py:409
  101.8 2.4 %diffuse.1 = f32[4,64]{1,0:T(4,128)} custom-call(s32[2]{0:T(128)S(1)} %pad_add_fusion.where_ref, f32[8,16,128]{2,1,0:T(8,128)S(1)} %bitcast.10), custom_call_target="tpu_custom_call" | custom-call | tf_op jit(solution)/shard_map/diffuse/pallas_call | solution.py:354
Async XLA Ops:
  1.5 25.2 %collective-permute-start = (f32[12,8]{1,0:T(8,128)S(1)}, f32[12,8]{1,0:T(8,128)S(1)}, u32[]{:S(2)}, u32[]{:S(2)}) collective-permute-start(f32[12,8]{1,0:T(8,128)S(1)} %get-tuple-element.32), channel_id=1, source_target_pairs={{0,1},{1,2},{2,3},{4,5},{5,6},{6,7},{8,9},{9,10},{10,11},{12,13},{... | collective-permute-start | bytes 1160 | tf_op jit(solution)/shard_map/ppermute | solution.py:388
  4.7 22.0 %collective-permute-start.1 = (f32[12,8]{1,0:T(8,128)S(1)}, f32[12,8]{1,0:T(8,128)S(1)}, u32[]{:S(2)}, u32[]{:S(2)}) collective-permute-start(f32[12,8]{1,0:T(8,128)S(1)} %get-tuple-element.31), channel_id=1, source_target_pairs={{1,0},{2,1},{3,2},{5,4},{6,5},{7,6},{9,8},{10,9},{11,10},{13,12},{... | collective-permute-start | bytes 1160 | tf_op jit(solution)/shard_map/ppermute | solution.py:389
  6.8 3.4 %copy-start = (bf16[2,4,2048,256]{3,2,1,0:T(8,128)(2,1)S(1)}, bf16[2,4,2048,256]{3,2,1,0:T(8,128)(2,1)}, u32[]{:S(2)}) copy-start(bf16[2,4,2048,256]{3,2,1,0:T(8,128)(2,1)} %param.6) | copy-start | bytes 25165828
  10.2 0.7 copy-start.1
  22.8 25.2 %collective-permute-start.2 = (f32[4,64,256]{2,1,0:T(8,128)S(1)}, f32[4,64,256]{2,1,0:T(8,128)S(1)}, u32[]{:S(2)}, u32[]{:S(2)}) collective-permute-start(f32[4,64,256]{2,1,0:T(8,128)S(1)} %get-tuple-element.19.refs_0_), channel_id=1, source_target_pairs={{0,24},{4,28},{8,16},{12,20},{16,8},{20,12},{24,0},{28,4},{1,25},{... | collective-permute-start | bytes 786440 | tf_op jit(solution)/shard_map/ppermute | solution.py:366
  25.0 23.7 %collective-permute-start.3 = (f32[4,64,256]{2,1,0:T(8,128)S(1)}, f32[4,64,256]{2,1,0:T(8,128)S(1)}, u32[]{:S(2)}, u32[]{:S(2)}) collective-permute-start(f32[4,64,256]{2,1,0:T(8,128)S(1)} %get-tuple-element.22), channel_id=1, source_target_pairs={{0,28},{4,24},{8,20},{12,16},{16,12},{20,8},{24,4},{28,0},{1,29},{... | collective-permute-start | bytes 786440 | tf_op jit(solution)/shard_map/ppermute | solution.py:366
  35.9 22.7 %copy-start.2 = (s32[16,32]{1,0:T(8,128)S(1)}, s32[16,32]{1,0:T(8,128)}, u32[]{:S(2)}) copy-start(s32[16,32]{1,0:T(8,128)} %foot_ref.7) | copy-start | bytes 6148
  35.9 56.0 %copy-start.3 = (f32[256]{0:T(256)S(1)}, f32[256]{0:T(256)}, u32[]{:S(2)}) copy-start(f32[256]{0:T(256)} %param.7) | copy-start | bytes 3076
  36.0 24.2 %collective-permute-start.7 = (f32[4,64,256]{2,1,0:T(8,128)S(1)}, f32[4,64,256]{2,1,0:T(8,128)S(1)}, u32[]{:S(2)}, u32[]{:S(2)}) collective-permute-start(f32[4,64,256]{2,1,0:T(8,128)S(1)} %get-tuple-element.20.refs_0_), channel_id=1, source_target_pairs={{0,16},{4,20},{8,24},{12,28},{16,0},{20,4},{24,8},{28,12},{1,17},{... | collective-permute-start | bytes 786440 | tf_op jit(solution)/shard_map/ppermute | solution.py:366
  46.7 12.0 %collective-permute-start.5 = (f32[4,64,256]{2,1,0:T(8,128)S(1)}, f32[4,64,256]{2,1,0:T(8,128)S(1)}, u32[]{:S(2)}, u32[]{:S(2)}) collective-permute-start(f32[4,64,256]{2,1,0:T(8,128)S(1)} %get-tuple-element.21.refs_0_), channel_id=1, source_target_pairs={{0,8},{4,12},{8,0},{12,4},{16,24},{20,28},{24,16},{28,20},{1,9},{5... | collective-permute-start | bytes 786440 | tf_op jit(solution)/shard_map/ppermute | solution.py:366
  48.0 12.2 %collective-permute-start.6 = (f32[4,64,256]{2,1,0:T(8,128)S(1)}, f32[4,64,256]{2,1,0:T(8,128)S(1)}, u32[]{:S(2)}, u32[]{:S(2)}) collective-permute-start(f32[4,64,256]{2,1,0:T(8,128)S(1)} %get-tuple-element.25), channel_id=1, source_target_pairs={{0,12},{4,8},{8,4},{12,0},{16,28},{20,24},{24,20},{28,16},{1,13},{... | collective-permute-start | bytes 786440 | tf_op jit(solution)/shard_map/ppermute | solution.py:366
  48.0 12.2 %collective-permute-start.8 = (f32[4,64,256]{2,1,0:T(8,128)S(1)}, f32[4,64,256]{2,1,0:T(8,128)S(1)}, u32[]{:S(2)}, u32[]{:S(2)}) collective-permute-start(f32[4,64,256]{2,1,0:T(8,128)S(1)} %get-tuple-element.26), channel_id=1, source_target_pairs={{0,20},{4,16},{8,28},{12,24},{16,4},{20,0},{24,12},{28,8},{1,21},{... | collective-permute-start | bytes 786440 | tf_op jit(solution)/shard_map/ppermute | solution.py:366
  58.1 2.2 %collective-permute-start.4 = (f32[4,64,256]{2,1,0:T(8,128)S(1)}, f32[4,64,256]{2,1,0:T(8,128)S(1)}, u32[]{:S(2)}, u32[]{:S(2)}) collective-permute-start(f32[4,64,256]{2,1,0:T(8,128)S(1)} %get-tuple-element.24), channel_id=1, source_target_pairs={{0,4},{4,0},{8,12},{12,8},{16,20},{20,16},{24,28},{28,24},{1,5},{5... | collective-permute-start | bytes 786440 | tf_op jit(solution)/shard_map/ppermute | solution.py:366
  63.0 18.8 %collective-permute-start.10 = (f32[4,72,256]{2,1,0:T(8,128)S(1)}, f32[4,72,256]{2,1,0:T(8,128)S(1)}, u32[]{:S(2)}, u32[]{:S(2)}) collective-permute-start(f32[4,72,256]{2,1,0:T(8,128)S(1)} %get-tuple-element.29), channel_id=1, source_target_pairs={{0,2},{1,3},{2,0},{3,1},{4,6},{5,7},{6,4},{7,5},{8,10},{9,11},{10,... | collective-permute-start | bytes 884744 | tf_op jit(solution)/shard_map/ppermute | solution.py:366
  63.1 28.8 %collective-permute-start.11 = (f32[4,72,256]{2,1,0:T(8,128)S(1)}, f32[4,72,256]{2,1,0:T(8,128)S(1)}, u32[]{:S(2)}, u32[]{:S(2)}) collective-permute-start(f32[4,72,256]{2,1,0:T(8,128)S(1)} %get-tuple-element.30), channel_id=1, source_target_pairs={{0,3},{1,2},{2,1},{3,0},{4,7},{5,6},{6,5},{7,4},{8,11},{9,10},{10,... | collective-permute-start | bytes 884744 | tf_op jit(solution)/shard_map/ppermute | solution.py:366
  65.6 26.4 %collective-permute-start.9 = (f32[4,72,256]{2,1,0:T(8,128)S(1)}, f32[4,72,256]{2,1,0:T(8,128)S(1)}, u32[]{:S(2)}, u32[]{:S(2)}) collective-permute-start(f32[4,72,256]{2,1,0:T(8,128)S(1)} %get-tuple-element.28), channel_id=1, source_target_pairs={{0,1},{1,0},{2,3},{3,2},{4,5},{5,4},{6,7},{7,6},{8,9},{9,8},{10,11... | collective-permute-start | bytes 884744 | tf_op jit(solution)/shard_map/ppermute | solution.py:366

commit v4 on v3

--- a/solution.py
+++ b/solution.py
@@ -22,13 +22,13 @@
 eps_value = 1e-06
 
 SIN_PI = tuple(
-    math.sqrt(2.0) * term
-    for term in (3.1415927410125732, -5.167710304260254, 2.550077438354492, -0.598291277885437, 0.07765766233205795)
+    math.sqrt(2.0) * (1.0 - 2e-6) * term
+    for term in (3.1415903568267822, -5.1674065589904785, 2.5440104007720947, -0.5594624280929565)
 )
-TINY = 1e-12
 
 HIGHEST = lax.Precision.HIGHEST
 VMEM_LIMIT = 24 * 1024 * 1024
+VMEM_LIMIT_FIRST = 42 * 1024 * 1024
 
 
 def half_turn(turns):
@@ -38,44 +38,41 @@
     for term in SIN_PI[-2::-1]:
         s = s * square + term
     s = s * x
-    rest = jnp.maximum(2.0 - s * s, TINY)
+    rest = 2.0 - s * s
     return rest * lax.rsqrt(rest), s, rest - 1.0
 
 
-def waves(distance, centre_turns, half_step, count):
-    c, s, cosine = half_turn(centre_turns * distance)
-    amplitude = lax.rsqrt(distance * (1.0 / top_depth))
-    mid_c = amplitude * cosine
-    mid_s = (amplitude * c) * s
-    c, s, step_c = half_turn(half_step * distance)
-    step_s = c * s
-    cc, ss, cs, sc = mid_c * step_c, mid_s * step_s, mid_c * step_s, mid_s * step_c
-    low, high = (cc + ss, sc - cs), (cc - ss, sc + cs)
-    lows, highs = [low], [high]
-    twice = step_c + step_c
-    factor = twice * twice - 2.0
-    before_low, before_high = high, low
-    for _ in range(count // 2 - 1):
-        low, before_low = tuple(factor * a - b for a, b in zip(low, before_low)), low
-        high, before_high = tuple(factor * a - b for a, b in zip(high, before_high)), high
-        lows.append(low)
-        highs.append(high)
-    return lows[::-1] + highs
-
-
-def project_kernel(sizes, part, first, waits, where_ref, foot_ref, basis_ref, *refs):
+def waves(distance, first_turns, step_turns, count):
+    c, s, cosine = half_turn(first_turns * distance)
+    amplitude = lax.rsqrt(distance)
+    last = amplitude * cosine, (amplitude * c) * s
+    c, s, cosine = half_turn(step_turns * distance)
+    sine = c * s
+    now = last[0] * cosine - last[1] * sine, last[1] * cosine + last[0] * sine
+    found = [last, now]
+    twice = cosine + cosine
+    for _ in range(count - 2):
+        now, last = tuple(twice * a - b for a, b in zip(now, last)), now
+        found.append(now)
+    return found[:count]
+
+
+def project_kernel(sizes, part, first, waits, *refs):
     pos_count, freqs, positions, elements, pos_local, freq_local, foot = sizes
     groups = pos_count // TH
     per_dest = TW // groups
     blocks = elements // ELEM_BLOCK
     steps = pos_local * blocks
-    rows = foot * TW
-    out_refs, refs = refs[waits : waits + groups], refs[waits + groups :]
+    where_ref, refs = refs[0], refs[1:]
     if first:
-        held_ref, refs, sems = refs[0], refs[1:-1], refs[-1]
+        (foot_ref, basis_ref, conduct_ref, baseline_ref), refs = refs[:4], refs[4:]
+        out_refs, refs = refs[:groups], refs[groups:]
+        held_ref, depth_ref, lateral_ref, element_ref, rims_ref, head_ref, tail_ref = refs[:7]
+        green_even, green_odd, total_ref, sems = refs[7:]
     else:
-        held_ref = basis_ref
-    green_even, green_odd, total_ref, depth_ref, lateral_ref, element_ref = refs
+        held_ref, depth_ref, lateral_ref, element_ref = refs[:4]
+        out_refs, refs = refs[4 + waits : 4 + waits + groups], refs[4 + waits + groups :]
+        green_even, green_odd, total_ref = refs
     my_pos, my_freq = where_ref[0], where_ref[1]
 
     def fetch(step):
@@ -87,39 +84,47 @@
         for step in range(steps):
             fetch(step).start()
 
-    cell_row = (my_pos // groups) ^ part
-    my_group = lax.rem(my_pos, groups)
     first_freq = (my_freq * freq_local).astype(jnp.float32)
-    centre_turns = 0.5 + (first_freq + 0.5 * (freq_local - 1)) / freqs
-    half_step = 0.5 / freqs
-
-    row = lax.broadcasted_iota(jnp.int32, (TW, LANES), 0)
-    lane = lax.broadcasted_iota(jnp.int32, (TW, LANES), 1)
-    cell_col = ((row // per_dest) ^ my_group) * per_dest + row % per_dest
-    for offset in range(pos_local):
-        pos_global = my_pos * pos_local + offset
-        centre = pos_global.astype(jnp.float32) * (cell_spacing * TW * TILE_DEV / positions)
-        for piece in range(elements // LANES):
-            index = (piece * LANES + lane).astype(jnp.float32)
-            element_ref[offset, piece] = (index - 0.5 * (elements - 1)) * elem_pitch + centre
-
-        def place(entry, _, offset=offset, pos_global=pos_global):
-            tile = foot_ref[pos_global, entry]
-            grid_row = (tile // TILE_DEV) * TH + cell_row
-            grid_col = ((tile % TILE_DEV) * TW + cell_col).astype(jnp.float32)
-            depth = top_depth + cell_spacing * jnp.full((TW, LANES), grid_row, jnp.int32).astype(jnp.float32)
-            depth_ref[offset, entry] = depth * depth
-            lateral_ref[offset, entry] = cell_spacing * grid_col
-            return 0
-
-        lax.fori_loop(0, foot, place, 0, unroll=4)
+    first_turns = top_depth * (0.5 + first_freq / freqs)
+    step_turns = top_depth / freqs
+
+    if first:
+        scale = 1.0 / top_depth
+        my_group = lax.rem(my_pos, groups)
+        row = lax.broadcasted_iota(jnp.int32, (TW, LANES), 0)
+        lane = lax.broadcasted_iota(jnp.int32, (TW, LANES), 1)
+        cell_col = ((row // per_dest) ^ my_group) * per_dest + row % per_dest
+        for offset in range(pos_local):
+            pos_global = my_pos * pos_local + offset
+            centre = pos_global.astype(jnp.float32) * (cell_spacing * TW * TILE_DEV / positions)
+            for piece in range(elements // LANES):
+                index = (piece * LANES + lane).astype(jnp.float32)
+                element_ref[offset, piece] = scale * ((index - 0.5 * (elements - 1)) * elem_pitch + centre)
+
+            def place(entry, _, offset=offset, pos_global=pos_global):
+                tile = foot_ref[pos_global, entry]
+                for other in range(TH):
+                    grid_row = (tile // TILE_DEV) * TH + ((my_pos // groups) ^ other)
+                    depth = scale * (top_depth + cell_spacing * jnp.full((TW, LANES), grid_row, jnp.int32).astype(jnp.float32))
+                    depth_ref[other, offset, entry] = depth * depth
+                grid_col = ((tile % TILE_DEV) * TW + cell_col).astype(jnp.float32)
+                lateral_ref[offset, entry] = scale * (cell_spacing * grid_col)
+                return 0
+
+            lax.fori_loop(0, foot, place, 0, unroll=8)
+        columns = rims_ref.shape[1]
+        for number, block in enumerate((conduct_ref[0], conduct_ref[1], baseline_ref[...])):
+            span = slice(number * TH, (number + 1) * TH)
+            rims_ref[span, :] = block
+            head_ref[span, :] = block[:, :TW]
+            tail_ref[span, :] = block[:, columns - TW :]
     total_ref[...] = jnp.zeros_like(total_ref)
 
     def green(step, green_ref):
         offset, block = step // blocks, step % blocks
         for pair in range(foot // 2):
             entry = 2 * pair
-            depth_square = depth_ref[offset, pl.ds(entry, 2)].reshape(2 * TW, LANES)
+            depth_square = depth_ref[part, offset, pl.ds(entry, 2)].reshape(2 * TW, LANES)
             lateral = lateral_ref[offset, pl.ds(entry, 2)].reshape(2 * TW, LANES)
             spot = pl.ds(entry * TW, 2 * TW)
             for sub in range(ELEM_BLOCK // LANES):
@@ -127,7 +132,7 @@
                 across = lateral - jnp.concatenate([element, element], axis=0)
                 square = depth_square + across * across
                 distance = square * lax.rsqrt(square)
-                for number, both in enumerate(waves(distance, centre_turns, half_step, freq_local)):
+                for number, both in enumerate(waves(distance, first_turns, step_turns, freq_local)):
                     for part_of, wave in enumerate(both):
                         start = (number * 2 + part_of) * ELEM_BLOCK + sub * LANES
                         green_ref[spot, start : start + LANES] = wave.astype(jnp.bfloat16)
@@ -167,48 +172,52 @@
                     )
 
 
-def project(sizes, part, first, where, footprint, basis, after):
+def project(sizes, part, first, operands, after):
     pos_count, freqs, positions, elements, pos_local, freq_local, foot = sizes
     groups = pos_count // TH
     per_dest = TW // groups
+    basis = operands[2] if first else operands[1]
     rank = basis.shape[-1]
     rows = foot * TW
     steps = pos_local * elements // ELEM_BLOCK
     flops = 2 * pos_local * rows * freq_local * 2 * elements * rank
+
+    def shape(*dims, dtype=jnp.float32):
+        return jax.ShapeDtypeStruct(dims, dtype)
+
+    vmem, smem = pl.BlockSpec(memory_space=pltpu.VMEM), pl.BlockSpec(memory_space=pltpu.SMEM)
+    out_shape = [shape(per_dest, pos_local * foot, rank)] * groups
+    if first:
+        in_specs = [smem, smem, pl.BlockSpec(memory_space=pl.ANY), vmem, vmem]
+        columns = operands[4].shape[1]
+        out_shape += [
+            shape(steps, freq_local, 2, ELEM_BLOCK, rank, dtype=jnp.bfloat16),
+            shape(TH, pos_local, foot, TW, LANES),
+            shape(pos_local, foot, TW, LANES),
+            shape(pos_local, elements // LANES, TW, LANES),
+            shape(3 * TH, columns),
+            shape(3 * TH, TW),
+            shape(3 * TH, TW),
+        ]
+    else:
+        in_specs = [smem] + [vmem] * 4 + [pl.BlockSpec(memory_space=pl.ANY)] * len(after)
     green = pltpu.VMEM((rows, freq_local * 2 * ELEM_BLOCK), jnp.bfloat16)
-    out_shape = [jax.ShapeDtypeStruct((per_dest, pos_local * foot, rank), jnp.float32)] * groups
-    if first:
-        out_shape.append(jax.ShapeDtypeStruct((steps, freq_local, 2, ELEM_BLOCK, rank), jnp.bfloat16))
     return pl.pallas_call(
         functools.partial(project_kernel, sizes, part, first, len(after)),
-        in_specs=[
-            pl.BlockSpec(memory_space=pltpu.SMEM),
-            pl.BlockSpec(memory_space=pltpu.SMEM),
-            pl.BlockSpec(memory_space=pltpu.HBM if first else pltpu.VMEM),
-        ]
-        + [pl.BlockSpec(memory_space=pl.ANY)] * len(after),
-        out_specs=[pl.BlockSpec(memory_space=pltpu.VMEM)] * len(out_shape),
+        in_specs=in_specs,
+        out_specs=[vmem] * len(out_shape),
         out_shape=out_shape,
-        scratch_shapes=[
-            green,
-            green,
-            pltpu.VMEM((pos_local, rank // LANES, rows, LANES), jnp.float32),
-            pltpu.VMEM((pos_local, foot, TW, LANES), jnp.float32),
-            pltpu.VMEM((pos_local, foot, TW, LANES), jnp.float32),
-            pltpu.VMEM((pos_local, elements // LANES, TW, LANES), jnp.float32),
-        ]
+        scratch_shapes=[green, green, pltpu.VMEM((pos_local, rank // LANES, rows, LANES), jnp.float32)]
         + ([pltpu.SemaphoreType.DMA((steps,))] if first else []),
-        compiler_params=pltpu.CompilerParams(vmem_limit_bytes=VMEM_LIMIT),
+        compiler_params=pltpu.CompilerParams(vmem_limit_bytes=VMEM_LIMIT_FIRST if first else VMEM_LIMIT),
         cost_estimate=pl.CostEstimate(flops=flops, bytes_accessed=flops, transcendentals=0),
         name=f"project_{part}",
-    )(where, footprint, basis, *after)
-
-
-def three_terms(values):
+    )(*operands, *after)
+
+
+def two_terms(values):
     high = values.astype(jnp.bfloat16)
-    rest = values - high.astype(jnp.float32)
-    mid = rest.astype(jnp.bfloat16)
-    return high, mid, (rest - mid.astype(jnp.float32)).astype(jnp.bfloat16)
+    return high, (values - high.astype(jnp.float32)).astype(jnp.bfloat16)
 
 
 def gather_kernel(pos_count, freq_count, tile_rows, where_ref, ids_ref, *refs):
@@ -231,10 +240,10 @@
             hit = (wanted + base == ids) & (col >= 0) & (col < TILE_DEV)
             hot_row.append(hit.astype(jnp.float32).astype(jnp.bfloat16))
         hot_row = jnp.concatenate(hot_row, axis=1)
-        hot.append(jnp.concatenate([hot_row] * 3, axis=1))
+        hot.append(jnp.concatenate([hot_row] * 2, axis=1))
     for cell in range(cells):
         values = jnp.concatenate([ref[cell] for ref in in_refs], axis=0)
-        terms = jnp.concatenate(three_terms(values), axis=0)
+        terms = jnp.concatenate(two_terms(values), axis=0)
         for other in range(freq_count):
             out_refs[other][cell] = jnp.dot(hot[other], terms, preferred_element_type=jnp.float32)
 
@@ -302,25 +311,26 @@
     here = (spot % tile_rows == tile_row) & (spot < shard)
     source = lax.broadcasted_iota(jnp.int32, (width, LANES), 0)
     target = lax.broadcasted_iota(jnp.int32, (width, LANES), 1)
-    field = [jnp.zeros((tile_rows, LANES), jnp.float32) for _ in range(TH)]
+    field = jnp.zeros((TH * tile_rows, LANES), jnp.float32)
     for group in range(groups):
         left = 1 if group * 2 >= groups else 0
         for cell in range(cells):
             col = (source // tile_rows - left) * TW + group * cells + cell
             place = ((target == (col + LANES) % LANES) & (source < shard)).astype(jnp.float32)
+            spread = []
             for row in range(TH):
                 line = strips_ref[row * groups + group, pl.ds(cell, 1), :]
-                spread = jnp.where(here, jnp.broadcast_to(line, (tile_rows, width)), 0.0)
-                field[row] = field[row] + jnp.dot(
-                    spread, place, precision=HIGHEST, preferred_element_type=jnp.float32
-                )
+                spread.append(jnp.where(here, jnp.broadcast_to(line, (tile_rows, width)), 0.0))
+            field = field + jnp.dot(
+                jnp.concatenate(spread, axis=0), place, precision=HIGHEST, preferred_element_type=jnp.float32
+            )
 
     def strip(which, row):
         return strips_ref[:, cells + which * TH + row, 0:LANES]
 
     across_k = [strip(0, row) for row in range(TH)]
     along_k = [strip(1, row) for row in range(TH)]
-    field = [field[row] + strip(2, row) for row in range(TH)]
+    field = [field[row * tile_rows : (row + 1) * tile_rows] + strip(2, row) for row in range(TH)]
 
     def above(rows, row):
         if row:
@@ -384,22 +394,23 @@
     )
     where = jnp.stack([lax.axis_index("pos"), lax.axis_index("freq")]).astype(jnp.int32)
     ids = footprint.reshape(pos_count, pos_local * foot)
-    rims = jnp.concatenate([conduct[0], conduct[1], baseline], axis=0)
-    left = lax.ppermute(rims[:, columns - TW :], "freq", [(i, i + 1) for i in range(freq_count - 1)])
-    right = lax.ppermute(rims[:, :TW], "freq", [(i + 1, i) for i in range(freq_count - 1)])
     split = basis.reshape(pos_local, freq_local, 2, elements, rank)
     groups = pos_count // TH
     parts = [None] * pos_count
-    held, after = split, ()
+    operands, after = (where, footprint, split, conduct, baseline), ()
     for part in range(TH - 1, -1, -1):
         first = part == TH - 1
-        sent = list(project(sizes, part, first, where, footprint, held, after))
-        held = sent.pop() if first else held
+        sent = project(sizes, part, first, operands, after)
         for group in range(groups):
             distance = part * groups + group
             parts[distance] = swap(sent[group], "pos", distance) if distance else sent[group]
         after = (sent[0],)
         if first:
+            held, depth, lateral, element, rims, head, tail = sent[groups:]
+            operands = where, held, depth, lateral, element
+            left = lax.ppermute(tail, "freq", [(i, i + 1) for i in range(freq_count - 1)])
+            right = lax.ppermute(head, "freq", [(i + 1, i) for i in range(freq_count - 1)])
+        if part == 2:
             after += (left, right)
         if part == 1:
             after += tuple(parts[-groups:])

time: 105 us -> 96 us (0.914)
  Pallas kernels: 45.5 us -> 38.7 us
  local copies, waits for them, and re-layouts: 4.93 us -> 2.14 us
  waiting for transfers between devices: 26.8 us -> 29.2 us
    pallas_call x4, Pallas kernels: 39.9 us -> 34.4 us  [project(): pl.pallas_call(functools.partial(project_kernel, sizes, part, first, len(...]
    ppermute x10, waiting for transfers between devices: 26.8 us -> 29.2 us  [swap(): lax.ppermute(array, axis, [(i, i ^ distance) for i in range(lax.axis_size...]
    unnamed x8 -> x10, local copies, waits for them, and re-layouts: 4.09 us -> 2.07 us
  transfers between devices with their start and end apart: 12 -> 12, of which waited for: 3 -> 3; matrix products, arithmetic and copies ran while one was open for 0% -> 0% of each run, Pallas kernels for 38% -> 24%
where the time goes in v4:
time: 96 us; the launch traced here: 95.7 us
  Pallas kernels  38.7 us (40%)
  waiting for transfers between devices  29.2 us (30%)
  starting transfers between devices  16.4 us (17%)
  blocking collectives  9.15 us (10%)
  local copies, waits for them, and re-layouts  2.14 us (2%)
    pallas_call x4, Pallas kernels, project(): pl.pallas_call(functools.partial(project_kernel, sizes, part, first, len(...  34.4 us
    ppermute x10, waiting for transfers between devices, swap(): lax.ppermute(array, axis, [(i, i ^ distance) for i in range(lax.axis_size...  29.2 us
    ppermute x10, starting transfers between devices, swap(): lax.ppermute(array, axis, [(i, i ^ distance) for i in range(lax.axis_size...  11.1 us
    all_gather x1, blocking collectives, body(): strips = lax.all_gather(strip, 'pos')  9.15 us
    ppermute x1, starting transfers between devices, body(): lax.ppermute(tail, 'freq', [(i, i + 1) for i in range(freq_count - 1)])  3.21 us
    pallas_call x1, Pallas kernels, gather_tiles(): pl.pallas_call(functools.partial(gather_kernel, pos_count, freq_count, ti...  2.12 us
    ppermute x1, starting transfers between devices, body(): lax.ppermute(head, 'freq', [(i + 1, i) for i in range(freq_count - 1)])  2.08 us
    unnamed x10, local copies, waits for them, and re-layouts  2.07 us
  transfers between devices with their start and end apart: 12, of which 3 were waited for; matrix products, arithmetic and copies ran while one was open for 0% of the time, Pallas kernels for 24%

profile of v4, /device:TPU:17, one launch (start us, length us, event | category | flops | bytes accessed | tf_op | source)
XLA Modules:
  0.0 95.7 jit_solution(2552244142382656252)
XLA Ops:
  0.0 0.1 pad_add_fusion.refs_0_.where_ref
  0.1 0.0 copy-start
  0.1 0.7 copy-done
  0.8 0.0 copy-start.2
  0.8 0.7 copy-done.2
  1.5 0.0 copy-start.3
  1.5 0.7 copy-done.3
  2.1 11.0 %project_3.1 = (f32[4,64,256]{2,1,0:T(8,128)S(1)}, f32[4,64,256]{2,1,0:T(8,128)S(1)}, bf16[8,4,2,256,256]{4,3,2,1,0:T(8,128)(2,1)S(1)}, f32[4,2,32,8,128]{4,3,2,...) custom-call(s32[2]{0:T(128)S(1)} %pad_add_fusion.refs_0_.where_ref, ...), custom_call_target="tpu_custom_call" | custom-call | flops 2147483648 | bytes 2147483648 | tf_op jit(solution)/shard_map/project_3/pallas_call | solution.py:205
  13.2 3.2 %collective-permute-start = (f32[12,8]{1,0:T(8,128)S(1)}, f32[12,8]{1,0:T(8,128)S(1)}, u32[]{:S(2)}, u32[]{:S(2)}) collective-permute-start(f32[12,8]{1,0:T(8,128)S(1)} %get-tuple-element.25), channel_id=1, source_target_pairs={{0,1},{1,2},{2,3},{4,5},{5,6},{6,7},{8,9},{9,10},{10,11},{12,13},{... | collective-permute-start | bytes 1160 | tf_op jit(solution)/shard_map/ppermute | solution.py:411
  16.4 2.1 %collective-permute-start.1 = (f32[12,8]{1,0:T(8,128)S(1)}, f32[12,8]{1,0:T(8,128)S(1)}, u32[]{:S(2)}, u32[]{:S(2)}) collective-permute-start(f32[12,8]{1,0:T(8,128)S(1)} %get-tuple-element.26), channel_id=1, source_target_pairs={{1,0},{2,1},{3,2},{5,4},{6,5},{7,6},{9,8},{10,9},{11,10},{13,12},{... | collective-permute-start | bytes 1160 | tf_op jit(solution)/shard_map/ppermute | solution.py:412
  18.5 2.2 %collective-permute-start.2 = (f32[4,64,256]{2,1,0:T(8,128)S(1)}, f32[4,64,256]{2,1,0:T(8,128)S(1)}, u32[]{:S(2)}, u32[]{:S(2)}) collective-permute-start(f32[4,64,256]{2,1,0:T(8,128)S(1)} %get-tuple-element.31.refs_5_), channel_id=1, source_target_pairs={{0,24},{4,28},{8,16},{12,20},{16,8},{20,12},{24,0},{28,4},{1,25},{... | collective-permute-start | bytes 786440 | tf_op jit(solution)/shard_map/ppermute | solution.py:376
  20.7 1.6 %collective-permute-start.3 = (f32[4,64,256]{2,1,0:T(8,128)S(1)}, f32[4,64,256]{2,1,0:T(8,128)S(1)}, u32[]{:S(2)}, u32[]{:S(2)}) collective-permute-start(f32[4,64,256]{2,1,0:T(8,128)S(1)} %get-tuple-element.34), channel_id=1, source_target_pairs={{0,28},{4,24},{8,20},{12,16},{16,12},{20,8},{24,4},{28,0},{1,29},{... | collective-permute-start | bytes 786440 | tf_op jit(solution)/shard_map/ppermute | solution.py:376
  22.3 7.9 %project_2.1 = (f32[4,64,256]{2,1,0:T(8,128)S(1)}, f32[4,64,256]{2,1,0:T(8,128)S(1)}) custom-call(s32[2]{0:T(128)S(1)} %pad_add_fusion.refs_0_.where_ref, bf16[8,4,2,256,256]{4,3,2,1,0:T(8,128)(2,1)S(1)} %get-tuple-element.27.refs_1_, f32[4,2,32,8,128]{4,3,2,1,0:T(8,128)S(1)} %get-tuple-element.28.refs_2_, f32[2,32,8,128]{3,2,1,0:T(8,128)S(1)} %get-tuple-element.29.refs_3_, ...), custom_call_target="tpu_custom_call" | custom-call | flops 2147483648 | bytes 2147483648 | tf_op jit(solution)/shard_map/project_2/pallas_call | solution.py:205
  30.2 1.3 %collective-permute-start.7 = (f32[4,64,256]{2,1,0:T(8,128)S(1)}, f32[4,64,256]{2,1,0:T(8,128)S(1)}, u32[]{:S(2)}, u32[]{:S(2)}) collective-permute-start(f32[4,64,256]{2,1,0:T(8,128)S(1)} %get-tuple-element.32.refs_5_), channel_id=1, source_target_pairs={{0,16},{4,20},{8,24},{12,28},{16,0},{20,4},{24,8},{28,12},{1,17},{... | collective-permute-start | bytes 786440 | tf_op jit(solution)/shard_map/ppermute | solution.py:376
  31.5 0.0 collective-permute-done.refs_6_.left_ref
  31.5 0.0 copy-start.1
  31.5 0.3 collective-permute-start.8
  31.8 0.0 collective-permute-done.1.refs_7_.right_ref
  31.8 7.7 %project_1.1 = (f32[4,64,256]{2,1,0:T(8,128)S(1)}, f32[4,64,256]{2,1,0:T(8,128)S(1)}) custom-call(s32[2]{0:T(128)S(1)} %pad_add_fusion.refs_0_.where_ref, bf16[8,4,2,256,256]{4,3,2,1,0:T(8,128)(2,1)S(1)} %get-tuple-element.27.refs_1_, f32[4,2,32,8,128]{4,3,2,1,0:T(8,128)S(1)} %get-tuple-element.28.refs_2_, f32[2,32,8,128]{3,2,1,0:T(8,128)S(1)} %get-tuple-element.29.refs_3_, ...), custom_call_target="tpu_custom_call" | custom-call | flops 2147483648 | bytes 2147483648 | tf_op jit(solution)/shard_map/project_1/pallas_call | solution.py:205
  39.6 0.0 copy-start.4
  39.6 1.0 %collective-permute-start.5 = (f32[4,64,256]{2,1,0:T(8,128)S(1)}, f32[4,64,256]{2,1,0:T(8,128)S(1)}, u32[]{:S(2)}, u32[]{:S(2)}) collective-permute-start(f32[4,64,256]{2,1,0:T(8,128)S(1)} %get-tuple-element.33.refs_5_), channel_id=1, source_target_pairs={{0,8},{4,12},{8,0},{12,4},{16,24},{20,28},{24,16},{28,20},{1,9},{5... | collective-permute-start | bytes 786440 | tf_op jit(solution)/shard_map/ppermute | solution.py:376
  40.6 0.0 collective-permute-done.2.refs_6_
  40.6 1.0 %collective-permute-start.6 = (f32[4,64,256]{2,1,0:T(8,128)S(1)}, f32[4,64,256]{2,1,0:T(8,128)S(1)}, u32[]{:S(2)}, u32[]{:S(2)}) collective-permute-start(f32[4,64,256]{2,1,0:T(8,128)S(1)} %get-tuple-element.37), channel_id=1, source_target_pairs={{0,12},{4,8},{8,4},{12,0},{16,28},{20,24},{24,20},{28,16},{1,13},{... | collective-permute-start | bytes 786440 | tf_op jit(solution)/shard_map/ppermute | solution.py:376
  41.6 0.0 collective-permute-done.3.refs_7_
  41.6 7.7 %project_0.1 = (f32[4,64,256]{2,1,0:T(8,128)S(1)}, f32[4,64,256]{2,1,0:T(8,128)S(1)}) custom-call(s32[2]{0:T(128)S(1)} %pad_add_fusion.refs_0_.where_ref, bf16[8,4,2,256,256]{4,3,2,1,0:T(8,128)(2,1)S(1)} %get-tuple-element.27.refs_1_, f32[4,2,32,8,128]{4,3,2,1,0:T(8,128)S(1)} %get-tuple-element.28.refs_2_, f32[2,32,8,128]{3,2,1,0:T(8,128)S(1)} %get-tuple-element.29.refs_3_, ...), custom_call_target="tpu_custom_call" | custom-call | flops 2147483648 | bytes 2147483648 | tf_op jit(solution)/shard_map/project_0/pallas_call | solution.py:205
  49.3 0.1 collective-permute-start.4
  49.4 0.0 copy-done.1
  49.4 0.1 reshape.11.ids_ref
  49.5 0.0 collective-permute-done.7.refs_4_
  49.5 0.0 collective-permute-done.8.refs_5_
  49.5 0.0 collective-permute-done.5.refs_2_
  49.5 3.8 %collective-permute-done.6.refs_3_ = f32[4,64,256]{2,1,0:T(8,128)S(1)} collective-permute-done((f32[4,64,256]{2,1,0:T(8,128)S(1)}, f32[4,64,256]{2,1,0:T(8,128)S(1)}, u32[]{:S(2)}, u32[]{:S(2)}) %collective-permute-start.6) | collective-permute-done | bytes 262176 | tf_op jit(solution)/shard_map/ppermute | solution.py:376
  53.3 0.0 collective-permute-done.4.refs_1_
  53.3 2.1 %tiles.1 = (f32[4,72,256]{2,1,0:T(8,128)S(1)}, f32[4,72,256]{2,1,0:T(8,128)S(1)}, f32[4,72,256]{2,1,0:T(8,128)S(1)}, f32[4,72,256]{2,1,0:T(8,128)S(1)}) custom-call(s32[2]{0:T(128)S(1)} %pad_add_fusion.refs_0_.where_ref, s32[8,64]{1,0:T(8,128)S(1)} %reshape.11.ids_ref, f32[4,64,256]{2,1,0:T(8,128)S(1)} %get-tuple-element.35.refs_0_, ...), custom_call_target="tpu_custom_call" | custom-call | tf_op jit(solution)/shard_map/tiles/pallas_call | solution.py:256
  55.4 0.1 collective-permute-start.10
  55.5 2.5 %collective-permute-start.11 = (f32[4,72,256]{2,1,0:T(8,128)S(1)}, f32[4,72,256]{2,1,0:T(8,128)S(1)}, u32[]{:S(2)}, u32[]{:S(2)}) collective-permute-start(f32[4,72,256]{2,1,0:T(8,128)S(1)} %get-tuple-element.42), channel_id=1, source_target_pairs={{0,3},{1,2},{2,1},{3,0},{4,7},{5,6},{6,5},{7,4},{8,11},{9,10},{10,... | collective-permute-start | bytes 884744 | tf_op jit(solution)/shard_map/ppermute | solution.py:376
  58.0 1.1 %collective-permute-start.9 = (f32[4,72,256]{2,1,0:T(8,128)S(1)}, f32[4,72,256]{2,1,0:T(8,128)S(1)}, u32[]{:S(2)}, u32[]{:S(2)}) collective-permute-start(f32[4,72,256]{2,1,0:T(8,128)S(1)} %get-tuple-element.40), channel_id=1, source_target_pairs={{0,1},{1,0},{2,3},{3,2},{4,5},{5,4},{6,7},{7,6},{8,9},{9,8},{10,11... | collective-permute-start | bytes 884744 | tf_op jit(solution)/shard_map/ppermute | solution.py:376
  59.0 15.8 %collective-permute-done.10.refs_2_ = f32[4,72,256]{2,1,0:T(8,128)S(1)} collective-permute-done((f32[4,72,256]{2,1,0:T(8,128)S(1)}, f32[4,72,256]{2,1,0:T(8,128)S(1)}, u32[]{:S(2)}, u32[]{:S(2)}) %collective-permute-start.10) | collective-permute-done | bytes 294944 | tf_op jit(solution)/shard_map/ppermute | solution.py:376
  74.9 9.5 %collective-permute-done.11.refs_3_ = f32[4,72,256]{2,1,0:T(8,128)S(1)} collective-permute-done((f32[4,72,256]{2,1,0:T(8,128)S(1)}, f32[4,72,256]{2,1,0:T(8,128)S(1)}, u32[]{:S(2)}, u32[]{:S(2)}) %collective-permute-start.11) | collective-permute-done | bytes 294944 | tf_op jit(solution)/shard_map/ppermute | solution.py:376
  84.4 0.0 collective-permute-done.9.refs_1_
  84.4 0.0 copy-done.4
  84.4 0.4 energies.1
  84.8 9.2 %all-gather = f32[128,128]{1,0:T(8,128)S(1)} all-gather(f32[16,128]{1,0:T(8,128)S(1)} %energies.1), channel_id=2, replica_groups=mesh['pos'=8,'freq'=4] {'pos'}, dimensions={0}, use_global_device_ids=true | all-gather | bytes 73728 | tf_op jit(solution)/shard_map/all_gather | solution.py:420
  93.9 1.8 %diffuse.1 = f32[4,64]{1,0:T(4,128)} custom-call(s32[2]{0:T(128)S(1)} %pad_add_fusion.refs_0_.where_ref, f32[8,16,128]{2,1,0:T(8,128)S(1)} %bitcast.5), custom_call_target="tpu_custom_call" | custom-call | tf_op jit(solution)/shard_map/diffuse/pallas_call | solution.py:364
Async XLA Ops:
  0.1 0.7 copy-start
  0.8 0.7 copy-start.2
  1.5 0.7 copy-start.3
  13.2 18.4 %collective-permute-start = (f32[12,8]{1,0:T(8,128)S(1)}, f32[12,8]{1,0:T(8,128)S(1)}, u32[]{:S(2)}, u32[]{:S(2)}) collective-permute-start(f32[12,8]{1,0:T(8,128)S(1)} %get-tuple-element.25), channel_id=1, source_target_pairs={{0,1},{1,2},{2,3},{4,5},{5,6},{6,7},{8,9},{9,10},{10,11},{12,13},{... | collective-permute-start | bytes 1160 | tf_op jit(solution)/shard_map/ppermute | solution.py:411
  16.4 15.5 %collective-permute-start.1 = (f32[12,8]{1,0:T(8,128)S(1)}, f32[12,8]{1,0:T(8,128)S(1)}, u32[]{:S(2)}, u32[]{:S(2)}) collective-permute-start(f32[12,8]{1,0:T(8,128)S(1)} %get-tuple-element.26), channel_id=1, source_target_pairs={{1,0},{2,1},{3,2},{5,4},{6,5},{7,6},{9,8},{10,9},{11,10},{13,12},{... | collective-permute-start | bytes 1160 | tf_op jit(solution)/shard_map/ppermute | solution.py:412
  18.5 22.1 %collective-permute-start.2 = (f32[4,64,256]{2,1,0:T(8,128)S(1)}, f32[4,64,256]{2,1,0:T(8,128)S(1)}, u32[]{:S(2)}, u32[]{:S(2)}) collective-permute-start(f32[4,64,256]{2,1,0:T(8,128)S(1)} %get-tuple-element.31.refs_5_), channel_id=1, source_target_pairs={{0,24},{4,28},{8,16},{12,20},{16,8},{20,12},{24,0},{28,4},{1,25},{... | collective-permute-start | bytes 786440 | tf_op jit(solution)/shard_map/ppermute | solution.py:376
  20.7 20.9 %collective-permute-start.3 = (f32[4,64,256]{2,1,0:T(8,128)S(1)}, f32[4,64,256]{2,1,0:T(8,128)S(1)}, u32[]{:S(2)}, u32[]{:S(2)}) collective-permute-start(f32[4,64,256]{2,1,0:T(8,128)S(1)} %get-tuple-element.34), channel_id=1, source_target_pairs={{0,28},{4,24},{8,20},{12,16},{16,12},{20,8},{24,4},{28,0},{1,29},{... | collective-permute-start | bytes 786440 | tf_op jit(solution)/shard_map/ppermute | solution.py:376
  30.2 19.3 %collective-permute-start.7 = (f32[4,64,256]{2,1,0:T(8,128)S(1)}, f32[4,64,256]{2,1,0:T(8,128)S(1)}, u32[]{:S(2)}, u32[]{:S(2)}) collective-permute-start(f32[4,64,256]{2,1,0:T(8,128)S(1)} %get-tuple-element.32.refs_5_), channel_id=1, source_target_pairs={{0,16},{4,20},{8,24},{12,28},{16,0},{20,4},{24,8},{28,12},{1,17},{... | collective-permute-start | bytes 786440 | tf_op jit(solution)/shard_map/ppermute | solution.py:376
  31.5 17.9 %copy-start.1 = (s32[16,32]{1,0:T(8,128)S(1)}, s32[16,32]{1,0:T(8,128)}, u32[]{:S(2)}) copy-start(s32[16,32]{1,0:T(8,128)} %refs_1_.1) | copy-start | bytes 6148
  31.5 18.0 %collective-permute-start.8 = (f32[4,64,256]{2,1,0:T(8,128)S(1)}, f32[4,64,256]{2,1,0:T(8,128)S(1)}, u32[]{:S(2)}, u32[]{:S(2)}) collective-permute-start(f32[4,64,256]{2,1,0:T(8,128)S(1)} %get-tuple-element.38), channel_id=1, source_target_pairs={{0,20},{4,16},{8,28},{12,24},{16,4},{20,0},{24,12},{28,8},{1,21},{... | collective-permute-start | bytes 786440 | tf_op jit(solution)/shard_map/ppermute | solution.py:376
  39.6 44.8 %copy-start.4 = (f32[256]{0:T(256)S(1)}, f32[256]{0:T(256)}, u32[]{:S(2)}) copy-start(f32[256]{0:T(256)} %param.7) | copy-start | bytes 3076
  39.6 9.9 %collective-permute-start.5 = (f32[4,64,256]{2,1,0:T(8,128)S(1)}, f32[4,64,256]{2,1,0:T(8,128)S(1)}, u32[]{:S(2)}, u32[]{:S(2)}) collective-permute-start(f32[4,64,256]{2,1,0:T(8,128)S(1)} %get-tuple-element.33.refs_5_), channel_id=1, source_target_pairs={{0,8},{4,12},{8,0},{12,4},{16,24},{20,28},{24,16},{28,20},{1,9},{5... | collective-permute-start | bytes 786440 | tf_op jit(solution)/shard_map/ppermute | solution.py:376
  40.6 12.7 %collective-permute-start.6 = (f32[4,64,256]{2,1,0:T(8,128)S(1)}, f32[4,64,256]{2,1,0:T(8,128)S(1)}, u32[]{:S(2)}, u32[]{:S(2)}) collective-permute-start(f32[4,64,256]{2,1,0:T(8,128)S(1)} %get-tuple-element.37), channel_id=1, source_target_pairs={{0,12},{4,8},{8,4},{12,0},{16,28},{20,24},{24,20},{28,16},{1,13},{... | collective-permute-start | bytes 786440 | tf_op jit(solution)/shard_map/ppermute | solution.py:376
  49.3 4.0 %collective-permute-start.4 = (f32[4,64,256]{2,1,0:T(8,128)S(1)}, f32[4,64,256]{2,1,0:T(8,128)S(1)}, u32[]{:S(2)}, u32[]{:S(2)}) collective-permute-start(f32[4,64,256]{2,1,0:T(8,128)S(1)} %get-tuple-element.36), channel_id=1, source_target_pairs={{0,4},{4,0},{8,12},{12,8},{16,20},{20,16},{24,28},{28,24},{1,5},{5... | collective-permute-start | bytes 786440 | tf_op jit(solution)/shard_map/ppermute | solution.py:376
  55.4 19.4 %collective-permute-start.10 = (f32[4,72,256]{2,1,0:T(8,128)S(1)}, f32[4,72,256]{2,1,0:T(8,128)S(1)}, u32[]{:S(2)}, u32[]{:S(2)}) collective-permute-start(f32[4,72,256]{2,1,0:T(8,128)S(1)} %get-tuple-element.41), channel_id=1, source_target_pairs={{0,2},{1,3},{2,0},{3,1},{4,6},{5,7},{6,4},{7,5},{8,10},{9,11},{10,... | collective-permute-start | bytes 884744 | tf_op jit(solution)/shard_map/ppermute | solution.py:376
  55.5 28.9 %collective-permute-start.11 = (f32[4,72,256]{2,1,0:T(8,128)S(1)}, f32[4,72,256]{2,1,0:T(8,128)S(1)}, u32[]{:S(2)}, u32[]{:S(2)}) collective-permute-start(f32[4,72,256]{2,1,0:T(8,128)S(1)} %get-tuple-element.42), channel_id=1, source_target_pairs={{0,3},{1,2},{2,1},{3,0},{4,7},{5,6},{6,5},{7,4},{8,11},{9,10},{10,... | collective-permute-start | bytes 884744 | tf_op jit(solution)/shard_map/ppermute | solution.py:376
  58.0 26.4 %collective-permute-start.9 = (f32[4,72,256]{2,1,0:T(8,128)S(1)}, f32[4,72,256]{2,1,0:T(8,128)S(1)}, u32[]{:S(2)}, u32[]{:S(2)}) collective-permute-start(f32[4,72,256]{2,1,0:T(8,128)S(1)} %get-tuple-element.40), channel_id=1, source_target_pairs={{0,1},{1,0},{2,3},{3,2},{4,5},{5,4},{6,7},{7,6},{8,9},{9,8},{10,11... | collective-permute-start | bytes 884744 | tf_op jit(solution)/shard_map/ppermute | solution.py:376

commit v5 on v4

--- a/solution.py
+++ b/solution.py
@@ -14,7 +14,9 @@
 TILE_DEV = 32
 PASSES = 3
 LANES = 128
+RIM_ROWS = 8
 ELEM_BLOCK = 256
+AHEAD = 3
 
 elem_pitch = 0.125
 cell_spacing = 0.7
@@ -57,7 +59,8 @@
     return found[:count]
 
 
-def project_kernel(sizes, part, first, waits, *refs):
+def project_kernel(sizes, rounds, turn, waits, *refs):
+    first = turn == 0
     pos_count, freqs, positions, elements, pos_local, freq_local, foot = sizes
     groups = pos_count // TH
     per_dest = TW // groups
@@ -65,10 +68,9 @@
     steps = pos_local * blocks
     where_ref, refs = refs[0], refs[1:]
     if first:
-        (foot_ref, basis_ref, conduct_ref, baseline_ref), refs = refs[:4], refs[4:]
+        (foot_ref, basis_ref), refs = refs[:2], refs[2:]
         out_refs, refs = refs[:groups], refs[groups:]
-        held_ref, depth_ref, lateral_ref, element_ref, rims_ref, head_ref, tail_ref = refs[:7]
-        green_even, green_odd, total_ref, sems = refs[7:]
+        held_ref, depth_ref, lateral_ref, element_ref, green_even, green_odd, total_ref, sems = refs
     else:
         held_ref, depth_ref, lateral_ref, element_ref = refs[:4]
         out_refs, refs = refs[4 + waits : 4 + waits + groups], refs[4 + waits + groups :]
@@ -81,7 +83,7 @@
         return pltpu.make_async_copy(basis_ref.at[offset, :, :, spot, :], held_ref.at[step], sems.at[step])
 
     if first:
-        for step in range(steps):
+        for step in range(AHEAD):
             fetch(step).start()
 
     first_freq = (my_freq * freq_local).astype(jnp.float32)
@@ -90,10 +92,14 @@
 
     if first:
         scale = 1.0 / top_depth
-        my_group = lax.rem(my_pos, groups)
         row = lax.broadcasted_iota(jnp.int32, (TW, LANES), 0)
         lane = lax.broadcasted_iota(jnp.int32, (TW, LANES), 1)
-        cell_col = ((row // per_dest) ^ my_group) * per_dest + row % per_dest
+        places = []
+        for distances in rounds:
+            target = my_pos ^ functools.reduce(
+                lambda rest, here: jnp.where(row // per_dest == here, distances[here], rest), range(1, groups), distances[0]
+            )
+            places.append((target // groups, (target % groups) * per_dest + row % per_dest))
         for offset in range(pos_local):
             pos_global = my_pos * pos_local + offset
             centre = pos_global.astype(jnp.float32) * (cell_spacing * TW * TILE_DEV / positions)
@@ -103,29 +109,23 @@
 
             def place(entry, _, offset=offset, pos_global=pos_global):
                 tile = foot_ref[pos_global, entry]
-                for other in range(TH):
-                    grid_row = (tile // TILE_DEV) * TH + ((my_pos // groups) ^ other)
-                    depth = scale * (top_depth + cell_spacing * jnp.full((TW, LANES), grid_row, jnp.int32).astype(jnp.float32))
-                    depth_ref[other, offset, entry] = depth * depth
-                grid_col = ((tile % TILE_DEV) * TW + cell_col).astype(jnp.float32)
-                lateral_ref[offset, entry] = scale * (cell_spacing * grid_col)
+                for number, (cell_row, cell_col) in enumerate(places):
+                    grid_row = ((tile // TILE_DEV) * TH + cell_row).astype(jnp.float32)
+                    grid_col = ((tile % TILE_DEV) * TW + cell_col).astype(jnp.float32)
+                    depth = scale * (top_depth + cell_spacing * grid_row)
+                    depth_ref[number, offset, entry] = depth * depth
+                    lateral_ref[number, offset, entry] = scale * (cell_spacing * grid_col)
                 return 0
 
-            lax.fori_loop(0, foot, place, 0, unroll=8)
-        columns = rims_ref.shape[1]
-        for number, block in enumerate((conduct_ref[0], conduct_ref[1], baseline_ref[...])):
-            span = slice(number * TH, (number + 1) * TH)
-            rims_ref[span, :] = block
-            head_ref[span, :] = block[:, :TW]
-            tail_ref[span, :] = block[:, columns - TW :]
+            lax.fori_loop(0, foot, place, 0, unroll=4)
     total_ref[...] = jnp.zeros_like(total_ref)
 
     def green(step, green_ref):
         offset, block = step // blocks, step % blocks
         for pair in range(foot // 2):
             entry = 2 * pair
-            depth_square = depth_ref[part, offset, pl.ds(entry, 2)].reshape(2 * TW, LANES)
-            lateral = lateral_ref[offset, pl.ds(entry, 2)].reshape(2 * TW, LANES)
+            depth_square = depth_ref[turn, offset, pl.ds(entry, 2)].reshape(2 * TW, LANES)
+            lateral = lateral_ref[turn, offset, pl.ds(entry, 2)].reshape(2 * TW, LANES)
             spot = pl.ds(entry * TW, 2 * TW)
             for sub in range(ELEM_BLOCK // LANES):
                 element = element_ref[offset, block * (ELEM_BLOCK // LANES) + sub]
@@ -148,6 +148,11 @@
         if use is not None:
             if first:
                 fetch(use).wait()
+                if isinstance(use, int):
+                    if use + AHEAD < steps:
+                        fetch(use + AHEAD).start()
+                else:
+                    pl.when(use + AHEAD < steps)(lambda: fetch(use + AHEAD).start())
             apply(use, out_of)
         if make is not None:
             green(make, into)
@@ -172,7 +177,8 @@
                     )
 
 
-def project(sizes, part, first, operands, after):
+def project(sizes, rounds, turn, operands, after):
+    first = turn == 0
     pos_count, freqs, positions, elements, pos_local, freq_local, foot = sizes
     groups = pos_count // TH
     per_dest = TW // groups
@@ -188,22 +194,18 @@
     vmem, smem = pl.BlockSpec(memory_space=pltpu.VMEM), pl.BlockSpec(memory_space=pltpu.SMEM)
     out_shape = [shape(per_dest, pos_local * foot, rank)] * groups
     if first:
-        in_specs = [smem, smem, pl.BlockSpec(memory_space=pl.ANY), vmem, vmem]
-        columns = operands[4].shape[1]
+        in_specs = [smem, smem, pl.BlockSpec(memory_space=pl.ANY)]
         out_shape += [
             shape(steps, freq_local, 2, ELEM_BLOCK, rank, dtype=jnp.bfloat16),
-            shape(TH, pos_local, foot, TW, LANES),
-            shape(pos_local, foot, TW, LANES),
+            shape(len(rounds), pos_local, foot, TW, LANES),
+            shape(len(rounds), pos_local, foot, TW, LANES),
             shape(pos_local, elements // LANES, TW, LANES),
-            shape(3 * TH, columns),
-            shape(3 * TH, TW),
-            shape(3 * TH, TW),
         ]
     else:
         in_specs = [smem] + [vmem] * 4 + [pl.BlockSpec(memory_space=pl.ANY)] * len(after)
     green = pltpu.VMEM((rows, freq_local * 2 * ELEM_BLOCK), jnp.bfloat16)
     return pl.pallas_call(
-        functools.partial(project_kernel, sizes, part, first, len(after)),
+        functools.partial(project_kernel, sizes, rounds, turn, len(after)),
         in_specs=in_specs,
         out_specs=[vmem] * len(out_shape),
         out_shape=out_shape,
@@ -211,7 +213,7 @@
         + ([pltpu.SemaphoreType.DMA((steps,))] if first else []),
         compiler_params=pltpu.CompilerParams(vmem_limit_bytes=VMEM_LIMIT_FIRST if first else VMEM_LIMIT),
         cost_estimate=pl.CostEstimate(flops=flops, bytes_accessed=flops, transcendentals=0),
-        name=f"project_{part}",
+        name=f"project_{turn}",
     )(*operands, *after)
 
 
@@ -220,10 +222,10 @@
     return high, (values - high.astype(jnp.float32)).astype(jnp.bfloat16)
 
 
-def gather_kernel(pos_count, freq_count, tile_rows, where_ref, ids_ref, *refs):
+def gather_kernel(pos_count, freq_count, tile_rows, shard, where_ref, ids_ref, conduct_ref, baseline_ref, *refs):
     in_refs, out_refs = refs[:pos_count], refs[pos_count:]
     cells, entries, rank = in_refs[0].shape
-    shard = out_refs[0].shape[1]
+    columns = baseline_ref.shape[1]
     tile_cols = shard // tile_rows
     groups = pos_count // TH
     my_pos, my_freq = where_ref[0], where_ref[1]
@@ -245,33 +247,43 @@
         values = jnp.concatenate([ref[cell] for ref in in_refs], axis=0)
         terms = jnp.concatenate(two_terms(values), axis=0)
         for other in range(freq_count):
-            out_refs[other][cell] = jnp.dot(hot[other], terms, preferred_element_type=jnp.float32)
-
-
-def gather_tiles(freq_count, where, ids, parts):
+            span = slice(cell * shard, (cell + 1) * shard)
+            out_refs[other][span, :] = jnp.dot(hot[other], terms, preferred_element_type=jnp.float32)
+    last = cells * shard
+    for ref in out_refs[1:]:
+        ref[last : last + RIM_ROWS, :] = jnp.zeros((RIM_ROWS, rank), jnp.float32)
+        for number, block in enumerate((conduct_ref[0], conduct_ref[1], baseline_ref[...])):
+            start = number * 2 * TW
+            ref[last : last + TH, start : start + TW] = block[:, :TW]
+            ref[last : last + TH, start + TW : start + 2 * TW] = block[:, columns - TW :]
+
+
+def gather_tiles(freq_count, where, ids, conduct, baseline, parts):
     pos_count = len(parts)
     cells, entries, rank = parts[0].shape
     tile_rows = pos_count
     shard = (TILE_DEV // freq_count + 1) * tile_rows
     return pl.pallas_call(
-        functools.partial(gather_kernel, pos_count, freq_count, tile_rows),
-        in_specs=[pl.BlockSpec(memory_space=pltpu.SMEM), pl.BlockSpec(memory_space=pltpu.VMEM)]
-        + [pl.BlockSpec(memory_space=pltpu.VMEM)] * pos_count,
+        functools.partial(gather_kernel, pos_count, freq_count, tile_rows, shard),
+        in_specs=[pl.BlockSpec(memory_space=pltpu.SMEM)] + [pl.BlockSpec(memory_space=pltpu.VMEM)] * (3 + pos_count),
         out_specs=[pl.BlockSpec(memory_space=pltpu.VMEM)] * freq_count,
-        out_shape=[jax.ShapeDtypeStruct((cells, shard, rank), jnp.float32)] * freq_count,
+        out_shape=[jax.ShapeDtypeStruct((cells * shard, rank), jnp.float32)]
+        + [jax.ShapeDtypeStruct((cells * shard + RIM_ROWS, rank), jnp.float32)] * (freq_count - 1),
         compiler_params=pltpu.CompilerParams(vmem_limit_bytes=VMEM_LIMIT),
         name="tiles",
-    )(where, ids, *parts)
-
-
-def energy_kernel(freq_count, weights_ref, rims_ref, left_ref, right_ref, *refs):
+    )(where, ids, conduct, baseline, *parts)
+
+
+def energy_kernel(cells, shard, freq_count, where_ref, weights_ref, conduct_ref, baseline_ref, *refs):
     in_refs, out_ref = refs[:freq_count], refs[freq_count]
-    cells, shard, rank = in_refs[0].shape
+    rank = in_refs[0].shape[1]
+    my_freq = where_ref[1]
     weights = jnp.broadcast_to(weights_ref[...], (8, rank))
     for cell in range(cells):
-        summed = in_refs[0][cell]
+        span = slice(cell * shard, (cell + 1) * shard)
+        summed = in_refs[0][span, :]
         for ref in in_refs[1:]:
-            summed = summed + ref[cell]
+            summed = summed + ref[span, :]
         energy = lax.dot_general(
             weights,
             summed * summed,
@@ -279,25 +291,35 @@
             precision=HIGHEST,
             preferred_element_type=jnp.float32,
         )
-        out_ref[pl.ds(cell, 1), 0:shard] = jnp.sqrt(energy[0:1] / rank + eps_value)
-    rims, edge = rims_ref.shape, left_ref.shape[1]
-    out_ref[cells : cells + rims[0], 0 : rims[1]] = rims_ref[...]
-    out_ref[cells : cells + rims[0], rims[1] : rims[1] + edge] = right_ref[...]
-    out_ref[cells : cells + rims[0], out_ref.shape[1] - edge :] = left_ref[...]
-
-
-def energies(weights, rims, left, right, shards):
-    cells, shard, rank = shards[0].shape
-    rows = cells + rims.shape[0]
-    width = -(-max(shard, rims.shape[1] + 2 * left.shape[1]) // LANES) * LANES
+        out_ref[cell : cell + 1, 0:shard] = jnp.sqrt(energy[0:1] / rank + eps_value)
+    last = cells * shard
+    left = jnp.zeros((TH, LANES), jnp.float32)
+    right = jnp.zeros((TH, LANES), jnp.float32)
+    for distance in range(1, freq_count):
+        edge = in_refs[distance][last : last + TH, 0:LANES]
+        partner = my_freq ^ distance
+        left = jnp.where(partner == my_freq - 1, edge, left)
+        right = jnp.where(partner == my_freq + 1, edge, right)
+    columns, width = baseline_ref.shape[1], out_ref.shape[1]
+    for number, block in enumerate((conduct_ref[0], conduct_ref[1], baseline_ref[...])):
+        span = slice(cells + number * TH, cells + (number + 1) * TH)
+        start = number * 2 * TW
+        out_ref[span, 0:columns] = block
+        out_ref[span, columns : columns + TW] = right[:, start : start + TW]
+        out_ref[span, LANES - TW : LANES] = left[:, start + TW : start + 2 * TW]
+
+
+def energies(cells, shard, where, weights, conduct, baseline, shards):
+    rows = cells + 3 * TH
+    width = -(-max(shard, baseline.shape[1] + 2 * TW) // LANES) * LANES
     return pl.pallas_call(
-        functools.partial(energy_kernel, len(shards)),
-        in_specs=[pl.BlockSpec(memory_space=pltpu.VMEM)] * (4 + len(shards)),
+        functools.partial(energy_kernel, cells, shard, len(shards)),
+        in_specs=[pl.BlockSpec(memory_space=pltpu.SMEM)] + [pl.BlockSpec(memory_space=pltpu.VMEM)] * (3 + len(shards)),
         out_specs=pl.BlockSpec(memory_space=pltpu.VMEM),
         out_shape=jax.ShapeDtypeStruct((rows, width), jnp.float32),
         compiler_params=pltpu.CompilerParams(vmem_limit_bytes=VMEM_LIMIT),
         name="energies",
-    )(weights, rims, left, right, *shards)
+    )(where, weights, conduct, baseline, *shards)
 
 
 def diffuse_kernel(cells, shard, where_ref, strips_ref, out_ref, field_ref):
@@ -396,29 +418,30 @@
     ids = footprint.reshape(pos_count, pos_local * foot)
     split = basis.reshape(pos_local, freq_local, 2, elements, rank)
     groups = pos_count // TH
+    half = groups // 2
     parts = [None] * pos_count
-    operands, after = (where, footprint, split, conduct, baseline), ()
-    for part in range(TH - 1, -1, -1):
-        first = part == TH - 1
-        sent = project(sizes, part, first, operands, after)
-        for group in range(groups):
-            distance = part * groups + group
-            parts[distance] = swap(sent[group], "pos", distance) if distance else sent[group]
+    rounds = (
+        tuple(range(3 * groups, 4 * groups)),
+        tuple(range(2 * groups, 2 * groups + half)) + tuple(range(groups, groups + half)),
+        tuple(range(2 * groups + half, 3 * groups)) + tuple(range(groups + half, 2 * groups)),
+        tuple(range(groups)),
+    )
+    operands, after = (where, footprint, split), ()
+    for turn, distances in enumerate(rounds):
+        sent = project(sizes, rounds, turn, operands, after)
+        for number, distance in enumerate(distances):
+            parts[distance] = swap(sent[number], "pos", distance) if distance else sent[number]
+        if turn == 0:
+            operands = (where,) + tuple(sent[groups:])
         after = (sent[0],)
-        if first:
-            held, depth, lateral, element, rims, head, tail = sent[groups:]
-            operands = where, held, depth, lateral, element
-            left = lax.ppermute(tail, "freq", [(i, i + 1) for i in range(freq_count - 1)])
-            right = lax.ppermute(head, "freq", [(i + 1, i) for i in range(freq_count - 1)])
-        if part == 2:
-            after += (left, right)
-        if part == 1:
-            after += tuple(parts[-groups:])
-    tiles = gather_tiles(freq_count, where, ids, parts)
+        if turn == 2:
+            after += tuple(parts[distance] for past in rounds[:2] for distance in past)
+    cells, shard = CELLS // pos_count, (TILE_DEV // freq_count + 1) * pos_count
+    tiles = gather_tiles(freq_count, where, ids, conduct, baseline, parts)
     shards = [swap(tiles[d], "freq", d) if d else tiles[d] for d in range(freq_count)]
-    strip = energies(weights.reshape(1, rank), rims, left, right, shards)
+    strip = energies(cells, shard, where, weights.reshape(1, rank), conduct, baseline, shards)
     strips = lax.all_gather(strip, "pos")
-    return diffuse(CELLS // pos_count, shards[0].shape[1], where, strips, columns)
+    return diffuse(cells, shard, where, strips, columns)
 
 
 def solution(mesh):

time: 96 us -> 96.5 us (level)
  waiting for transfers between devices: 29.2 us -> 35 us
  starting transfers between devices: 16.4 us -> 10.8 us
  local copies, waits for them, and re-layouts: 2.14 us -> 0.79 us
  blocking collectives: 9.15 us -> 10.3 us
    ppermute x10, waiting for transfers between devices: 29.2 us -> 35 us  [swap(): lax.ppermute(array, axis, [(i, i ^ distance) for i in range(lax.axis_size...]
    ppermute x2 -> x0, starting transfers between devices: 5.28 us -> none  [the longest x1 3.21 us: body(): lax.ppermute(tail, 'freq', [(i, i + 1) for i in range(freq_count - 1)])]
    unnamed x10, local copies, waits for them, and re-layouts: 2.07 us -> 0.72 us
    all_gather x1, blocking collectives: 9.15 us -> 10.3 us  [body(): strips = lax.all_gather(strip, 'pos')]
  transfers between devices with their start and end apart: 12 -> 10, of which waited for: 3 -> 5; matrix products, arithmetic and copies ran while one was open for 0% -> 0% of each run, Pallas kernels for 24% -> 16%
where the time goes in v5:
time: 96.5 us; the launch traced here: 96.2 us
  Pallas kernels  39.2 us (41%)
  waiting for transfers between devices  35 us (36%)
  starting transfers between devices  10.8 us (11%)
  blocking collectives  10.3 us (11%)
    ppermute x10, waiting for transfers between devices, swap(): lax.ppermute(array, axis, [(i, i ^ distance) for i in range(lax.axis_size...  35 us
    pallas_call x4, Pallas kernels, project(): pl.pallas_call(functools.partial(project_kernel, sizes, rounds, turn, len...  34.4 us
    ppermute x10, starting transfers between devices, swap(): lax.ppermute(array, axis, [(i, i ^ distance) for i in range(lax.axis_size...  10.8 us
    all_gather x1, blocking collectives, body(): strips = lax.all_gather(strip, 'pos')  10.3 us
    pallas_call x1, Pallas kernels, gather_tiles(): pl.pallas_call(functools.partial(gather_kernel, pos_count, freq_count, ti...  2.12 us
  transfers between devices with their start and end apart: 10, of which 5 were waited for; matrix products, arithmetic and copies ran while one was open for 0% of the time, Pallas kernels for 16%

profile of v5, /device:TPU:17, one launch (start us, length us, event | category | flops | bytes accessed | tf_op | source)
XLA Modules:
  0.0 96.2 jit_solution(6842151782735914061)
XLA Ops:
  0.0 0.1 pad_add_fusion.refs_0_.where_ref
  0.1 0.0 copy-start
  0.1 0.7 copy-done
  0.8 11.0 %project_0.1 = (f32[4,64,256]{2,1,0:T(8,128)S(1)}, f32[4,64,256]{2,1,0:T(8,128)S(1)}, bf16[8,4,2,256,256]{4,3,2,1,0:T(8,128)(2,1)S(1)}, f32[4,2,32,8,128]{4,3,2,...) custom-call(s32[2]{0:T(128)S(1)} %pad_add_fusion.refs_0_.where_ref, ...), custom_call_target="tpu_custom_call" | custom-call | flops 2147483648 | bytes 2147483648 | tf_op jit(solution)/shard_map/project_0/pallas_call | solution.py:207
  11.8 7.7 %project_1.1 = (f32[4,64,256]{2,1,0:T(8,128)S(1)}, f32[4,64,256]{2,1,0:T(8,128)S(1)}) custom-call(s32[2]{0:T(128)S(1)} %pad_add_fusion.refs_0_.where_ref, bf16[8,4,2,256,256]{4,3,2,1,0:T(8,128)(2,1)S(1)} %get-tuple-element.21.refs_1_, f32[4,2,32,8,128]{4,3,2,1,0:T(8,128)S(1)} %get-tuple-element.22.refs_2_, ...), custom_call_target="tpu_custom_call" | custom-call | flops 2147483648 | bytes 2147483648 | tf_op jit(solution)/shard_map/project_1/pallas_call | solution.py:207
  19.5 1.3 %collective-permute-start.2 = (f32[4,64,256]{2,1,0:T(8,128)S(1)}, f32[4,64,256]{2,1,0:T(8,128)S(1)}, u32[]{:S(2)}, u32[]{:S(2)}) collective-permute-start(f32[4,64,256]{2,1,0:T(8,128)S(1)} %get-tuple-element.26.refs_5_), channel_id=1, source_target_pairs={{0,16},{4,20},{8,24},{12,28},{16,0},{20,4},{24,8},{28,12},{1,17},{... | collective-permute-start | bytes 786440 | tf_op jit(solution)/shard_map/ppermute | solution.py:398
  20.8 1.2 %collective-permute-start = (f32[4,64,256]{2,1,0:T(8,128)S(1)}, f32[4,64,256]{2,1,0:T(8,128)S(1)}, u32[]{:S(2)}, u32[]{:S(2)}) collective-permute-start(f32[4,64,256]{2,1,0:T(8,128)S(1)} %get-tuple-element.25.refs_5_), channel_id=1, source_target_pairs={{0,24},{4,28},{8,16},{12,20},{16,8},{20,12},{24,0},{28,4},{1,25},{... | collective-permute-start | bytes 786440 | tf_op jit(solution)/shard_map/ppermute | solution.py:398
  22.0 0.3 collective-permute-start.3
  22.2 3.6 %collective-permute-start.1 = (f32[4,64,256]{2,1,0:T(8,128)S(1)}, f32[4,64,256]{2,1,0:T(8,128)S(1)}, u32[]{:S(2)}, u32[]{:S(2)}) collective-permute-start(f32[4,64,256]{2,1,0:T(8,128)S(1)} %get-tuple-element.28), channel_id=1, source_target_pairs={{0,28},{4,24},{8,20},{12,16},{16,12},{20,8},{24,4},{28,0},{1,29},{... | collective-permute-start | bytes 786440 | tf_op jit(solution)/shard_map/ppermute | solution.py:398
  25.8 7.7 %project_2.1 = (f32[4,64,256]{2,1,0:T(8,128)S(1)}, f32[4,64,256]{2,1,0:T(8,128)S(1)}) custom-call(s32[2]{0:T(128)S(1)} %pad_add_fusion.refs_0_.where_ref, bf16[8,4,2,256,256]{4,3,2,1,0:T(8,128)(2,1)S(1)} %get-tuple-element.21.refs_1_, f32[4,2,32,8,128]{4,3,2,1,0:T(8,128)S(1)} %get-tuple-element.22.refs_2_, ...), custom_call_target="tpu_custom_call" | custom-call | flops 2147483648 | bytes 2147483648 | tf_op jit(solution)/shard_map/project_2/pallas_call | solution.py:207
  33.5 0.0 copy-start.1
  33.5 0.0 copy-start.2
  33.6 0.0 copy-start.3
  33.6 0.0 copy-start.4
  33.6 0.1 collective-permute-start.5
  33.7 0.0 collective-permute-done.2.refs_8_.refs_4_
  33.7 1.6 %collective-permute-start.6 = (f32[4,64,256]{2,1,0:T(8,128)S(1)}, f32[4,64,256]{2,1,0:T(8,128)S(1)}, u32[]{:S(2)}, u32[]{:S(2)}) collective-permute-start(f32[4,64,256]{2,1,0:T(8,128)S(1)} %get-tuple-element.27.refs_5_), channel_id=1, source_target_pairs={{0,20},{4,16},{8,28},{12,24},{16,4},{20,0},{24,12},{28,8},{1,21},{... | collective-permute-start | bytes 786440 | tf_op jit(solution)/shard_map/ppermute | solution.py:398
  35.3 0.0 collective-permute-done.3.refs_9_.refs_2_
  35.3 0.0 collective-permute-done.refs_6_
  35.3 7.2 %collective-permute-done.1.refs_7_ = f32[4,64,256]{2,1,0:T(8,128)S(1)} collective-permute-done((f32[4,64,256]{2,1,0:T(8,128)S(1)}, f32[4,64,256]{2,1,0:T(8,128)S(1)}, u32[]{:S(2)}, u32[]{:S(2)}) %collective-permute-start.1) | collective-permute-done | bytes 262176 | tf_op jit(solution)/shard_map/ppermute | solution.py:398
  42.5 7.9 %project_3.1 = (f32[4,64,256]{2,1,0:T(8,128)S(1)}, f32[4,64,256]{2,1,0:T(8,128)S(1)}) custom-call(s32[2]{0:T(128)S(1)} %pad_add_fusion.refs_0_.where_ref, bf16[8,4,2,256,256]{4,3,2,1,0:T(8,128)(2,1)S(1)} %get-tuple-element.21.refs_1_, f32[4,2,32,8,128]{4,3,2,1,0:T(8,128)S(1)} %get-tuple-element.22.refs_2_, ...), custom_call_target="tpu_custom_call" | custom-call | flops 2147483648 | bytes 2147483648 | tf_op jit(solution)/shard_map/project_3/pallas_call | solution.py:207
  50.4 0.1 collective-permute-start.4
  50.5 0.0 copy-done.1
  50.5 0.1 reshape.10.ids_ref
  50.6 0.0 collective-permute-done.5.refs_3_
  50.6 0.0 collective-permute-done.6.refs_5_
  50.6 1.4 %collective-permute-done.4.refs_1_ = f32[4,64,256]{2,1,0:T(8,128)S(1)} collective-permute-done((f32[4,64,256]{2,1,0:T(8,128)S(1)}, f32[4,64,256]{2,1,0:T(8,128)S(1)}, u32[]{:S(2)}, u32[]{:S(2)}) %collective-permute-start.4) | collective-permute-done | bytes 262176 | tf_op jit(solution)/shard_map/ppermute | solution.py:398
  52.0 0.0 copy-done.2
  52.0 0.0 copy-done.3
  52.0 2.1 %tiles.1 = (f32[288,256]{1,0:T(8,128)S(1)}, f32[296,256]{1,0:T(8,128)S(1)}, f32[296,256]{1,0:T(8,128)S(1)}, f32[296,256]{1,0:T(8,128)S(1)}) custom-call(s32[2]{0:T(128)S(1)} %pad_add_fusion.refs_0_.where_ref, s32[8,64]{1,0:T(8,128)S(1)} %reshape.10.ids_ref, f32[2,4,64]{2,1,0:T(4,128)S(1)} %copy-done.2, f32[4,64]{1,0:T(4,128)S(1)} %copy-done.3, ...), custom_call_target="tpu_custom_call" | custom-call | tf_op jit(solution)/shard_map/tiles/pallas_call | solution.py:266
  54.1 1.4 %collective-permute-start.7 = (f32[296,256]{1,0:T(8,128)S(1)}, f32[296,256]{1,0:T(8,128)S(1)}, u32[]{:S(2)}, u32[]{:S(2)}) collective-permute-start(f32[296,256]{1,0:T(8,128)S(1)} %get-tuple-element.34), channel_id=1, source_target_pairs={{0,1},{1,0},{2,3},{3,2},{4,5},{5,4},{6,7},{7,6},{8,9},{9,8},{10,11... | collective-permute-start | bytes 909320 | tf_op jit(solution)/shard_map/ppermute | solution.py:398
  55.5 0.1 collective-permute-start.8
  55.6 1.3 %collective-permute-start.9 = (f32[296,256]{1,0:T(8,128)S(1)}, f32[296,256]{1,0:T(8,128)S(1)}, u32[]{:S(2)}, u32[]{:S(2)}) collective-permute-start(f32[296,256]{1,0:T(8,128)S(1)} %get-tuple-element.36), channel_id=1, source_target_pairs={{0,3},{1,2},{2,1},{3,0},{4,7},{5,6},{6,5},{7,4},{8,11},{9,10},{10,... | collective-permute-start | bytes 909320 | tf_op jit(solution)/shard_map/ppermute | solution.py:398
  56.9 10.3 %collective-permute-done.7.refs_1_ = f32[296,256]{1,0:T(8,128)S(1)} collective-permute-done((f32[296,256]{1,0:T(8,128)S(1)}, f32[296,256]{1,0:T(8,128)S(1)}, u32[]{:S(2)}, u32[]{:S(2)}) %collective-permute-start.7) | collective-permute-done | bytes 303136 | tf_op jit(solution)/shard_map/ppermute | solution.py:398
  67.2 2.1 %collective-permute-done.8.refs_2_ = f32[296,256]{1,0:T(8,128)S(1)} collective-permute-done((f32[296,256]{1,0:T(8,128)S(1)}, f32[296,256]{1,0:T(8,128)S(1)}, u32[]{:S(2)}, u32[]{:S(2)}) %collective-permute-start.8) | collective-permute-done | bytes 303136 | tf_op jit(solution)/shard_map/ppermute | solution.py:398
  69.3 14.0 %collective-permute-done.9.refs_3_ = f32[296,256]{1,0:T(8,128)S(1)} collective-permute-done((f32[296,256]{1,0:T(8,128)S(1)}, f32[296,256]{1,0:T(8,128)S(1)}, u32[]{:S(2)}, u32[]{:S(2)}) %collective-permute-start.9) | collective-permute-done | bytes 303136 | tf_op jit(solution)/shard_map/ppermute | solution.py:398
  83.2 0.0 copy-done.4
  83.2 0.9 energies.1
  84.2 10.3 %all-gather = f32[128,128]{1,0:T(8,128)S(1)} all-gather(f32[16,128]{1,0:T(8,128)S(1)} %energies.1), channel_id=2, replica_groups=mesh['pos'=8,'freq'=4] {'pos'}, dimensions={0}, use_global_device_ids=true | all-gather | bytes 73728 | tf_op jit(solution)/shard_map/all_gather | solution.py:443
  94.5 1.8 %diffuse.1 = f32[4,64]{1,0:T(4,128)} custom-call(s32[2]{0:T(128)S(1)} %pad_add_fusion.refs_0_.where_ref, f32[8,16,128]{2,1,0:T(8,128)S(1)} %bitcast.5), custom_call_target="tpu_custom_call" | custom-call | tf_op jit(solution)/shard_map/diffuse/pallas_call | solution.py:386
Async XLA Ops:
  0.1 0.7 copy-start
  19.5 14.1 %collective-permute-start.2 = (f32[4,64,256]{2,1,0:T(8,128)S(1)}, f32[4,64,256]{2,1,0:T(8,128)S(1)}, u32[]{:S(2)}, u32[]{:S(2)}) collective-permute-start(f32[4,64,256]{2,1,0:T(8,128)S(1)} %get-tuple-element.26.refs_5_), channel_id=1, source_target_pairs={{0,16},{4,20},{8,24},{12,28},{16,0},{20,4},{24,8},{28,12},{1,17},{... | collective-permute-start | bytes 786440 | tf_op jit(solution)/shard_map/ppermute | solution.py:398
  20.8 14.5 %collective-permute-start = (f32[4,64,256]{2,1,0:T(8,128)S(1)}, f32[4,64,256]{2,1,0:T(8,128)S(1)}, u32[]{:S(2)}, u32[]{:S(2)}) collective-permute-start(f32[4,64,256]{2,1,0:T(8,128)S(1)} %get-tuple-element.25.refs_5_), channel_id=1, source_target_pairs={{0,24},{4,28},{8,16},{12,20},{16,8},{20,12},{24,0},{28,4},{1,25},{... | collective-permute-start | bytes 786440 | tf_op jit(solution)/shard_map/ppermute | solution.py:398
  22.0 13.3 %collective-permute-start.3 = (f32[4,64,256]{2,1,0:T(8,128)S(1)}, f32[4,64,256]{2,1,0:T(8,128)S(1)}, u32[]{:S(2)}, u32[]{:S(2)}) collective-permute-start(f32[4,64,256]{2,1,0:T(8,128)S(1)} %get-tuple-element.29), channel_id=1, source_target_pairs={{0,8},{4,12},{8,0},{12,4},{16,24},{20,28},{24,16},{28,20},{1,9},{5... | collective-permute-start | bytes 786440 | tf_op jit(solution)/shard_map/ppermute | solution.py:398
  22.2 20.3 %collective-permute-start.1 = (f32[4,64,256]{2,1,0:T(8,128)S(1)}, f32[4,64,256]{2,1,0:T(8,128)S(1)}, u32[]{:S(2)}, u32[]{:S(2)}) collective-permute-start(f32[4,64,256]{2,1,0:T(8,128)S(1)} %get-tuple-element.28), channel_id=1, source_target_pairs={{0,28},{4,24},{8,20},{12,16},{16,12},{20,8},{24,4},{28,0},{1,29},{... | collective-permute-start | bytes 786440 | tf_op jit(solution)/shard_map/ppermute | solution.py:398
  33.5 17.0 %copy-start.1 = (s32[16,32]{1,0:T(8,128)S(1)}, s32[16,32]{1,0:T(8,128)}, u32[]{:S(2)}) copy-start(s32[16,32]{1,0:T(8,128)} %refs_1_.1) | copy-start | bytes 6148
  33.5 18.5 %copy-start.2 = (f32[2,4,64]{2,1,0:T(4,128)S(1)}, f32[2,4,64]{2,1,0:T(4,128)}, u32[]{:S(2)}) copy-start(f32[2,4,64]{2,1,0:T(4,128)} %conduct_ref.3) | copy-start | bytes 6148
  33.6 18.5 %copy-start.3 = (f32[4,64]{1,0:T(4,128)S(1)}, f32[4,64]{1,0:T(4,128)}, u32[]{:S(2)}) copy-start(f32[4,64]{1,0:T(4,128)} %baseline_ref.3) | copy-start | bytes 3076
  33.6 49.7 %copy-start.4 = (f32[256]{0:T(256)S(1)}, f32[256]{0:T(256)}, u32[]{:S(2)}) copy-start(f32[256]{0:T(256)} %param.7) | copy-start | bytes 3076
  33.6 17.0 %collective-permute-start.5 = (f32[4,64,256]{2,1,0:T(8,128)S(1)}, f32[4,64,256]{2,1,0:T(8,128)S(1)}, u32[]{:S(2)}, u32[]{:S(2)}) collective-permute-start(f32[4,64,256]{2,1,0:T(8,128)S(1)} %get-tuple-element.32), channel_id=1, source_target_pairs={{0,12},{4,8},{8,4},{12,0},{16,28},{20,24},{24,20},{28,16},{1,13},{... | collective-permute-start | bytes 786440 | tf_op jit(solution)/shard_map/ppermute | solution.py:398
  33.7 16.9 %collective-permute-start.6 = (f32[4,64,256]{2,1,0:T(8,128)S(1)}, f32[4,64,256]{2,1,0:T(8,128)S(1)}, u32[]{:S(2)}, u32[]{:S(2)}) collective-permute-start(f32[4,64,256]{2,1,0:T(8,128)S(1)} %get-tuple-element.27.refs_5_), channel_id=1, source_target_pairs={{0,20},{4,16},{8,28},{12,24},{16,4},{20,0},{24,12},{28,8},{1,21},{... | collective-permute-start | bytes 786440 | tf_op jit(solution)/shard_map/ppermute | solution.py:398
  50.4 1.6 %collective-permute-start.4 = (f32[4,64,256]{2,1,0:T(8,128)S(1)}, f32[4,64,256]{2,1,0:T(8,128)S(1)}, u32[]{:S(2)}, u32[]{:S(2)}) collective-permute-start(f32[4,64,256]{2,1,0:T(8,128)S(1)} %get-tuple-element.31), channel_id=1, source_target_pairs={{0,4},{4,0},{8,12},{12,8},{16,20},{20,16},{24,28},{28,24},{1,5},{5... | collective-permute-start | bytes 786440 | tf_op jit(solution)/shard_map/ppermute | solution.py:398
  54.1 13.1 %collective-permute-start.7 = (f32[296,256]{1,0:T(8,128)S(1)}, f32[296,256]{1,0:T(8,128)S(1)}, u32[]{:S(2)}, u32[]{:S(2)}) collective-permute-start(f32[296,256]{1,0:T(8,128)S(1)} %get-tuple-element.34), channel_id=1, source_target_pairs={{0,1},{1,0},{2,3},{3,2},{4,5},{5,4},{6,7},{7,6},{8,9},{9,8},{10,11... | collective-permute-start | bytes 909320 | tf_op jit(solution)/shard_map/ppermute | solution.py:398
  55.5 13.8 %collective-permute-start.8 = (f32[296,256]{1,0:T(8,128)S(1)}, f32[296,256]{1,0:T(8,128)S(1)}, u32[]{:S(2)}, u32[]{:S(2)}) collective-permute-start(f32[296,256]{1,0:T(8,128)S(1)} %get-tuple-element.35), channel_id=1, source_target_pairs={{0,2},{1,3},{2,0},{3,1},{4,6},{5,7},{6,4},{7,5},{8,10},{9,11},{10,... | collective-permute-start | bytes 909320 | tf_op jit(solution)/shard_map/ppermute | solution.py:398
  55.6 27.7 %collective-permute-start.9 = (f32[296,256]{1,0:T(8,128)S(1)}, f32[296,256]{1,0:T(8,128)S(1)}, u32[]{:S(2)}, u32[]{:S(2)}) collective-permute-start(f32[296,256]{1,0:T(8,128)S(1)} %get-tuple-element.36), channel_id=1, source_target_pairs={{0,3},{1,2},{2,1},{3,0},{4,7},{5,6},{6,5},{7,4},{8,11},{9,10},{10,... | collective-permute-start | bytes 909320 | tf_op jit(solution)/shard_map/ppermute | solution.py:398

commit v6 on v5

--- a/solution.py
+++ b/solution.py
@@ -70,7 +70,7 @@
     if first:
         (foot_ref, basis_ref), refs = refs[:2], refs[2:]
         out_refs, refs = refs[:groups], refs[groups:]
-        held_ref, depth_ref, lateral_ref, element_ref, green_even, green_odd, total_ref, sems = refs
+        kept_ref, depth_ref, lateral_ref, element_ref, green_even, green_odd, total_ref, held_ref, sems, kept_sems = refs
     else:
         held_ref, depth_ref, lateral_ref, element_ref = refs[:4]
         out_refs, refs = refs[4 + waits : 4 + waits + groups], refs[4 + waits + groups :]
@@ -81,6 +81,9 @@
         offset, block = step // blocks, step % blocks
         spot = pl.ds(block * ELEM_BLOCK, ELEM_BLOCK)
         return pltpu.make_async_copy(basis_ref.at[offset, :, :, spot, :], held_ref.at[step], sems.at[step])
+
+    def keep(step):
+        return pltpu.make_async_copy(held_ref.at[step], kept_ref.at[step], kept_sems.at[step])
 
     if first:
         for step in range(AHEAD):
@@ -148,6 +151,7 @@
         if use is not None:
             if first:
                 fetch(use).wait()
+                keep(use).start()
                 if isinstance(use, int):
                     if use + AHEAD < steps:
                         fetch(use + AHEAD).start()
@@ -168,6 +172,9 @@
     run(steps - 1, green_odd, steps - 2, green_even)
     run(None, None, steps - 1, green_odd)
 
+    if first:
+        for step in range(steps):
+            keep(step).wait()
     for offset in range(pos_local):
         for group in range(groups):
             for cell in range(per_dest):
@@ -207,10 +214,19 @@
     return pl.pallas_call(
         functools.partial(project_kernel, sizes, rounds, turn, len(after)),
         in_specs=in_specs,
-        out_specs=[vmem] * len(out_shape),
+        out_specs=[vmem] * groups
+        + ([pl.BlockSpec(memory_space=pl.ANY)] + [vmem] * 3 if first else []),
         out_shape=out_shape,
         scratch_shapes=[green, green, pltpu.VMEM((pos_local, rank // LANES, rows, LANES), jnp.float32)]
-        + ([pltpu.SemaphoreType.DMA((steps,))] if first else []),
+        + (
+            [
+                pltpu.VMEM((steps, freq_local, 2, ELEM_BLOCK, rank), jnp.bfloat16),
+                pltpu.SemaphoreType.DMA((steps,)),
+                pltpu.SemaphoreType.DMA((steps,)),
+            ]
+            if first
+            else []
+        ),
         compiler_params=pltpu.CompilerParams(vmem_limit_bytes=VMEM_LIMIT_FIRST if first else VMEM_LIMIT),
         cost_estimate=pl.CostEstimate(flops=flops, bytes_accessed=flops, transcendentals=0),
         name=f"project_{turn}",
@@ -220,6 +236,11 @@
 def two_terms(values):
     high = values.astype(jnp.bfloat16)
     return high, (values - high.astype(jnp.float32)).astype(jnp.bfloat16)
+
+
+def rim_spot(last, number):
+    start = last + number % 2 * TH
+    return slice(start, start + TH), number // 2 * LANES
 
 
 def gather_kernel(pos_count, freq_count, tile_rows, shard, where_ref, ids_ref, conduct_ref, baseline_ref, *refs):
@@ -251,11 +272,10 @@
             out_refs[other][span, :] = jnp.dot(hot[other], terms, preferred_element_type=jnp.float32)
     last = cells * shard
     for ref in out_refs[1:]:
-        ref[last : last + RIM_ROWS, :] = jnp.zeros((RIM_ROWS, rank), jnp.float32)
         for number, block in enumerate((conduct_ref[0], conduct_ref[1], baseline_ref[...])):
-            start = number * 2 * TW
-            ref[last : last + TH, start : start + TW] = block[:, :TW]
-            ref[last : last + TH, start + TW : start + 2 * TW] = block[:, columns - TW :]
+            rows, lane = rim_spot(last, number)
+            ref[rows, lane + columns : lane + columns + TW] = block[:, :TW]
+            ref[rows, lane + LANES - TW : lane + LANES] = block[:, columns - TW :]
 
 
 def gather_tiles(freq_count, where, ids, conduct, baseline, parts):
@@ -293,20 +313,20 @@
         )
         out_ref[cell : cell + 1, 0:shard] = jnp.sqrt(energy[0:1] / rank + eps_value)
     last = cells * shard
-    left = jnp.zeros((TH, LANES), jnp.float32)
-    right = jnp.zeros((TH, LANES), jnp.float32)
-    for distance in range(1, freq_count):
-        edge = in_refs[distance][last : last + TH, 0:LANES]
-        partner = my_freq ^ distance
-        left = jnp.where(partner == my_freq - 1, edge, left)
-        right = jnp.where(partner == my_freq + 1, edge, right)
-    columns, width = baseline_ref.shape[1], out_ref.shape[1]
+    columns = baseline_ref.shape[1]
     for number, block in enumerate((conduct_ref[0], conduct_ref[1], baseline_ref[...])):
+        rows, lane = rim_spot(last, number)
+        left = jnp.zeros((TH, LANES), jnp.float32)
+        right = jnp.zeros((TH, LANES), jnp.float32)
+        for distance in range(1, freq_count):
+            edge = in_refs[distance][rows, lane : lane + LANES]
+            partner = my_freq ^ distance
+            left = jnp.where(partner == my_freq - 1, edge, left)
+            right = jnp.where(partner == my_freq + 1, edge, right)
         span = slice(cells + number * TH, cells + (number + 1) * TH)
-        start = number * 2 * TW
         out_ref[span, 0:columns] = block
-        out_ref[span, columns : columns + TW] = right[:, start : start + TW]
-        out_ref[span, LANES - TW : LANES] = left[:, start + TW : start + 2 * TW]
+        out_ref[span, columns : columns + TW] = right[:, columns : columns + TW]
+        out_ref[span, LANES - TW : LANES] = left[:, LANES - TW :]
 
 
 def energies(cells, shard, where, weights, conduct, baseline, shards):
@@ -435,7 +455,7 @@
             operands = (where,) + tuple(sent[groups:])
         after = (sent[0],)
         if turn == 2:
-            after += tuple(parts[distance] for past in rounds[:2] for distance in past)
+            after += tuple(parts[-groups:])
     cells, shard = CELLS // pos_count, (TILE_DEV // freq_count + 1) * pos_count
     tiles = gather_tiles(freq_count, where, ids, conduct, baseline, parts)
     shards = [swap(tiles[d], "freq", d) if d else tiles[d] for d in range(freq_count)]

time: 96.5 us -> 89.9 us (0.932)
  waiting for transfers between devices: 35 us -> 27.7 us
  blocking collectives: 10.3 us -> 11.3 us
    ppermute x10, waiting for transfers between devices: 35 us -> 27.7 us  [swap(): lax.ppermute(array, axis, [(i, i ^ distance) for i in range(lax.axis_size...]
    all_gather x1, blocking collectives: 10.3 us -> 11.3 us  [body(): strips = lax.all_gather(strip, 'pos')]
  transfers between devices with their start and end apart: 10 -> 10, of which waited for: 5 -> 4; matrix products, arithmetic and copies ran while one was open for 0% -> 0% of each run, Pallas kernels for 16% -> 26%
where the time goes in v6:
time: 89.9 us; the launch traced here: 89.7 us
  Pallas kernels  39.9 us (44%)
  waiting for transfers between devices  27.7 us (31%)
  blocking collectives  11.3 us (13%)
  starting transfers between devices  9.87 us (11%)
    pallas_call x4, Pallas kernels, project(): pl.pallas_call(functools.partial(project_kernel, sizes, rounds, turn, len...  35 us
    ppermute x10, waiting for transfers between devices, swap(): lax.ppermute(array, axis, [(i, i ^ distance) for i in range(lax.axis_size...  27.7 us
    all_gather x1, blocking collectives, body(): strips = lax.all_gather(strip, 'pos')  11.3 us
    ppermute x10, starting transfers between devices, swap(): lax.ppermute(array, axis, [(i, i ^ distance) for i in range(lax.axis_size...  9.87 us
    pallas_call x1, Pallas kernels, gather_tiles(): pl.pallas_call(functools.partial(gather_kernel, pos_count, freq_count, ti...  2.13 us
  transfers between devices with their start and end apart: 10, of which 4 were waited for; matrix products, arithmetic and copies ran while one was open for 0% of the time, Pallas kernels for 26%

profile of v6, /device:TPU:17, one launch (start us, length us, event | category | flops | bytes accessed | tf_op | source)
XLA Modules:
  0.0 89.7 jit_solution(9638368106161376894)
XLA Ops:
  0.0 0.1 pad_add_fusion.refs_0_.where_ref
  0.1 0.0 copy-start
  0.1 0.7 copy-done
  0.8 11.7 %project_0.1 = (f32[4,64,256]{2,1,0:T(8,128)S(1)}, f32[4,64,256]{2,1,0:T(8,128)S(1)}, bf16[8,4,2,256,256]{4,3,2,1,0:T(8,128)(2,1)S(1)}, f32[4,2,32,8,128]{4,3,2,...) custom-call(s32[2]{0:T(128)S(1)} %pad_add_fusion.refs_0_.where_ref, ...), custom_call_target="tpu_custom_call" | custom-call | flops 2147483648 | bytes 2147483648 | tf_op jit(solution)/shard_map/project_0/pallas_call | solution.py:214
  12.5 2.2 %collective-permute-start = (f32[4,64,256]{2,1,0:T(8,128)S(1)}, f32[4,64,256]{2,1,0:T(8,128)S(1)}, u32[]{:S(2)}, u32[]{:S(2)}) collective-permute-start(f32[4,64,256]{2,1,0:T(8,128)S(1)} %get-tuple-element.25.refs_5_), channel_id=1, source_target_pairs={{0,24},{4,28},{8,16},{12,20},{16,8},{20,12},{24,0},{28,4},{1,25},{... | collective-permute-start | bytes 786440 | tf_op jit(solution)/shard_map/ppermute | solution.py:418
  14.7 1.0 %collective-permute-start.1 = (f32[4,64,256]{2,1,0:T(8,128)S(1)}, f32[4,64,256]{2,1,0:T(8,128)S(1)}, u32[]{:S(2)}, u32[]{:S(2)}) collective-permute-start(f32[4,64,256]{2,1,0:T(8,128)S(1)} %get-tuple-element.28), channel_id=1, source_target_pairs={{0,28},{4,24},{8,20},{12,16},{16,12},{20,8},{24,4},{28,0},{1,29},{... | collective-permute-start | bytes 786440 | tf_op jit(solution)/shard_map/ppermute | solution.py:418
  15.7 7.7 %project_1.1 = (f32[4,64,256]{2,1,0:T(8,128)S(1)}, f32[4,64,256]{2,1,0:T(8,128)S(1)}) custom-call(s32[2]{0:T(128)S(1)} %pad_add_fusion.refs_0_.where_ref, bf16[8,4,2,256,256]{4,3,2,1,0:T(8,128)(2,1)S(1)} %get-tuple-element.21.refs_1_, f32[4,2,32,8,128]{4,3,2,1,0:T(8,128)S(1)} %get-tuple-element.22.refs_2_, ...), custom_call_target="tpu_custom_call" | custom-call | flops 2147483648 | bytes 2147483648 | tf_op jit(solution)/shard_map/project_1/pallas_call | solution.py:214
  23.5 0.0 copy-start.1
  23.5 0.0 copy-start.2
  23.5 0.0 copy-start.3
  23.5 1.3 %collective-permute-start.5 = (f32[4,64,256]{2,1,0:T(8,128)S(1)}, f32[4,64,256]{2,1,0:T(8,128)S(1)}, u32[]{:S(2)}, u32[]{:S(2)}) collective-permute-start(f32[4,64,256]{2,1,0:T(8,128)S(1)} %get-tuple-element.26.refs_5_), channel_id=1, source_target_pairs={{0,16},{4,20},{8,24},{12,28},{16,0},{20,4},{24,8},{28,12},{1,17},{... | collective-permute-start | bytes 786440 | tf_op jit(solution)/shard_map/ppermute | solution.py:418
  24.8 7.7 %project_2.1 = (f32[4,64,256]{2,1,0:T(8,128)S(1)}, f32[4,64,256]{2,1,0:T(8,128)S(1)}) custom-call(s32[2]{0:T(128)S(1)} %pad_add_fusion.refs_0_.where_ref, bf16[8,4,2,256,256]{4,3,2,1,0:T(8,128)(2,1)S(1)} %get-tuple-element.21.refs_1_, f32[4,2,32,8,128]{4,3,2,1,0:T(8,128)S(1)} %get-tuple-element.22.refs_2_, ...), custom_call_target="tpu_custom_call" | custom-call | flops 2147483648 | bytes 2147483648 | tf_op jit(solution)/shard_map/project_2/pallas_call | solution.py:214
  32.5 0.0 copy-start.4
  32.5 1.0 %collective-permute-start.4 = (f32[4,64,256]{2,1,0:T(8,128)S(1)}, f32[4,64,256]{2,1,0:T(8,128)S(1)}, u32[]{:S(2)}, u32[]{:S(2)}) collective-permute-start(f32[4,64,256]{2,1,0:T(8,128)S(1)} %get-tuple-element.32), channel_id=1, source_target_pairs={{0,12},{4,8},{8,4},{12,0},{16,28},{20,24},{24,20},{28,16},{1,13},{... | collective-permute-start | bytes 786440 | tf_op jit(solution)/shard_map/ppermute | solution.py:418
  33.5 0.8 collective-permute-start.6
  34.3 0.0 collective-permute-done.refs_6_
  34.3 0.3 collective-permute-start.3
  34.6 0.0 collective-permute-done.1.refs_7_
  34.6 7.9 %project_3.1 = (f32[4,64,256]{2,1,0:T(8,128)S(1)}, f32[4,64,256]{2,1,0:T(8,128)S(1)}) custom-call(s32[2]{0:T(128)S(1)} %pad_add_fusion.refs_0_.where_ref, bf16[8,4,2,256,256]{4,3,2,1,0:T(8,128)(2,1)S(1)} %get-tuple-element.21.refs_1_, f32[4,2,32,8,128]{4,3,2,1,0:T(8,128)S(1)} %get-tuple-element.22.refs_2_, ...), custom_call_target="tpu_custom_call" | custom-call | flops 2147483648 | bytes 2147483648 | tf_op jit(solution)/shard_map/project_3/pallas_call | solution.py:214
  42.5 0.5 collective-permute-start.2
  43.1 0.0 copy-done.1
  43.1 0.1 reshape.10.ids_ref
  43.1 0.0 collective-permute-done.4.refs_3_
  43.1 0.0 collective-permute-done.6.refs_5_
  43.1 2.4 %collective-permute-done.3.refs_2_ = f32[4,64,256]{2,1,0:T(8,128)S(1)} collective-permute-done((f32[4,64,256]{2,1,0:T(8,128)S(1)}, f32[4,64,256]{2,1,0:T(8,128)S(1)}, u32[]{:S(2)}, u32[]{:S(2)}) %collective-permute-start.3) | collective-permute-done | bytes 262176 | tf_op jit(solution)/shard_map/ppermute | solution.py:418
  45.5 0.0 collective-permute-done.5.refs_4_
  45.5 0.0 collective-permute-done.2.refs_1_
  45.5 0.0 copy-done.2
  45.5 0.0 copy-done.3
  45.5 2.1 %tiles.1 = (f32[288,256]{1,0:T(8,128)S(1)}, f32[296,256]{1,0:T(8,128)S(1)}, f32[296,256]{1,0:T(8,128)S(1)}, f32[296,256]{1,0:T(8,128)S(1)}) custom-call(s32[2]{0:T(128)S(1)} %pad_add_fusion.refs_0_.where_ref, s32[8,64]{1,0:T(8,128)S(1)} %reshape.10.ids_ref, f32[2,4,64]{2,1,0:T(4,128)S(1)} %copy-done.2, f32[4,64]{1,0:T(4,128)S(1)} %copy-done.3, ...), custom_call_target="tpu_custom_call" | custom-call | tf_op jit(solution)/shard_map/tiles/pallas_call | solution.py:286
  47.7 1.4 %collective-permute-start.7 = (f32[296,256]{1,0:T(8,128)S(1)}, f32[296,256]{1,0:T(8,128)S(1)}, u32[]{:S(2)}, u32[]{:S(2)}) collective-permute-start(f32[296,256]{1,0:T(8,128)S(1)} %get-tuple-element.34), channel_id=1, source_target_pairs={{0,1},{1,0},{2,3},{3,2},{4,5},{5,4},{6,7},{7,6},{8,9},{9,8},{10,11... | collective-permute-start | bytes 909320 | tf_op jit(solution)/shard_map/ppermute | solution.py:418
  49.0 0.1 collective-permute-start.8
  49.1 1.3 %collective-permute-start.9 = (f32[296,256]{1,0:T(8,128)S(1)}, f32[296,256]{1,0:T(8,128)S(1)}, u32[]{:S(2)}, u32[]{:S(2)}) collective-permute-start(f32[296,256]{1,0:T(8,128)S(1)} %get-tuple-element.36), channel_id=1, source_target_pairs={{0,3},{1,2},{2,1},{3,0},{4,7},{5,6},{6,5},{7,4},{8,11},{9,10},{10,... | collective-permute-start | bytes 909320 | tf_op jit(solution)/shard_map/ppermute | solution.py:418
  50.4 9.3 %collective-permute-done.7.refs_1_ = f32[296,256]{1,0:T(8,128)S(1)} collective-permute-done((f32[296,256]{1,0:T(8,128)S(1)}, f32[296,256]{1,0:T(8,128)S(1)}, u32[]{:S(2)}, u32[]{:S(2)}) %collective-permute-start.7) | collective-permute-done | bytes 303136 | tf_op jit(solution)/shard_map/ppermute | solution.py:418
  59.7 2.0 %collective-permute-done.8.refs_2_ = f32[296,256]{1,0:T(8,128)S(1)} collective-permute-done((f32[296,256]{1,0:T(8,128)S(1)}, f32[296,256]{1,0:T(8,128)S(1)}, u32[]{:S(2)}, u32[]{:S(2)}) %collective-permute-start.8) | collective-permute-done | bytes 303136 | tf_op jit(solution)/shard_map/ppermute | solution.py:418
  61.6 14.0 %collective-permute-done.9.refs_3_ = f32[296,256]{1,0:T(8,128)S(1)} collective-permute-done((f32[296,256]{1,0:T(8,128)S(1)}, f32[296,256]{1,0:T(8,128)S(1)}, u32[]{:S(2)}, u32[]{:S(2)}) %collective-permute-start.9) | collective-permute-done | bytes 303136 | tf_op jit(solution)/shard_map/ppermute | solution.py:418
  75.7 0.0 copy-done.4
  75.7 0.9 %energies.1 = f32[16,128]{1,0:T(8,128)S(1)} custom-call(s32[2]{0:T(128)S(1)} %pad_add_fusion.refs_0_.where_ref, f32[1,256]{1,0:T(1,128)S(1)} %bitcast.6, f32[2,4,64]{2,1,0:T(4,128)S(1)} %copy-done.2, f32[4,64]{1,0:T(4,128)S(1)} %copy-done.3, f32[288,256]{1,0:T(8,128)S(1)} %get-tuple-element.33.refs_0_, f32[296,256]{1,0:T(8,128)S(1)} %collective-permute-done.7.refs_1_, ...), custom_call_target="tpu_custom_call" | custom-call | tf_op jit(solution)/shard_map/energies/pallas_call | solution.py:335
  76.6 11.3 %all-gather = f32[128,128]{1,0:T(8,128)S(1)} all-gather(f32[16,128]{1,0:T(8,128)S(1)} %energies.1), channel_id=2, replica_groups=mesh['pos'=8,'freq'=4] {'pos'}, dimensions={0}, use_global_device_ids=true | all-gather | bytes 73728 | tf_op jit(solution)/shard_map/all_gather | solution.py:463
  87.9 1.8 %diffuse.1 = f32[4,64]{1,0:T(4,128)} custom-call(s32[2]{0:T(128)S(1)} %pad_add_fusion.refs_0_.where_ref, f32[8,16,128]{2,1,0:T(8,128)S(1)} %bitcast.5), custom_call_target="tpu_custom_call" | custom-call | tf_op jit(solution)/shard_map/diffuse/pallas_call | solution.py:406
Async XLA Ops:
  0.1 0.7 copy-start
  12.5 21.9 %collective-permute-start = (f32[4,64,256]{2,1,0:T(8,128)S(1)}, f32[4,64,256]{2,1,0:T(8,128)S(1)}, u32[]{:S(2)}, u32[]{:S(2)}) collective-permute-start(f32[4,64,256]{2,1,0:T(8,128)S(1)} %get-tuple-element.25.refs_5_), channel_id=1, source_target_pairs={{0,24},{4,28},{8,16},{12,20},{16,8},{20,12},{24,0},{28,4},{1,25},{... | collective-permute-start | bytes 786440 | tf_op jit(solution)/shard_map/ppermute | solution.py:418
  14.7 19.9 %collective-permute-start.1 = (f32[4,64,256]{2,1,0:T(8,128)S(1)}, f32[4,64,256]{2,1,0:T(8,128)S(1)}, u32[]{:S(2)}, u32[]{:S(2)}) collective-permute-start(f32[4,64,256]{2,1,0:T(8,128)S(1)} %get-tuple-element.28), channel_id=1, source_target_pairs={{0,28},{4,24},{8,20},{12,16},{16,12},{20,8},{24,4},{28,0},{1,29},{... | collective-permute-start | bytes 786440 | tf_op jit(solution)/shard_map/ppermute | solution.py:418
  23.5 19.6 %copy-start.1 = (s32[16,32]{1,0:T(8,128)S(1)}, s32[16,32]{1,0:T(8,128)}, u32[]{:S(2)}) copy-start(s32[16,32]{1,0:T(8,128)} %refs_1_.1) | copy-start | bytes 6148
  23.5 22.0 %copy-start.2 = (f32[2,4,64]{2,1,0:T(4,128)S(1)}, f32[2,4,64]{2,1,0:T(4,128)}, u32[]{:S(2)}) copy-start(f32[2,4,64]{2,1,0:T(4,128)} %conduct_ref.3) | copy-start | bytes 6148
  23.5 22.0 %copy-start.3 = (f32[4,64]{1,0:T(4,128)S(1)}, f32[4,64]{1,0:T(4,128)}, u32[]{:S(2)}) copy-start(f32[4,64]{1,0:T(4,128)} %baseline_ref.3) | copy-start | bytes 3076
  23.5 22.0 %collective-permute-start.5 = (f32[4,64,256]{2,1,0:T(8,128)S(1)}, f32[4,64,256]{2,1,0:T(8,128)S(1)}, u32[]{:S(2)}, u32[]{:S(2)}) collective-permute-start(f32[4,64,256]{2,1,0:T(8,128)S(1)} %get-tuple-element.26.refs_5_), channel_id=1, source_target_pairs={{0,16},{4,20},{8,24},{12,28},{16,0},{20,4},{24,8},{28,12},{1,17},{... | collective-permute-start | bytes 786440 | tf_op jit(solution)/shard_map/ppermute | solution.py:418
  32.5 43.1 %copy-start.4 = (f32[256]{0:T(256)S(1)}, f32[256]{0:T(256)}, u32[]{:S(2)}) copy-start(f32[256]{0:T(256)} %param.7) | copy-start | bytes 3076
  32.5 10.6 %collective-permute-start.4 = (f32[4,64,256]{2,1,0:T(8,128)S(1)}, f32[4,64,256]{2,1,0:T(8,128)S(1)}, u32[]{:S(2)}, u32[]{:S(2)}) collective-permute-start(f32[4,64,256]{2,1,0:T(8,128)S(1)} %get-tuple-element.32), channel_id=1, source_target_pairs={{0,12},{4,8},{8,4},{12,0},{16,28},{20,24},{24,20},{28,16},{1,13},{... | collective-permute-start | bytes 786440 | tf_op jit(solution)/shard_map/ppermute | solution.py:418
  33.5 9.6 %collective-permute-start.6 = (f32[4,64,256]{2,1,0:T(8,128)S(1)}, f32[4,64,256]{2,1,0:T(8,128)S(1)}, u32[]{:S(2)}, u32[]{:S(2)}) collective-permute-start(f32[4,64,256]{2,1,0:T(8,128)S(1)} %get-tuple-element.27.refs_5_), channel_id=1, source_target_pairs={{0,20},{4,16},{8,28},{12,24},{16,4},{20,0},{24,12},{28,8},{1,21},{... | collective-permute-start | bytes 786440 | tf_op jit(solution)/shard_map/ppermute | solution.py:418
  34.3 11.2 %collective-permute-start.3 = (f32[4,64,256]{2,1,0:T(8,128)S(1)}, f32[4,64,256]{2,1,0:T(8,128)S(1)}, u32[]{:S(2)}, u32[]{:S(2)}) collective-permute-start(f32[4,64,256]{2,1,0:T(8,128)S(1)} %get-tuple-element.31), channel_id=1, source_target_pairs={{0,8},{4,12},{8,0},{12,4},{16,24},{20,28},{24,16},{28,20},{1,9},{5... | collective-permute-start | bytes 786440 | tf_op jit(solution)/shard_map/ppermute | solution.py:418
  42.5 3.0 %collective-permute-start.2 = (f32[4,64,256]{2,1,0:T(8,128)S(1)}, f32[4,64,256]{2,1,0:T(8,128)S(1)}, u32[]{:S(2)}, u32[]{:S(2)}) collective-permute-start(f32[4,64,256]{2,1,0:T(8,128)S(1)} %get-tuple-element.30), channel_id=1, source_target_pairs={{0,4},{4,0},{8,12},{12,8},{16,20},{20,16},{24,28},{28,24},{1,5},{5... | collective-permute-start | bytes 786440 | tf_op jit(solution)/shard_map/ppermute | solution.py:418
  47.7 12.0 %collective-permute-start.7 = (f32[296,256]{1,0:T(8,128)S(1)}, f32[296,256]{1,0:T(8,128)S(1)}, u32[]{:S(2)}, u32[]{:S(2)}) collective-permute-start(f32[296,256]{1,0:T(8,128)S(1)} %get-tuple-element.34), channel_id=1, source_target_pairs={{0,1},{1,0},{2,3},{3,2},{4,5},{5,4},{6,7},{7,6},{8,9},{9,8},{10,11... | collective-permute-start | bytes 909320 | tf_op jit(solution)/shard_map/ppermute | solution.py:418
  49.0 12.6 %collective-permute-start.8 = (f32[296,256]{1,0:T(8,128)S(1)}, f32[296,256]{1,0:T(8,128)S(1)}, u32[]{:S(2)}, u32[]{:S(2)}) collective-permute-start(f32[296,256]{1,0:T(8,128)S(1)} %get-tuple-element.35), channel_id=1, source_target_pairs={{0,2},{1,3},{2,0},{3,1},{4,6},{5,7},{6,4},{7,5},{8,10},{9,11},{10,... | collective-permute-start | bytes 909320 | tf_op jit(solution)/shard_map/ppermute | solution.py:418
  49.1 26.6 %collective-permute-start.9 = (f32[296,256]{1,0:T(8,128)S(1)}, f32[296,256]{1,0:T(8,128)S(1)}, u32[]{:S(2)}, u32[]{:S(2)}) collective-permute-start(f32[296,256]{1,0:T(8,128)S(1)} %get-tuple-element.36), channel_id=1, source_target_pairs={{0,3},{1,2},{2,1},{3,0},{4,7},{5,6},{6,5},{7,4},{8,11},{9,10},{10,... | collective-permute-start | bytes 909320 | tf_op jit(solution)/shard_map/ppermute | solution.py:418

commit v7 on v6

--- a/solution.py
+++ b/solution.py
@@ -66,24 +66,20 @@
     per_dest = TW // groups
     blocks = elements // ELEM_BLOCK
     steps = pos_local * blocks
-    where_ref, refs = refs[0], refs[1:]
     if first:
         (foot_ref, basis_ref), refs = refs[:2], refs[2:]
         out_refs, refs = refs[:groups], refs[groups:]
-        kept_ref, depth_ref, lateral_ref, element_ref, green_even, green_odd, total_ref, held_ref, sems, kept_sems = refs
+        held_ref, depth_ref, lateral_ref, element_ref, green_even, green_odd, total_ref, sems = refs
     else:
         held_ref, depth_ref, lateral_ref, element_ref = refs[:4]
         out_refs, refs = refs[4 + waits : 4 + waits + groups], refs[4 + waits + groups :]
         green_even, green_odd, total_ref = refs
-    my_pos, my_freq = where_ref[0], where_ref[1]
+    my_pos, my_freq = lax.axis_index("pos"), lax.axis_index("freq")
 
     def fetch(step):
         offset, block = step // blocks, step % blocks
         spot = pl.ds(block * ELEM_BLOCK, ELEM_BLOCK)
         return pltpu.make_async_copy(basis_ref.at[offset, :, :, spot, :], held_ref.at[step], sems.at[step])
-
-    def keep(step):
-        return pltpu.make_async_copy(held_ref.at[step], kept_ref.at[step], kept_sems.at[step])
 
     if first:
         for step in range(AHEAD):
@@ -151,7 +147,6 @@
         if use is not None:
             if first:
                 fetch(use).wait()
-                keep(use).start()
                 if isinstance(use, int):
                     if use + AHEAD < steps:
                         fetch(use + AHEAD).start()
@@ -172,9 +167,6 @@
     run(steps - 1, green_odd, steps - 2, green_even)
     run(None, None, steps - 1, green_odd)
 
-    if first:
-        for step in range(steps):
-            keep(step).wait()
     for offset in range(pos_local):
         for group in range(groups):
             for cell in range(per_dest):
@@ -189,7 +181,7 @@
     pos_count, freqs, positions, elements, pos_local, freq_local, foot = sizes
     groups = pos_count // TH
     per_dest = TW // groups
-    basis = operands[2] if first else operands[1]
+    basis = operands[1] if first else operands[0]
     rank = basis.shape[-1]
     rows = foot * TW
     steps = pos_local * elements // ELEM_BLOCK
@@ -201,7 +193,7 @@
     vmem, smem = pl.BlockSpec(memory_space=pltpu.VMEM), pl.BlockSpec(memory_space=pltpu.SMEM)
     out_shape = [shape(per_dest, pos_local * foot, rank)] * groups
     if first:
-        in_specs = [smem, smem, pl.BlockSpec(memory_space=pl.ANY)]
+        in_specs = [smem, pl.BlockSpec(memory_space=pl.ANY)]
         out_shape += [
             shape(steps, freq_local, 2, ELEM_BLOCK, rank, dtype=jnp.bfloat16),
             shape(len(rounds), pos_local, foot, TW, LANES),
@@ -209,24 +201,15 @@
             shape(pos_local, elements // LANES, TW, LANES),
         ]
     else:
-        in_specs = [smem] + [vmem] * 4 + [pl.BlockSpec(memory_space=pl.ANY)] * len(after)
+        in_specs = [vmem] * 4 + [pl.BlockSpec(memory_space=pl.ANY)] * len(after)
     green = pltpu.VMEM((rows, freq_local * 2 * ELEM_BLOCK), jnp.bfloat16)
     return pl.pallas_call(
         functools.partial(project_kernel, sizes, rounds, turn, len(after)),
         in_specs=in_specs,
-        out_specs=[vmem] * groups
-        + ([pl.BlockSpec(memory_space=pl.ANY)] + [vmem] * 3 if first else []),
+        out_specs=[vmem] * len(out_shape),
         out_shape=out_shape,
         scratch_shapes=[green, green, pltpu.VMEM((pos_local, rank // LANES, rows, LANES), jnp.float32)]
-        + (
-            [
-                pltpu.VMEM((steps, freq_local, 2, ELEM_BLOCK, rank), jnp.bfloat16),
-                pltpu.SemaphoreType.DMA((steps,)),
-                pltpu.SemaphoreType.DMA((steps,)),
-            ]
-            if first
-            else []
-        ),
+        + ([pltpu.SemaphoreType.DMA((steps,))] if first else []),
         compiler_params=pltpu.CompilerParams(vmem_limit_bytes=VMEM_LIMIT_FIRST if first else VMEM_LIMIT),
         cost_estimate=pl.CostEstimate(flops=flops, bytes_accessed=flops, transcendentals=0),
         name=f"project_{turn}",
@@ -243,13 +226,13 @@
     return slice(start, start + TH), number // 2 * LANES
 
 
-def gather_kernel(pos_count, freq_count, tile_rows, shard, where_ref, ids_ref, conduct_ref, baseline_ref, *refs):
+def gather_kernel(pos_count, freq_count, tile_rows, shard, ids_ref, conduct_ref, baseline_ref, *refs):
     in_refs, out_refs = refs[:pos_count], refs[pos_count:]
     cells, entries, rank = in_refs[0].shape
     columns = baseline_ref.shape[1]
     tile_cols = shard // tile_rows
     groups = pos_count // TH
-    my_pos, my_freq = where_ref[0], where_ref[1]
+    my_pos, my_freq = lax.axis_index("pos"), lax.axis_index("freq")
     left = (lax.rem(my_pos, groups) * 2 >= groups).astype(jnp.int32)
     row = lax.broadcasted_iota(jnp.int32, (shard, entries), 0)
     wanted = (row % tile_rows) * TILE_DEV + row // tile_rows - left
@@ -278,26 +261,26 @@
             ref[rows, lane + LANES - TW : lane + LANES] = block[:, columns - TW :]
 
 
-def gather_tiles(freq_count, where, ids, conduct, baseline, parts):
+def gather_tiles(freq_count, ids, conduct, baseline, parts):
     pos_count = len(parts)
     cells, entries, rank = parts[0].shape
     tile_rows = pos_count
     shard = (TILE_DEV // freq_count + 1) * tile_rows
     return pl.pallas_call(
         functools.partial(gather_kernel, pos_count, freq_count, tile_rows, shard),
-        in_specs=[pl.BlockSpec(memory_space=pltpu.SMEM)] + [pl.BlockSpec(memory_space=pltpu.VMEM)] * (3 + pos_count),
+        in_specs=[pl.BlockSpec(memory_space=pltpu.VMEM)] * (3 + pos_count),
         out_specs=[pl.BlockSpec(memory_space=pltpu.VMEM)] * freq_count,
         out_shape=[jax.ShapeDtypeStruct((cells * shard, rank), jnp.float32)]
         + [jax.ShapeDtypeStruct((cells * shard + RIM_ROWS, rank), jnp.float32)] * (freq_count - 1),
         compiler_params=pltpu.CompilerParams(vmem_limit_bytes=VMEM_LIMIT),
         name="tiles",
-    )(where, ids, conduct, baseline, *parts)
-
-
-def energy_kernel(cells, shard, freq_count, where_ref, weights_ref, conduct_ref, baseline_ref, *refs):
+    )(ids, conduct, baseline, *parts)
+
+
+def energy_kernel(cells, shard, freq_count, weights_ref, conduct_ref, baseline_ref, *refs):
     in_refs, out_ref = refs[:freq_count], refs[freq_count]
     rank = in_refs[0].shape[1]
-    my_freq = where_ref[1]
+    my_freq = lax.axis_index("freq")
     weights = jnp.broadcast_to(weights_ref[...], (8, rank))
     for cell in range(cells):
         span = slice(cell * shard, (cell + 1) * shard)
@@ -329,25 +312,25 @@
         out_ref[span, LANES - TW : LANES] = left[:, LANES - TW :]
 
 
-def energies(cells, shard, where, weights, conduct, baseline, shards):
+def energies(cells, shard, weights, conduct, baseline, shards):
     rows = cells + 3 * TH
     width = -(-max(shard, baseline.shape[1] + 2 * TW) // LANES) * LANES
     return pl.pallas_call(
         functools.partial(energy_kernel, cells, shard, len(shards)),
-        in_specs=[pl.BlockSpec(memory_space=pltpu.SMEM)] + [pl.BlockSpec(memory_space=pltpu.VMEM)] * (3 + len(shards)),
+        in_specs=[pl.BlockSpec(memory_space=pltpu.VMEM)] * (3 + len(shards)),
         out_specs=pl.BlockSpec(memory_space=pltpu.VMEM),
         out_shape=jax.ShapeDtypeStruct((rows, width), jnp.float32),
         compiler_params=pltpu.CompilerParams(vmem_limit_bytes=VMEM_LIMIT),
         name="energies",
-    )(where, weights, conduct, baseline, *shards)
-
-
-def diffuse_kernel(cells, shard, where_ref, strips_ref, out_ref, field_ref):
+    )(weights, conduct, baseline, *shards)
+
+
+def diffuse_kernel(cells, shard, strips_ref, out_ref, field_ref):
     pos_count, _, width = strips_ref.shape
     tile_rows = pos_count
     tile_cols = shard // tile_rows
     groups = pos_count // TH
-    my_pos = where_ref[0]
+    my_pos = lax.axis_index("pos")
     tile_row = lax.broadcasted_iota(jnp.int32, (tile_rows, width), 0)
     spot = lax.broadcasted_iota(jnp.int32, (tile_rows, width), 1)
     here = (spot % tile_rows == tile_row) & (spot < shard)
@@ -402,16 +385,16 @@
         out_ref[pl.ds(row, 1), :] = field_ref[pl.ds(my_pos, 1), 0 : out_ref.shape[1]]
 
 
-def diffuse(cells, shard, where, strips, columns):
+def diffuse(cells, shard, strips, columns):
     return pl.pallas_call(
         functools.partial(diffuse_kernel, cells, shard),
-        in_specs=[pl.BlockSpec(memory_space=pltpu.SMEM), pl.BlockSpec(memory_space=pltpu.VMEM)],
+        in_specs=[pl.BlockSpec(memory_space=pltpu.VMEM)],
         out_specs=pl.BlockSpec(memory_space=pltpu.VMEM),
         out_shape=jax.ShapeDtypeStruct((TH, columns), jnp.float32),
         scratch_shapes=[pltpu.VMEM((strips.shape[0], LANES), jnp.float32)],
         compiler_params=pltpu.CompilerParams(vmem_limit_bytes=VMEM_LIMIT),
         name="diffuse",
-    )(where, strips)
+    )(strips)
 
 
 def swap(array, axis, distance):
@@ -434,7 +417,6 @@
         freq_local,
         foot,
     )
-    where = jnp.stack([lax.axis_index("pos"), lax.axis_index("freq")]).astype(jnp.int32)
     ids = footprint.reshape(pos_count, pos_local * foot)
     split = basis.reshape(pos_local, freq_local, 2, elements, rank)
     groups = pos_count // TH
@@ -446,22 +428,22 @@
         tuple(range(2 * groups + half, 3 * groups)) + tuple(range(groups + half, 2 * groups)),
         tuple(range(groups)),
     )
-    operands, after = (where, footprint, split), ()
+    operands, after = (footprint, split), ()
     for turn, distances in enumerate(rounds):
         sent = project(sizes, rounds, turn, operands, after)
         for number, distance in enumerate(distances):
             parts[distance] = swap(sent[number], "pos", distance) if distance else sent[number]
         if turn == 0:
-            operands = (where,) + tuple(sent[groups:])
+            operands = tuple(sent[groups:])
         after = (sent[0],)
         if turn == 2:
             after += tuple(parts[-groups:])
     cells, shard = CELLS // pos_count, (TILE_DEV // freq_count + 1) * pos_count
-    tiles = gather_tiles(freq_count, where, ids, conduct, baseline, parts)
+    tiles = gather_tiles(freq_count, ids, conduct, baseline, parts)
     shards = [swap(tiles[d], "freq", d) if d else tiles[d] for d in range(freq_count)]
-    strip = energies(cells, shard, where, weights.reshape(1, rank), conduct, baseline, shards)
+    strip = energies(cells, shard, weights.reshape(1, rank), conduct, baseline, shards)
     strips = lax.all_gather(strip, "pos")
-    return diffuse(cells, shard, where, strips, columns)
+    return diffuse(cells, shard, strips, columns)
 
 
 def solution(mesh):

time: 89.9 us -> 86.7 us (0.964)
  Pallas kernels: 39.9 us -> 36.3 us
    pallas_call x4, Pallas kernels: 35 us -> 33.1 us  [project(): pl.pallas_call(functools.partial(project_kernel, sizes, rounds, turn, len...]
where the time goes in v7:
time: 86.7 us; the launch traced here: 86.5 us
  Pallas kernels  36.3 us (42%)
  waiting for transfers between devices  28.1 us (32%)
  blocking collectives  11.3 us (13%)
  starting transfers between devices  9.87 us (11%)
    pallas_call x4, Pallas kernels, project(): pl.pallas_call(functools.partial(project_kernel, sizes, rounds, turn, len...  33.1 us
    ppermute x10, waiting for transfers between devices, swap(): lax.ppermute(array, axis, [(i, i ^ distance) for i in range(lax.axis_size...  28.1 us
    all_gather x1, blocking collectives, body(): strips = lax.all_gather(strip, 'pos')  11.3 us
    ppermute x10, starting transfers between devices, swap(): lax.ppermute(array, axis, [(i, i ^ distance) for i in range(lax.axis_size...  9.87 us
  transfers between devices with their start and end apart: 10, of which 4 were waited for; matrix products, arithmetic and copies ran while one was open for 0% of the time, Pallas kernels for 26%

profile of v7, /device:TPU:17, one launch (start us, length us, event | category | flops | bytes accessed | tf_op | source)
XLA Modules:
  0.0 86.5 jit_solution(5585383509531298581)
XLA Ops:
  0.0 0.0 copy-start
  0.0 0.7 copy-done
  0.7 11.0 %project_0.1 = (f32[4,64,256]{2,1,0:T(8,128)S(1)}, f32[4,64,256]{2,1,0:T(8,128)S(1)}, bf16[8,4,2,256,256]{4,3,2,1,0:T(8,128)(2,1)S(1)}, f32[4,2,32,8,128]{4,3,2,...) custom-call(s32[16,32]{1,0:T(8,128)S(1)} %copy-done, bf16[2,4,2,1024,256]{4,3,2,1,0:T(8,128)(2,1)} %bitcast.5), custom_call_target="tpu_custom_call" | custom-call | flops 2147483648 | bytes 2147483648 | tf_op jit(solution)/shard_map/project_0/pallas_call | solution.py:206
  11.7 2.2 %collective-permute-start = (f32[4,64,256]{2,1,0:T(8,128)S(1)}, f32[4,64,256]{2,1,0:T(8,128)S(1)}, u32[]{:S(2)}, u32[]{:S(2)}) collective-permute-start(f32[4,64,256]{2,1,0:T(8,128)S(1)} %get-tuple-element.25.refs_4_), channel_id=1, source_target_pairs={{0,24},{4,28},{8,16},{12,20},{16,8},{20,12},{24,0},{28,4},{1,25},{... | collective-permute-start | bytes 786440 | tf_op jit(solution)/shard_map/ppermute | solution.py:401
  14.0 1.0 %collective-permute-start.1 = (f32[4,64,256]{2,1,0:T(8,128)S(1)}, f32[4,64,256]{2,1,0:T(8,128)S(1)}, u32[]{:S(2)}, u32[]{:S(2)}) collective-permute-start(f32[4,64,256]{2,1,0:T(8,128)S(1)} %get-tuple-element.28), channel_id=1, source_target_pairs={{0,28},{4,24},{8,20},{12,16},{16,12},{20,8},{24,4},{28,0},{1,29},{... | collective-permute-start | bytes 786440 | tf_op jit(solution)/shard_map/ppermute | solution.py:401
  15.0 7.3 %project_1.1 = (f32[4,64,256]{2,1,0:T(8,128)S(1)}, f32[4,64,256]{2,1,0:T(8,128)S(1)}) custom-call(bf16[8,4,2,256,256]{4,3,2,1,0:T(8,128)(2,1)S(1)} %get-tuple-element.21.refs_0_, f32[4,2,32,8,128]{4,3,2,1,0:T(8,128)S(1)} %get-tuple-element.22.refs_1_, f32[4,2,32,8,128]{4,3,2,1,0:T(8,128)S(1)} %get-tuple-element.23.refs_2_, ...), custom_call_target="tpu_custom_call" | custom-call | flops 2147483648 | bytes 2147483648 | tf_op jit(solution)/shard_map/project_1/pallas_call | solution.py:206
  22.3 0.0 copy-start.1
  22.3 0.0 copy-start.2
  22.3 0.0 copy-start.3
  22.4 1.3 %collective-permute-start.5 = (f32[4,64,256]{2,1,0:T(8,128)S(1)}, f32[4,64,256]{2,1,0:T(8,128)S(1)}, u32[]{:S(2)}, u32[]{:S(2)}) collective-permute-start(f32[4,64,256]{2,1,0:T(8,128)S(1)} %get-tuple-element.26.refs_4_), channel_id=1, source_target_pairs={{0,16},{4,20},{8,24},{12,28},{16,0},{20,4},{24,8},{28,12},{1,17},{... | collective-permute-start | bytes 786440 | tf_op jit(solution)/shard_map/ppermute | solution.py:401
  23.7 7.3 %project_2.1 = (f32[4,64,256]{2,1,0:T(8,128)S(1)}, f32[4,64,256]{2,1,0:T(8,128)S(1)}) custom-call(bf16[8,4,2,256,256]{4,3,2,1,0:T(8,128)(2,1)S(1)} %get-tuple-element.21.refs_0_, f32[4,2,32,8,128]{4,3,2,1,0:T(8,128)S(1)} %get-tuple-element.22.refs_1_, f32[4,2,32,8,128]{4,3,2,1,0:T(8,128)S(1)} %get-tuple-element.23.refs_2_, ...), custom_call_target="tpu_custom_call" | custom-call | flops 2147483648 | bytes 2147483648 | tf_op jit(solution)/shard_map/project_2/pallas_call | solution.py:206
  31.0 0.0 copy-start.4
  31.0 1.0 %collective-permute-start.4 = (f32[4,64,256]{2,1,0:T(8,128)S(1)}, f32[4,64,256]{2,1,0:T(8,128)S(1)}, u32[]{:S(2)}, u32[]{:S(2)}) collective-permute-start(f32[4,64,256]{2,1,0:T(8,128)S(1)} %get-tuple-element.32), channel_id=1, source_target_pairs={{0,12},{4,8},{8,4},{12,0},{16,28},{20,24},{24,20},{28,16},{1,13},{... | collective-permute-start | bytes 786440 | tf_op jit(solution)/shard_map/ppermute | solution.py:401
  32.0 0.8 collective-permute-start.6
  32.8 0.0 collective-permute-done.refs_5_.refs_6_
  32.8 0.3 collective-permute-start.3
  33.0 0.0 collective-permute-done.1.refs_6_.refs_7_
  33.0 7.5 %project_3.1 = (f32[4,64,256]{2,1,0:T(8,128)S(1)}, f32[4,64,256]{2,1,0:T(8,128)S(1)}) custom-call(bf16[8,4,2,256,256]{4,3,2,1,0:T(8,128)(2,1)S(1)} %get-tuple-element.21.refs_0_, f32[4,2,32,8,128]{4,3,2,1,0:T(8,128)S(1)} %get-tuple-element.22.refs_1_, f32[4,2,32,8,128]{4,3,2,1,0:T(8,128)S(1)} %get-tuple-element.23.refs_2_, ...), custom_call_target="tpu_custom_call" | custom-call | flops 2147483648 | bytes 2147483648 | tf_op jit(solution)/shard_map/project_3/pallas_call | solution.py:206
  40.5 0.5 collective-permute-start.2
  41.1 0.0 copy-done.1
  41.1 0.1 reshape.10.ids_ref
  41.2 0.0 collective-permute-done.4.refs_3_
  41.2 0.0 collective-permute-done.6.refs_5_
  41.2 0.0 collective-permute-done.5.refs_4_
  41.2 2.8 %collective-permute-done.3.refs_2_ = f32[4,64,256]{2,1,0:T(8,128)S(1)} collective-permute-done((f32[4,64,256]{2,1,0:T(8,128)S(1)}, f32[4,64,256]{2,1,0:T(8,128)S(1)}, u32[]{:S(2)}, u32[]{:S(2)}) %collective-permute-start.3) | collective-permute-done | bytes 262176 | tf_op jit(solution)/shard_map/ppermute | solution.py:401
  44.0 0.0 collective-permute-done.2.refs_1_
  44.0 0.0 copy-done.2
  44.0 0.0 copy-done.3
  44.0 1.6 %tiles.1 = (f32[288,256]{1,0:T(8,128)S(1)}, f32[296,256]{1,0:T(8,128)S(1)}, f32[296,256]{1,0:T(8,128)S(1)}, f32[296,256]{1,0:T(8,128)S(1)}) custom-call(s32[8,64]{1,0:T(8,128)S(1)} %reshape.10.ids_ref, f32[2,4,64]{2,1,0:T(4,128)S(1)} %copy-done.2, f32[4,64]{1,0:T(4,128)S(1)} %copy-done.3, f32[4,64,256]{2,1,0:T(8,128)S(1)} %get-tuple-element.29.refs_0_, ...), custom_call_target="tpu_custom_call" | custom-call | tf_op jit(solution)/shard_map/tiles/pallas_call | solution.py:269
  45.6 1.4 %collective-permute-start.7 = (f32[296,256]{1,0:T(8,128)S(1)}, f32[296,256]{1,0:T(8,128)S(1)}, u32[]{:S(2)}, u32[]{:S(2)}) collective-permute-start(f32[296,256]{1,0:T(8,128)S(1)} %get-tuple-element.34), channel_id=1, source_target_pairs={{0,1},{1,0},{2,3},{3,2},{4,5},{5,4},{6,7},{7,6},{8,9},{9,8},{10,11... | collective-permute-start | bytes 909320 | tf_op jit(solution)/shard_map/ppermute | solution.py:401
  46.9 0.1 collective-permute-start.8
  47.0 1.3 %collective-permute-start.9 = (f32[296,256]{1,0:T(8,128)S(1)}, f32[296,256]{1,0:T(8,128)S(1)}, u32[]{:S(2)}, u32[]{:S(2)}) collective-permute-start(f32[296,256]{1,0:T(8,128)S(1)} %get-tuple-element.36), channel_id=1, source_target_pairs={{0,3},{1,2},{2,1},{3,0},{4,7},{5,6},{6,5},{7,4},{8,11},{9,10},{10,... | collective-permute-start | bytes 909320 | tf_op jit(solution)/shard_map/ppermute | solution.py:401
  48.3 9.3 %collective-permute-done.7.refs_1_ = f32[296,256]{1,0:T(8,128)S(1)} collective-permute-done((f32[296,256]{1,0:T(8,128)S(1)}, f32[296,256]{1,0:T(8,128)S(1)}, u32[]{:S(2)}, u32[]{:S(2)}) %collective-permute-start.7) | collective-permute-done | bytes 303136 | tf_op jit(solution)/shard_map/ppermute | solution.py:401
  57.6 1.9 %collective-permute-done.8.refs_2_ = f32[296,256]{1,0:T(8,128)S(1)} collective-permute-done((f32[296,256]{1,0:T(8,128)S(1)}, f32[296,256]{1,0:T(8,128)S(1)}, u32[]{:S(2)}, u32[]{:S(2)}) %collective-permute-start.8) | collective-permute-done | bytes 303136 | tf_op jit(solution)/shard_map/ppermute | solution.py:401
  59.5 14.1 %collective-permute-done.9.refs_3_ = f32[296,256]{1,0:T(8,128)S(1)} collective-permute-done((f32[296,256]{1,0:T(8,128)S(1)}, f32[296,256]{1,0:T(8,128)S(1)}, u32[]{:S(2)}, u32[]{:S(2)}) %collective-permute-start.9) | collective-permute-done | bytes 303136 | tf_op jit(solution)/shard_map/ppermute | solution.py:401
  73.6 0.0 copy-done.4
  73.6 0.4 energies.1
  74.0 11.3 %all-gather = f32[128,128]{1,0:T(8,128)S(1)} all-gather(f32[16,128]{1,0:T(8,128)S(1)} %energies.1), channel_id=2, replica_groups=mesh['pos'=8,'freq'=4] {'pos'}, dimensions={0}, use_global_device_ids=true | all-gather | bytes 73728 | tf_op jit(solution)/shard_map/all_gather | solution.py:445
  85.3 1.2 %diffuse.1 = f32[4,64]{1,0:T(4,128)} custom-call(f32[8,16,128]{2,1,0:T(8,128)S(1)} %bitcast.3), custom_call_target="tpu_custom_call" | custom-call | tf_op jit(solution)/shard_map/diffuse/pallas_call | solution.py:389
Async XLA Ops:
  0.0 0.7 copy-start
  11.7 21.1 %collective-permute-start = (f32[4,64,256]{2,1,0:T(8,128)S(1)}, f32[4,64,256]{2,1,0:T(8,128)S(1)}, u32[]{:S(2)}, u32[]{:S(2)}) collective-permute-start(f32[4,64,256]{2,1,0:T(8,128)S(1)} %get-tuple-element.25.refs_4_), channel_id=1, source_target_pairs={{0,24},{4,28},{8,16},{12,20},{16,8},{20,12},{24,0},{28,4},{1,25},{... | collective-permute-start | bytes 786440 | tf_op jit(solution)/shard_map/ppermute | solution.py:401
  14.0 19.1 %collective-permute-start.1 = (f32[4,64,256]{2,1,0:T(8,128)S(1)}, f32[4,64,256]{2,1,0:T(8,128)S(1)}, u32[]{:S(2)}, u32[]{:S(2)}) collective-permute-start(f32[4,64,256]{2,1,0:T(8,128)S(1)} %get-tuple-element.28), channel_id=1, source_target_pairs={{0,28},{4,24},{8,20},{12,16},{16,12},{20,8},{24,4},{28,0},{1,29},{... | collective-permute-start | bytes 786440 | tf_op jit(solution)/shard_map/ppermute | solution.py:401
  22.3 18.8 %copy-start.1 = (s32[16,32]{1,0:T(8,128)S(1)}, s32[16,32]{1,0:T(8,128)}, u32[]{:S(2)}) copy-start(s32[16,32]{1,0:T(8,128)} %refs_0_.1) | copy-start | bytes 6148
  22.3 21.6 %copy-start.2 = (f32[2,4,64]{2,1,0:T(4,128)S(1)}, f32[2,4,64]{2,1,0:T(4,128)}, u32[]{:S(2)}) copy-start(f32[2,4,64]{2,1,0:T(4,128)} %conduct_ref.3) | copy-start | bytes 6148
  22.3 21.6 %copy-start.3 = (f32[4,64]{1,0:T(4,128)S(1)}, f32[4,64]{1,0:T(4,128)}, u32[]{:S(2)}) copy-start(f32[4,64]{1,0:T(4,128)} %baseline_ref.3) | copy-start | bytes 3076
  22.4 18.8 %collective-permute-start.5 = (f32[4,64,256]{2,1,0:T(8,128)S(1)}, f32[4,64,256]{2,1,0:T(8,128)S(1)}, u32[]{:S(2)}, u32[]{:S(2)}) collective-permute-start(f32[4,64,256]{2,1,0:T(8,128)S(1)} %get-tuple-element.26.refs_4_), channel_id=1, source_target_pairs={{0,16},{4,20},{8,24},{12,28},{16,0},{20,4},{24,8},{28,12},{1,17},{... | collective-permute-start | bytes 786440 | tf_op jit(solution)/shard_map/ppermute | solution.py:401
  31.0 42.6 %copy-start.4 = (f32[256]{0:T(256)S(1)}, f32[256]{0:T(256)}, u32[]{:S(2)}) copy-start(f32[256]{0:T(256)} %param.7) | copy-start | bytes 3076
  31.0 10.2 %collective-permute-start.4 = (f32[4,64,256]{2,1,0:T(8,128)S(1)}, f32[4,64,256]{2,1,0:T(8,128)S(1)}, u32[]{:S(2)}, u32[]{:S(2)}) collective-permute-start(f32[4,64,256]{2,1,0:T(8,128)S(1)} %get-tuple-element.32), channel_id=1, source_target_pairs={{0,12},{4,8},{8,4},{12,0},{16,28},{20,24},{24,20},{28,16},{1,13},{... | collective-permute-start | bytes 786440 | tf_op jit(solution)/shard_map/ppermute | solution.py:401
  32.0 9.2 %collective-permute-start.6 = (f32[4,64,256]{2,1,0:T(8,128)S(1)}, f32[4,64,256]{2,1,0:T(8,128)S(1)}, u32[]{:S(2)}, u32[]{:S(2)}) collective-permute-start(f32[4,64,256]{2,1,0:T(8,128)S(1)} %get-tuple-element.27.refs_4_), channel_id=1, source_target_pairs={{0,20},{4,16},{8,28},{12,24},{16,4},{20,0},{24,12},{28,8},{1,21},{... | collective-permute-start | bytes 786440 | tf_op jit(solution)/shard_map/ppermute | solution.py:401
  32.8 11.2 %collective-permute-start.3 = (f32[4,64,256]{2,1,0:T(8,128)S(1)}, f32[4,64,256]{2,1,0:T(8,128)S(1)}, u32[]{:S(2)}, u32[]{:S(2)}) collective-permute-start(f32[4,64,256]{2,1,0:T(8,128)S(1)} %get-tuple-element.31), channel_id=1, source_target_pairs={{0,8},{4,12},{8,0},{12,4},{16,24},{20,28},{24,16},{28,20},{1,9},{5... | collective-permute-start | bytes 786440 | tf_op jit(solution)/shard_map/ppermute | solution.py:401
  40.5 3.4 %collective-permute-start.2 = (f32[4,64,256]{2,1,0:T(8,128)S(1)}, f32[4,64,256]{2,1,0:T(8,128)S(1)}, u32[]{:S(2)}, u32[]{:S(2)}) collective-permute-start(f32[4,64,256]{2,1,0:T(8,128)S(1)} %get-tuple-element.30), channel_id=1, source_target_pairs={{0,4},{4,0},{8,12},{12,8},{16,20},{20,16},{24,28},{28,24},{1,5},{5... | collective-permute-start | bytes 786440 | tf_op jit(solution)/shard_map/ppermute | solution.py:401
  45.6 12.0 %collective-permute-start.7 = (f32[296,256]{1,0:T(8,128)S(1)}, f32[296,256]{1,0:T(8,128)S(1)}, u32[]{:S(2)}, u32[]{:S(2)}) collective-permute-start(f32[296,256]{1,0:T(8,128)S(1)} %get-tuple-element.34), channel_id=1, source_target_pairs={{0,1},{1,0},{2,3},{3,2},{4,5},{5,4},{6,7},{7,6},{8,9},{9,8},{10,11... | collective-permute-start | bytes 909320 | tf_op jit(solution)/shard_map/ppermute | solution.py:401
  46.9 12.6 %collective-permute-start.8 = (f32[296,256]{1,0:T(8,128)S(1)}, f32[296,256]{1,0:T(8,128)S(1)}, u32[]{:S(2)}, u32[]{:S(2)}) collective-permute-start(f32[296,256]{1,0:T(8,128)S(1)} %get-tuple-element.35), channel_id=1, source_target_pairs={{0,2},{1,3},{2,0},{3,1},{4,6},{5,7},{6,4},{7,5},{8,10},{9,11},{10,... | collective-permute-start | bytes 909320 | tf_op jit(solution)/shard_map/ppermute | solution.py:401
  47.0 26.6 %collective-permute-start.9 = (f32[296,256]{1,0:T(8,128)S(1)}, f32[296,256]{1,0:T(8,128)S(1)}, u32[]{:S(2)}, u32[]{:S(2)}) collective-permute-start(f32[296,256]{1,0:T(8,128)S(1)} %get-tuple-element.36), channel_id=1, source_target_pairs={{0,3},{1,2},{2,1},{3,0},{4,7},{5,6},{6,5},{7,4},{8,11},{9,10},{10,... | collective-permute-start | bytes 909320 | tf_op jit(solution)/shard_map/ppermute | solution.py:401

commit v8 on v7

--- a/solution.py
+++ b/solution.py
@@ -420,12 +420,11 @@
     ids = footprint.reshape(pos_count, pos_local * foot)
     split = basis.reshape(pos_local, freq_local, 2, elements, rank)
     groups = pos_count // TH
-    half = groups // 2
     parts = [None] * pos_count
     rounds = (
         tuple(range(3 * groups, 4 * groups)),
-        tuple(range(2 * groups, 2 * groups + half)) + tuple(range(groups, groups + half)),
-        tuple(range(2 * groups + half, 3 * groups)) + tuple(range(groups + half, 2 * groups)),
+        tuple(range(2 * groups, 3 * groups)),
+        tuple(range(groups, 2 * groups)),
         tuple(range(groups)),
     )
     operands, after = (footprint, split), ()

time: 86.7 us -> 87.6 us (1.010)
  waiting for transfers between devices: 28.1 us -> 29.7 us
    ppermute x10, waiting for transfers between devices: 28.1 us -> 29.7 us  [swap(): lax.ppermute(array, axis, [(i, i ^ distance) for i in range(lax.axis_size...]
  transfers between devices with their start and end apart: 10 -> 10, of which waited for: 4 -> 4; matrix products, arithmetic and copies ran while one was open for 0% -> 0% of each run, Pallas kernels for 26% -> 25%
where the time goes in v8:
time: 87.6 us; the launch traced here: 87.3 us
  Pallas kernels  36.3 us (41%)
  waiting for transfers between devices  29.7 us (34%)
  blocking collectives  10.5 us (12%)
  starting transfers between devices  9.87 us (11%)
    pallas_call x4, Pallas kernels, project(): pl.pallas_call(functools.partial(project_kernel, sizes, rounds, turn, len...  33.1 us
    ppermute x10, waiting for transfers between devices, swap(): lax.ppermute(array, axis, [(i, i ^ distance) for i in range(lax.axis_size...  29.7 us
    all_gather x1, blocking collectives, body(): strips = lax.all_gather(strip, 'pos')  10.5 us
    ppermute x10, starting transfers between devices, swap(): lax.ppermute(array, axis, [(i, i ^ distance) for i in range(lax.axis_size...  9.87 us
  transfers between devices with their start and end apart: 10, of which 4 were waited for; matrix products, arithmetic and copies ran while one was open for 0% of the time, Pallas kernels for 25%

profile of v8, /device:TPU:17, one launch (start us, length us, event | category | flops | bytes accessed | tf_op | source)
XLA Modules:
  0.0 87.3 jit_solution(17124512650261483799)
XLA Ops:
  0.0 0.0 copy-start
  0.0 0.7 copy-done
  0.7 11.0 %project_0.1 = (f32[4,64,256]{2,1,0:T(8,128)S(1)}, f32[4,64,256]{2,1,0:T(8,128)S(1)}, bf16[8,4,2,256,256]{4,3,2,1,0:T(8,128)(2,1)S(1)}, f32[4,2,32,8,128]{4,3,2,...) custom-call(s32[16,32]{1,0:T(8,128)S(1)} %copy-done, bf16[2,4,2,1024,256]{4,3,2,1,0:T(8,128)(2,1)} %bitcast.5), custom_call_target="tpu_custom_call" | custom-call | flops 2147483648 | bytes 2147483648 | tf_op jit(solution)/shard_map/project_0/pallas_call | solution.py:206
  11.7 2.2 %collective-permute-start = (f32[4,64,256]{2,1,0:T(8,128)S(1)}, f32[4,64,256]{2,1,0:T(8,128)S(1)}, u32[]{:S(2)}, u32[]{:S(2)}) collective-permute-start(f32[4,64,256]{2,1,0:T(8,128)S(1)} %get-tuple-element.25.refs_4_), channel_id=1, source_target_pairs={{0,24},{4,28},{8,16},{12,20},{16,8},{20,12},{24,0},{28,4},{1,25},{... | collective-permute-start | bytes 786440 | tf_op jit(solution)/shard_map/ppermute | solution.py:401
  14.0 1.0 %collective-permute-start.1 = (f32[4,64,256]{2,1,0:T(8,128)S(1)}, f32[4,64,256]{2,1,0:T(8,128)S(1)}, u32[]{:S(2)}, u32[]{:S(2)}) collective-permute-start(f32[4,64,256]{2,1,0:T(8,128)S(1)} %get-tuple-element.28), channel_id=1, source_target_pairs={{0,28},{4,24},{8,20},{12,16},{16,12},{20,8},{24,4},{28,0},{1,29},{... | collective-permute-start | bytes 786440 | tf_op jit(solution)/shard_map/ppermute | solution.py:401
  15.0 7.3 %project_1.1 = (f32[4,64,256]{2,1,0:T(8,128)S(1)}, f32[4,64,256]{2,1,0:T(8,128)S(1)}) custom-call(bf16[8,4,2,256,256]{4,3,2,1,0:T(8,128)(2,1)S(1)} %get-tuple-element.21.refs_0_, f32[4,2,32,8,128]{4,3,2,1,0:T(8,128)S(1)} %get-tuple-element.22.refs_1_, f32[4,2,32,8,128]{4,3,2,1,0:T(8,128)S(1)} %get-tuple-element.23.refs_2_, ...), custom_call_target="tpu_custom_call" | custom-call | flops 2147483648 | bytes 2147483648 | tf_op jit(solution)/shard_map/project_1/pallas_call | solution.py:206
  22.3 0.0 copy-start.1
  22.3 0.0 copy-start.2
  22.3 0.0 copy-start.3
  22.4 1.3 %collective-permute-start.5 = (f32[4,64,256]{2,1,0:T(8,128)S(1)}, f32[4,64,256]{2,1,0:T(8,128)S(1)}, u32[]{:S(2)}, u32[]{:S(2)}) collective-permute-start(f32[4,64,256]{2,1,0:T(8,128)S(1)} %get-tuple-element.26.refs_4_), channel_id=1, source_target_pairs={{0,16},{4,20},{8,24},{12,28},{16,0},{20,4},{24,8},{28,12},{1,17},{... | collective-permute-start | bytes 786440 | tf_op jit(solution)/shard_map/ppermute | solution.py:401
  23.7 7.3 %project_2.1 = (f32[4,64,256]{2,1,0:T(8,128)S(1)}, f32[4,64,256]{2,1,0:T(8,128)S(1)}) custom-call(bf16[8,4,2,256,256]{4,3,2,1,0:T(8,128)(2,1)S(1)} %get-tuple-element.21.refs_0_, f32[4,2,32,8,128]{4,3,2,1,0:T(8,128)S(1)} %get-tuple-element.22.refs_1_, f32[4,2,32,8,128]{4,3,2,1,0:T(8,128)S(1)} %get-tuple-element.23.refs_2_, ...), custom_call_target="tpu_custom_call" | custom-call | flops 2147483648 | bytes 2147483648 | tf_op jit(solution)/shard_map/project_2/pallas_call | solution.py:206
  31.0 0.0 copy-start.4
  31.0 1.3 %collective-permute-start.3 = (f32[4,64,256]{2,1,0:T(8,128)S(1)}, f32[4,64,256]{2,1,0:T(8,128)S(1)}, u32[]{:S(2)}, u32[]{:S(2)}) collective-permute-start(f32[4,64,256]{2,1,0:T(8,128)S(1)} %get-tuple-element.27.refs_4_), channel_id=1, source_target_pairs={{0,8},{4,12},{8,0},{12,4},{16,24},{20,28},{24,16},{28,20},{1,9},{5... | collective-permute-start | bytes 786440 | tf_op jit(solution)/shard_map/ppermute | solution.py:401
  32.3 0.3 collective-permute-start.4
  32.5 0.0 collective-permute-done.refs_5_.refs_6_
  32.5 0.5 collective-permute-start.6
  33.0 0.0 collective-permute-done.1.refs_6_.refs_7_
  33.0 7.5 %project_3.1 = (f32[4,64,256]{2,1,0:T(8,128)S(1)}, f32[4,64,256]{2,1,0:T(8,128)S(1)}) custom-call(bf16[8,4,2,256,256]{4,3,2,1,0:T(8,128)(2,1)S(1)} %get-tuple-element.21.refs_0_, f32[4,2,32,8,128]{4,3,2,1,0:T(8,128)S(1)} %get-tuple-element.22.refs_1_, f32[4,2,32,8,128]{4,3,2,1,0:T(8,128)S(1)} %get-tuple-element.23.refs_2_, ...), custom_call_target="tpu_custom_call" | custom-call | flops 2147483648 | bytes 2147483648 | tf_op jit(solution)/shard_map/project_3/pallas_call | solution.py:206
  40.5 0.5 collective-permute-start.2
  41.1 0.0 copy-done.1
  41.1 0.1 reshape.10.ids_ref
  41.2 0.0 collective-permute-done.3.refs_2_
  41.2 3.6 %collective-permute-done.4.refs_3_ = f32[4,64,256]{2,1,0:T(8,128)S(1)} collective-permute-done((f32[4,64,256]{2,1,0:T(8,128)S(1)}, f32[4,64,256]{2,1,0:T(8,128)S(1)}, u32[]{:S(2)}, u32[]{:S(2)}) %collective-permute-start.4) | collective-permute-done | bytes 262176 | tf_op jit(solution)/shard_map/ppermute | solution.py:401
  44.7 0.0 collective-permute-done.5.refs_4_
  44.7 0.0 collective-permute-done.6.refs_5_
  44.7 0.0 collective-permute-done.2.refs_1_
  44.7 0.0 copy-done.2
  44.7 0.0 copy-done.3
  44.7 1.6 %tiles.1 = (f32[288,256]{1,0:T(8,128)S(1)}, f32[296,256]{1,0:T(8,128)S(1)}, f32[296,256]{1,0:T(8,128)S(1)}, f32[296,256]{1,0:T(8,128)S(1)}) custom-call(s32[8,64]{1,0:T(8,128)S(1)} %reshape.10.ids_ref, f32[2,4,64]{2,1,0:T(4,128)S(1)} %copy-done.2, f32[4,64]{1,0:T(4,128)S(1)} %copy-done.3, f32[4,64,256]{2,1,0:T(8,128)S(1)} %get-tuple-element.29.refs_0_, ...), custom_call_target="tpu_custom_call" | custom-call | tf_op jit(solution)/shard_map/tiles/pallas_call | solution.py:269
  46.3 1.4 %collective-permute-start.7 = (f32[296,256]{1,0:T(8,128)S(1)}, f32[296,256]{1,0:T(8,128)S(1)}, u32[]{:S(2)}, u32[]{:S(2)}) collective-permute-start(f32[296,256]{1,0:T(8,128)S(1)} %get-tuple-element.34), channel_id=1, source_target_pairs={{0,1},{1,0},{2,3},{3,2},{4,5},{5,4},{6,7},{7,6},{8,9},{9,8},{10,11... | collective-permute-start | bytes 909320 | tf_op jit(solution)/shard_map/ppermute | solution.py:401
  47.7 0.1 collective-permute-start.8
  47.8 1.3 %collective-permute-start.9 = (f32[296,256]{1,0:T(8,128)S(1)}, f32[296,256]{1,0:T(8,128)S(1)}, u32[]{:S(2)}, u32[]{:S(2)}) collective-permute-start(f32[296,256]{1,0:T(8,128)S(1)} %get-tuple-element.36), channel_id=1, source_target_pairs={{0,3},{1,2},{2,1},{3,0},{4,7},{5,6},{6,5},{7,4},{8,11},{9,10},{10,... | collective-permute-start | bytes 909320 | tf_op jit(solution)/shard_map/ppermute | solution.py:401
  49.0 10.1 %collective-permute-done.7.refs_1_ = f32[296,256]{1,0:T(8,128)S(1)} collective-permute-done((f32[296,256]{1,0:T(8,128)S(1)}, f32[296,256]{1,0:T(8,128)S(1)}, u32[]{:S(2)}, u32[]{:S(2)}) %collective-permute-start.7) | collective-permute-done | bytes 303136 | tf_op jit(solution)/shard_map/ppermute | solution.py:401
  59.1 2.1 %collective-permute-done.8.refs_2_ = f32[296,256]{1,0:T(8,128)S(1)} collective-permute-done((f32[296,256]{1,0:T(8,128)S(1)}, f32[296,256]{1,0:T(8,128)S(1)}, u32[]{:S(2)}, u32[]{:S(2)}) %collective-permute-start.8) | collective-permute-done | bytes 303136 | tf_op jit(solution)/shard_map/ppermute | solution.py:401
  61.2 14.0 %collective-permute-done.9.refs_3_ = f32[296,256]{1,0:T(8,128)S(1)} collective-permute-done((f32[296,256]{1,0:T(8,128)S(1)}, f32[296,256]{1,0:T(8,128)S(1)}, u32[]{:S(2)}, u32[]{:S(2)}) %collective-permute-start.9) | collective-permute-done | bytes 303136 | tf_op jit(solution)/shard_map/ppermute | solution.py:401
  75.2 0.0 copy-done.4
  75.2 0.4 energies.1
  75.6 10.5 %all-gather = f32[128,128]{1,0:T(8,128)S(1)} all-gather(f32[16,128]{1,0:T(8,128)S(1)} %energies.1), channel_id=2, replica_groups=mesh['pos'=8,'freq'=4] {'pos'}, dimensions={0}, use_global_device_ids=true | all-gather | bytes 73728 | tf_op jit(solution)/shard_map/all_gather | solution.py:444
  86.1 1.2 %diffuse.1 = f32[4,64]{1,0:T(4,128)} custom-call(f32[8,16,128]{2,1,0:T(8,128)S(1)} %bitcast.3), custom_call_target="tpu_custom_call" | custom-call | tf_op jit(solution)/shard_map/diffuse/pallas_call | solution.py:389
Async XLA Ops:
  0.0 0.7 copy-start
  11.7 20.8 %collective-permute-start = (f32[4,64,256]{2,1,0:T(8,128)S(1)}, f32[4,64,256]{2,1,0:T(8,128)S(1)}, u32[]{:S(2)}, u32[]{:S(2)}) collective-permute-start(f32[4,64,256]{2,1,0:T(8,128)S(1)} %get-tuple-element.25.refs_4_), channel_id=1, source_target_pairs={{0,24},{4,28},{8,16},{12,20},{16,8},{20,12},{24,0},{28,4},{1,25},{... | collective-permute-start | bytes 786440 | tf_op jit(solution)/shard_map/ppermute | solution.py:401
  14.0 19.1 %collective-permute-start.1 = (f32[4,64,256]{2,1,0:T(8,128)S(1)}, f32[4,64,256]{2,1,0:T(8,128)S(1)}, u32[]{:S(2)}, u32[]{:S(2)}) collective-permute-start(f32[4,64,256]{2,1,0:T(8,128)S(1)} %get-tuple-element.28), channel_id=1, source_target_pairs={{0,28},{4,24},{8,20},{12,16},{16,12},{20,8},{24,4},{28,0},{1,29},{... | collective-permute-start | bytes 786440 | tf_op jit(solution)/shard_map/ppermute | solution.py:401
  22.3 18.8 %copy-start.1 = (s32[16,32]{1,0:T(8,128)S(1)}, s32[16,32]{1,0:T(8,128)}, u32[]{:S(2)}) copy-start(s32[16,32]{1,0:T(8,128)} %refs_0_.1) | copy-start | bytes 6148
  22.3 22.4 %copy-start.2 = (f32[2,4,64]{2,1,0:T(4,128)S(1)}, f32[2,4,64]{2,1,0:T(4,128)}, u32[]{:S(2)}) copy-start(f32[2,4,64]{2,1,0:T(4,128)} %conduct_ref.3) | copy-start | bytes 6148
  22.3 22.4 %copy-start.3 = (f32[4,64]{1,0:T(4,128)S(1)}, f32[4,64]{1,0:T(4,128)}, u32[]{:S(2)}) copy-start(f32[4,64]{1,0:T(4,128)} %baseline_ref.3) | copy-start | bytes 3076
  22.4 22.4 %collective-permute-start.5 = (f32[4,64,256]{2,1,0:T(8,128)S(1)}, f32[4,64,256]{2,1,0:T(8,128)S(1)}, u32[]{:S(2)}, u32[]{:S(2)}) collective-permute-start(f32[4,64,256]{2,1,0:T(8,128)S(1)} %get-tuple-element.26.refs_4_), channel_id=1, source_target_pairs={{0,16},{4,20},{8,24},{12,28},{16,0},{20,4},{24,8},{28,12},{1,17},{... | collective-permute-start | bytes 786440 | tf_op jit(solution)/shard_map/ppermute | solution.py:401
  31.0 44.2 %copy-start.4 = (f32[256]{0:T(256)S(1)}, f32[256]{0:T(256)}, u32[]{:S(2)}) copy-start(f32[256]{0:T(256)} %param.7) | copy-start | bytes 3076
  31.0 10.2 %collective-permute-start.3 = (f32[4,64,256]{2,1,0:T(8,128)S(1)}, f32[4,64,256]{2,1,0:T(8,128)S(1)}, u32[]{:S(2)}, u32[]{:S(2)}) collective-permute-start(f32[4,64,256]{2,1,0:T(8,128)S(1)} %get-tuple-element.27.refs_4_), channel_id=1, source_target_pairs={{0,8},{4,12},{8,0},{12,4},{16,24},{20,28},{24,16},{28,20},{1,9},{5... | collective-permute-start | bytes 786440 | tf_op jit(solution)/shard_map/ppermute | solution.py:401
  32.3 12.4 %collective-permute-start.4 = (f32[4,64,256]{2,1,0:T(8,128)S(1)}, f32[4,64,256]{2,1,0:T(8,128)S(1)}, u32[]{:S(2)}, u32[]{:S(2)}) collective-permute-start(f32[4,64,256]{2,1,0:T(8,128)S(1)} %get-tuple-element.31), channel_id=1, source_target_pairs={{0,12},{4,8},{8,4},{12,0},{16,28},{20,24},{24,20},{28,16},{1,13},{... | collective-permute-start | bytes 786440 | tf_op jit(solution)/shard_map/ppermute | solution.py:401
  32.5 12.2 %collective-permute-start.6 = (f32[4,64,256]{2,1,0:T(8,128)S(1)}, f32[4,64,256]{2,1,0:T(8,128)S(1)}, u32[]{:S(2)}, u32[]{:S(2)}) collective-permute-start(f32[4,64,256]{2,1,0:T(8,128)S(1)} %get-tuple-element.32), channel_id=1, source_target_pairs={{0,20},{4,16},{8,28},{12,24},{16,4},{20,0},{24,12},{28,8},{1,21},{... | collective-permute-start | bytes 786440 | tf_op jit(solution)/shard_map/ppermute | solution.py:401
  40.5 4.2 %collective-permute-start.2 = (f32[4,64,256]{2,1,0:T(8,128)S(1)}, f32[4,64,256]{2,1,0:T(8,128)S(1)}, u32[]{:S(2)}, u32[]{:S(2)}) collective-permute-start(f32[4,64,256]{2,1,0:T(8,128)S(1)} %get-tuple-element.30), channel_id=1, source_target_pairs={{0,4},{4,0},{8,12},{12,8},{16,20},{20,16},{24,28},{28,24},{1,5},{5... | collective-permute-start | bytes 786440 | tf_op jit(solution)/shard_map/ppermute | solution.py:401
  46.3 12.8 %collective-permute-start.7 = (f32[296,256]{1,0:T(8,128)S(1)}, f32[296,256]{1,0:T(8,128)S(1)}, u32[]{:S(2)}, u32[]{:S(2)}) collective-permute-start(f32[296,256]{1,0:T(8,128)S(1)} %get-tuple-element.34), channel_id=1, source_target_pairs={{0,1},{1,0},{2,3},{3,2},{4,5},{5,4},{6,7},{7,6},{8,9},{9,8},{10,11... | collective-permute-start | bytes 909320 | tf_op jit(solution)/shard_map/ppermute | solution.py:401
  47.7 13.5 %collective-permute-start.8 = (f32[296,256]{1,0:T(8,128)S(1)}, f32[296,256]{1,0:T(8,128)S(1)}, u32[]{:S(2)}, u32[]{:S(2)}) collective-permute-start(f32[296,256]{1,0:T(8,128)S(1)} %get-tuple-element.35), channel_id=1, source_target_pairs={{0,2},{1,3},{2,0},{3,1},{4,6},{5,7},{6,4},{7,5},{8,10},{9,11},{10,... | collective-permute-start | bytes 909320 | tf_op jit(solution)/shard_map/ppermute | solution.py:401
  47.8 27.5 %collective-permute-start.9 = (f32[296,256]{1,0:T(8,128)S(1)}, f32[296,256]{1,0:T(8,128)S(1)}, u32[]{:S(2)}, u32[]{:S(2)}) collective-permute-start(f32[296,256]{1,0:T(8,128)S(1)} %get-tuple-element.36), channel_id=1, source_target_pairs={{0,3},{1,2},{2,1},{3,0},{4,7},{5,6},{6,5},{7,4},{8,11},{9,10},{10,... | collective-permute-start | bytes 909320 | tf_op jit(solution)/shard_map/ppermute | solution.py:401
